TPU v7x, 32 devices: a whole 2x2x4 slice. The times are simulated.
32 devices in a mesh: dp: 8 (over z, y), tensor: 4 (over x, core).
Axes of the slice: x: 2, y: 2, z: 4, core: 2. Of those that a mesh axis runs over, the one named last changes fastest.
Arguments:
- block_input: bfloat16 [4096, 1024], P('dp'), may hold values from -6 to 6
- lengths: int32 [8], P('dp'), may hold values from 16 to 512, as said below
- norm_params: float32 [8, 1024], replicated
- qkv_weight: float32 [1024, 3, 1024], P(None, None, 'tensor')
- out_weight: float32 [1024, 1024], P('tensor')
- up_weight: float32 [1024, 4096], P(None, 'tensor')
- down_weight: float32 [4096, 1024], P('tensor')
- qkv_first: float32 [1024, 3, 1024], P('dp', None, 'tensor'), may hold values from -40 to 40
- qkv_second: float32 [1024, 3, 1024], P('dp', None, 'tensor')
- out_first: float32 [1024, 1024], P('tensor', 'dp'), may hold values from -40 to 40
- out_second: float32 [1024, 1024], P('tensor', 'dp')
- up_first: float32 [1024, 4096], P('dp', 'tensor'), may hold values from -20 to 20
- up_second: float32 [1024, 4096], P('dp', 'tensor')
- down_first: float32 [4096, 1024], P('tensor', 'dp'), may hold values from -40 to 40
- down_second: float32 [4096, 1024], P('tensor', 'dp')
- norm_first: float32 [8, 1024], P(None, 'dp'), may hold values from -40 to 40
- norm_second: float32 [8, 1024], P(None, 'dp')
- out_grad: bfloat16 [4096, 1024], P('dp'), may hold values from -6 to 6
Outputs:
- block_output: bfloat16 [4096, 1024], P('dp')
- input_grad: bfloat16 [4096, 1024], P('dp')
- qkv_new: float32 [1024, 3, 1024], P('dp', None, 'tensor')
- qkv_first_new: float32 [1024, 3, 1024], P('dp', None, 'tensor')
- qkv_second_new: float32 [1024, 3, 1024], P('dp', None, 'tensor')
- out_new: float32 [1024, 1024], P('tensor', 'dp')
- out_first_new: float32 [1024, 1024], P('tensor', 'dp')
- out_second_new: float32 [1024, 1024], P('tensor', 'dp')
- up_new: float32 [1024, 4096], P('dp', 'tensor')
- up_first_new: float32 [1024, 4096], P('dp', 'tensor')
- up_second_new: float32 [1024, 4096], P('dp', 'tensor')
- down_new: float32 [4096, 1024], P('tensor', 'dp')
- down_first_new: float32 [4096, 1024], P('tensor', 'dp')
- down_second_new: float32 [4096, 1024], P('tensor', 'dp')
- norm_new: float32 [8, 1024], P(None, 'dp')
- norm_first_new: float32 [8, 1024], P(None, 'dp')
- norm_second_new: float32 [8, 1024], P(None, 'dp')
- matrix_norms: float32 [2, 4], replicated
Inputs may be any that keep to these rules, and one draw needn't show every extreme that they name: `lengths`: each slot holds one sequence of that many live tokens at its head, the rest padding; some sequence fills its slot.
All inputs are finite; a program needn't handle non-finite values.
Results may differ from a plain program's by a relative error of at most 0.014.
The roundings to bfloat16 on the way count: a program that leaves them out, or rounds other values in their place, can miss the bound.
Values sent between devices are 32-bit elements; how exact they have to be, the bound alone decides.
No kernel may reach another device: no remote copies, remote signals or barrier semaphores. Data moves between devices by JAX's collectives and lax.ppermute only.
A program may use at most 128 MiB of HBM per device.

v0:
```python
import jax
import jax.numpy as jnp
from jax import lax
from jax.sharding import PartitionSpec as P

HEAD_DIM = 64
STEP = 10


norm_epsilon = 1e-05
rotary_base = 10000.0
mask_fill = -1000000000.0
first_decay = 0.9
second_decay = 0.999
adam_epsilon = 1e-06
trust_epsilon = 1e-06
decay_rate = 0.01
learn_rate = 0.25


def layer_norm(values, gain, offset):
    center = values - jnp.mean(values, axis=-1, keepdims=True)
    inverse = lax.rsqrt(jnp.mean(center * center, axis=-1, keepdims=True) + norm_epsilon)
    normed = center * inverse
    return (normed * gain + offset, normed, inverse)


def norm_back(incoming, normed, inverse, gain):
    scaled = incoming * gain
    inner = (
        scaled
        - jnp.mean(scaled, axis=-1, keepdims=True)
        - normed * jnp.mean(scaled * normed, axis=-1, keepdims=True)
    )
    return (inner * inverse, jnp.sum(incoming * normed, axis=0), jnp.sum(incoming, axis=0))


def rotary_tables(length, head_size):
    half_size = head_size // 2
    frequency = rotary_base ** (-(jnp.arange(half_size, dtype=jnp.float32) * 2.0 / head_size))
    angles = jnp.arange(length, dtype=jnp.float32)[:, None] * frequency[None, :]
    return (jnp.cos(angles), jnp.sin(angles))


def rotate(values, cosine_table, sine_table):
    half_size = values.shape[-1] // 2
    leading = values[..., :half_size]
    trailing = values[..., half_size:]
    cosine_part = cosine_table[:, None, :]
    sine_part = sine_table[:, None, :]
    return jnp.concatenate(
        [
            leading * cosine_part - trailing * sine_part,
            trailing * cosine_part + leading * sine_part,
        ],
        axis=-1,
    )


def rotate_back(incoming, cosine_table, sine_table):
    half_size = incoming.shape[-1] // 2
    leading = incoming[..., :half_size]
    trailing = incoming[..., half_size:]
    cosine_part = cosine_table[:, None, :]
    sine_part = sine_table[:, None, :]
    return jnp.concatenate(
        [
            leading * cosine_part + trailing * sine_part,
            trailing * cosine_part - leading * sine_part,
        ],
        axis=-1,
    )


def moment_step(gradient, first_state, second_state):
    first_new = first_decay * first_state + (1.0 - first_decay) * gradient
    second_new = second_decay * second_state + (1.0 - second_decay) * gradient * gradient
    direction = (
        first_new
        / (1.0 - first_decay**STEP)
        / (jnp.sqrt(second_new / (1.0 - second_decay**STEP)) + adam_epsilon)
    )
    return (first_new, second_new, direction)


def gelu_exact(values):
    return jax.nn.gelu(values, approximate=False)


def shards(
    block_input,
    lengths,
    norm_params,
    qkv_weight,
    out_weight,
    up_weight,
    down_weight,
    qkv_first,
    qkv_second,
    out_first,
    out_second,
    up_first,
    up_second,
    down_first,
    down_second,
    norm_first,
    norm_second,
    out_grad,
):
    row_count, width = block_input.shape
    head_size = HEAD_DIM
    local_width = qkv_weight.shape[2]
    local_heads = local_width // head_size
    score_scale = head_size ** (-0.5)
    group_count = lax.axis_size("dp")
    group_rank = lax.axis_index("dp")
    own_rows = width // group_count
    own_start = group_rank * own_rows
    qkv_own = lax.dynamic_slice_in_dim(qkv_weight, own_start, own_rows, 0)
    out_own = lax.dynamic_slice_in_dim(out_weight, own_start, own_rows, 1)
    up_own = lax.dynamic_slice_in_dim(up_weight, own_start, own_rows, 0)
    down_own = lax.dynamic_slice_in_dim(down_weight, own_start, own_rows, 1)
    norm_own = lax.dynamic_slice_in_dim(norm_params, own_start, own_rows, 1)
    masters = (qkv_own, out_own, up_own, down_own)
    weight_local = jnp.stack([jnp.sum(master * master) for master in masters])
    qkv_low = qkv_weight.reshape(width, 3 * local_width).astype(jnp.bfloat16)
    out_low = out_weight.astype(jnp.bfloat16)
    up_low = up_weight.astype(jnp.bfloat16)
    down_low = down_weight.astype(jnp.bfloat16)
    residual = block_input.astype(jnp.float32)
    live_len = lengths[0]
    positions = jnp.arange(row_count)
    query_live = (positions < live_len).astype(jnp.float32)[:, None, None]
    visible = (positions[None, :] <= positions[:, None]) & (positions[None, :] < live_len)
    cosine_table, sine_table = rotary_tables(row_count, head_size)
    normed_in, stat_in, inverse_in = layer_norm(residual, norm_params[0], norm_params[1])
    normed_in_low = normed_in.astype(jnp.bfloat16)
    projected = jnp.dot(normed_in_low, qkv_low, preferred_element_type=jnp.float32)
    projected = projected.reshape(row_count, 3, local_heads, head_size)
    query = rotate(projected[:, 0], cosine_table, sine_table).astype(jnp.bfloat16)
    keys = rotate(projected[:, 1], cosine_table, sine_table).astype(jnp.bfloat16)
    values = projected[:, 2].astype(jnp.bfloat16)

    def scores_of(query_part, key_part):
        raw_scores = (
            jnp.einsum("qhd,khd->hqk", query_part, key_part, preferred_element_type=jnp.float32)
            * score_scale
        )
        return jnp.where(visible[None], raw_scores, mask_fill)

    scores = scores_of(query, keys)
    top_score = jnp.max(scores, axis=-1, keepdims=True)
    expo = jnp.exp(scores - top_score)
    total_mass = jnp.sum(expo, axis=-1, keepdims=True)
    probs = expo / total_mass
    log_total = top_score + jnp.log(total_mass)
    mixed = (
        jnp.einsum(
            "hqk,khd->qhd", probs.astype(jnp.bfloat16), values, preferred_element_type=jnp.float32
        )
        * query_live
    )
    attn_low = mixed.reshape(row_count, local_width).astype(jnp.bfloat16)
    branch = lax.psum(jnp.dot(attn_low, out_low, preferred_element_type=jnp.float32), "tensor")
    branch_out, stat_branch, inverse_branch = layer_norm(branch, norm_params[2], norm_params[3])
    hidden_state = residual + branch_out
    normed_mid, stat_mid, inverse_mid = layer_norm(hidden_state, norm_params[4], norm_params[5])
    normed_mid_low = normed_mid.astype(jnp.bfloat16)
    up_part = jnp.dot(normed_mid_low, up_low, preferred_element_type=jnp.float32)
    active_low = gelu_exact(up_part).astype(jnp.bfloat16)
    mlp_out = lax.psum(jnp.dot(active_low, down_low, preferred_element_type=jnp.float32), "tensor")
    mlp_norm, stat_mlp, inverse_mlp = layer_norm(mlp_out, norm_params[6], norm_params[7])
    block_output = (hidden_state + mlp_norm).astype(jnp.bfloat16)
    grad_final = out_grad.astype(jnp.float32)
    grad_mlp, gain_grad_three, offset_grad_three = norm_back(
        grad_final, stat_mlp, inverse_mlp, norm_params[6]
    )
    grad_mlp_low = grad_mlp.astype(jnp.bfloat16)
    grad_down = jnp.dot(active_low.T, grad_mlp_low, preferred_element_type=jnp.float32)
    grad_active = jnp.dot(grad_mlp_low, down_low.T, preferred_element_type=jnp.float32)
    gelu_pull = jax.vjp(gelu_exact, up_part)[1]
    grad_up_low = gelu_pull(grad_active)[0].astype(jnp.bfloat16)
    grad_up = jnp.dot(normed_mid_low.T, grad_up_low, preferred_element_type=jnp.float32)
    grad_mid = lax.psum(
        jnp.dot(grad_up_low, up_low.T, preferred_element_type=jnp.float32), "tensor"
    )
    grad_mid_in, gain_grad_two, offset_grad_two = norm_back(
        grad_mid, stat_mid, inverse_mid, norm_params[4]
    )
    grad_hidden = grad_final + grad_mid_in
    grad_branch, gain_grad_one, offset_grad_one = norm_back(
        grad_hidden, stat_branch, inverse_branch, norm_params[2]
    )
    grad_branch_low = grad_branch.astype(jnp.bfloat16)
    grad_out = jnp.dot(attn_low.T, grad_branch_low, preferred_element_type=jnp.float32)
    grad_attn = jnp.dot(grad_branch_low, out_low.T, preferred_element_type=jnp.float32)
    grad_mixed = grad_attn.astype(jnp.bfloat16).reshape(
        row_count, local_heads, head_size
    ) * query_live.astype(jnp.bfloat16)
    scores_again = scores_of(query, keys)
    probs_again = jnp.exp(scores_again - log_total)
    grad_values = jnp.einsum(
        "hqk,qhd->khd",
        probs_again.astype(jnp.bfloat16),
        grad_mixed,
        preferred_element_type=jnp.float32,
    )
    grad_probs = jnp.einsum("qhd,khd->hqk", grad_mixed, values, preferred_element_type=jnp.float32)
    row_inner = jnp.sum(grad_probs * probs_again, axis=-1, keepdims=True)
    grad_scores = (probs_again * (grad_probs - row_inner)).astype(jnp.bfloat16)
    grad_query = (
        jnp.einsum("hqk,khd->qhd", grad_scores, keys, preferred_element_type=jnp.float32)
        * score_scale
    )
    grad_keys = (
        jnp.einsum("hqk,qhd->khd", grad_scores, query, preferred_element_type=jnp.float32)
        * score_scale
    )
    grad_rows = jnp.stack(
        [
            rotate_back(grad_query, cosine_table, sine_table),
            rotate_back(grad_keys, cosine_table, sine_table),
            grad_values,
        ],
        axis=1,
    )
    grad_rows_low = grad_rows.reshape(row_count, 3 * local_width).astype(jnp.bfloat16)
    grad_qkv = jnp.dot(normed_in_low.T, grad_rows_low, preferred_element_type=jnp.float32).reshape(
        width, 3, local_width
    )
    grad_normed_in = lax.psum(
        jnp.dot(grad_rows_low, qkv_low.T, preferred_element_type=jnp.float32), "tensor"
    )
    grad_in_add, gain_grad_zero, offset_grad_zero = norm_back(
        grad_normed_in, stat_in, inverse_in, norm_params[0]
    )
    input_grad = (grad_hidden + grad_in_add).astype(jnp.bfloat16)
    grad_norms = jnp.stack(
        [
            gain_grad_zero,
            offset_grad_zero,
            gain_grad_one,
            offset_grad_one,
            gain_grad_two,
            offset_grad_two,
            gain_grad_three,
            offset_grad_three,
        ]
    )
    summed = lax.psum((grad_qkv, grad_out, grad_up, grad_down, grad_norms), "dp")
    own_grads = (
        lax.dynamic_slice_in_dim(summed[0], own_start, own_rows, 0),
        lax.dynamic_slice_in_dim(summed[1], own_start, own_rows, 1),
        lax.dynamic_slice_in_dim(summed[2], own_start, own_rows, 0),
        lax.dynamic_slice_in_dim(summed[3], own_start, own_rows, 1),
        lax.dynamic_slice_in_dim(summed[4], own_start, own_rows, 1),
    )
    firsts = (qkv_first, out_first, up_first, down_first)
    seconds = (qkv_second, out_second, up_second, down_second)
    stepped = [
        moment_step(gradient, first_state, second_state)
        for gradient, first_state, second_state in zip(own_grads[:4], firsts, seconds)
    ]
    updates = [entry[2] + decay_rate * master for entry, master in zip(stepped, masters)]
    update_local = jnp.stack([jnp.sum(update * update) for update in updates])
    weight_squares, update_squares = lax.psum((weight_local, update_local), ("dp", "tensor"))
    weight_magnitude = jnp.sqrt(weight_squares)
    update_magnitude = jnp.sqrt(update_squares + trust_epsilon)
    new_masters = [
        master - learn_rate * (weight_magnitude[index] / update_magnitude[index]) * update
        for index, (master, update) in enumerate(zip(masters, updates))
    ]
    norm_first_new, norm_second_new, norm_direction = moment_step(
        own_grads[4], norm_first, norm_second
    )
    norm_new = norm_own - learn_rate * norm_direction
    matrix_norms = jnp.stack([weight_magnitude, update_magnitude])
    return (
        block_output,
        input_grad,
        new_masters[0],
        stepped[0][0],
        stepped[0][1],
        new_masters[1],
        stepped[1][0],
        stepped[1][1],
        new_masters[2],
        stepped[2][0],
        stepped[2][1],
        new_masters[3],
        stepped[3][0],
        stepped[3][1],
        norm_new,
        norm_first_new,
        norm_second_new,
        matrix_norms,
    )


def solution(mesh):
    in_specs = (
        P("dp", None),
        P("dp"),
        P(),
        P(None, None, "tensor"),
        P("tensor", None),
        P(None, "tensor"),
        P("tensor", None),
        P("dp", None, "tensor"),
        P("dp", None, "tensor"),
        P("tensor", "dp"),
        P("tensor", "dp"),
        P("dp", "tensor"),
        P("dp", "tensor"),
        P("tensor", "dp"),
        P("tensor", "dp"),
        P(None, "dp"),
        P(None, "dp"),
        P("dp", None),
    )
    out_specs = (
        P("dp", None),
        P("dp", None),
        P("dp", None, "tensor"),
        P("dp", None, "tensor"),
        P("dp", None, "tensor"),
        P("tensor", "dp"),
        P("tensor", "dp"),
        P("tensor", "dp"),
        P("dp", "tensor"),
        P("dp", "tensor"),
        P("dp", "tensor"),
        P("tensor", "dp"),
        P("tensor", "dp"),
        P("tensor", "dp"),
        P(None, "dp"),
        P(None, "dp"),
        P(None, "dp"),
        P(),
    )
    return jax.shard_map(shards, mesh=mesh, in_specs=in_specs, out_specs=out_specs, check_vma=False)
```

profile of v0, /device:TPU:0, one launch (start us, length us, event | category | flops | bytes accessed | tf_op | source)
XLA Modules:
  0.0 771.3 jit_solution(17628316393183005444)
XLA Ops:
  8.5 1.4 convert_reduce_fusion.1
  9.9 1.6 fusion.19
  11.6 0.6 fusion.90
  12.7 2.3 copy.41
  15.0 1.2 fusion.42
  16.6 0.9 fusion.93
  18.2 1.3 copy-done
  19.5 0.8 fusion.41
  20.7 1.8 fusion.62
  22.6 54.2 %all-reduce.8.cloned.1.call-done = f32[512,1024]{1,0:T(8,128)} async-done(((f32[512,1024]{1,0:T(8,128)}), f32[512,1024]{1,0:T(8,128)}) %all-reduce.8.cloned.1.call-update) | async-done | bytes 2097168 | tf_op jit(solution)/shard_map/psum | solution.py:164
  76.8 2.5 reduce_sum.309
  79.3 0.8 broadcast_multiply_fusion.10
  80.9 1.6 fusion.89
  83.3 7.2 multiply_convert_fusion.2
  90.6 1.0 copy-done.18
  91.6 2.6 fusion.48
  94.4 51.4 %all-reduce.10.cloned.1.call-done = f32[512,1024]{1,0:T(8,128)} async-done(((f32[512,1024]{1,0:T(8,128)}), f32[512,1024]{1,0:T(8,128)}) %all-reduce.10.cloned.1.call-update) | async-done | bytes 2097168 | tf_op jit(solution)/shard_map/psum | solution.py:171
  145.8 2.3 reduce_sum.313
  148.2 0.8 broadcast_multiply_fusion.8
  149.0 1.9 multiply_reduce_fusion.5
  151.0 2.9 fusion.27
  153.9 1.9 fusion.22
  155.8 0.7 copy-done.40
  156.5 1.1 copy-done.77
  157.5 1.8 add_convert_fusion
  159.4 1.0 copy-done.22
  160.3 2.7 fusion.52
  163.1 0.7 log_add_fusion
  163.8 50.8 %all-reduce.12.cloned.1.call-done = f32[512,1024]{1,0:T(8,128)} async-done(((f32[512,1024]{1,0:T(8,128)}), f32[512,1024]{1,0:T(8,128)}) %all-reduce.12.cloned.1.call-update) | async-done | bytes 2097168 | tf_op jit(solution)/shard_map/psum | solution.py:184
  214.7 3.2 multiply_reduce_fusion.1
  217.9 4.0 multiply_reduce_fusion.2
  222.0 0.6 multiply_convert_fusion.1
  222.7 0.7 copy-done.7
  223.3 0.6 copy-done.16
  224.5 1.2 copy-done.1
  225.6 0.8 fusion.35
  226.4 2.0 multiply_reduce_fusion
  228.4 1.2 multiply_convert_fusion
  229.7 0.8 fusion.38
  231.4 0.9 copy-done.24
  232.8 2.3 fusion.94
  235.4 4.8 fusion.96
  240.3 3.4 fusion.82
  243.8 1.5 fusion.95
  245.3 3.0 fusion.44
  248.4 38.3 %all-reduce.14.cloned.1.call-done = f32[512,1024]{1,0:T(8,128)} async-done(((f32[512,1024]{1,0:T(8,128)}), f32[512,1024]{1,0:T(8,128)}) %all-reduce.14.cloned.1.call-update) | async-done | bytes 2097168 | tf_op jit(solution)/shard_map/psum | solution.py:231
  286.7 2.5 fusion.18
  289.3 39.4 %psum.87 = f32[8,1024]{1,0:T(8,128)} all-reduce(f32[8,1024]{1,0:T(8,128)S(1)} %stack.100), channel_id=1, replica_groups=mesh['dp'=8,'tensor'=4] {'dp'}, use_global_device_ids=true, to_apply=%region_45.46 | all-reduce | flops 8192 | bytes 65536 | tf_op jit(solution)/shard_map/psum | solution.py:250
  328.7 3.3 fusion.17
  332.1 360.4 %all-reduce.16.cloned.1.call-done = (f32[1024,3,256]{2,0,1:T(8,128)}, f32[1024,1024]{1,0:T(8,128)}, f32[1024,1024]{1,0:T(8,128)}, f32[256,1024]{1,0:T(8,128)}) async-done(((f32[1024,3,256]{2,0,1:T(8,128)}, f32[1024,1024]{1,0:T(8,128)}, f32[1024,1024]{1,0:T(8,128)}, f32[256,1024]{1,0:T(8,128)}), (f32[1024,3,256]{2,0,1:T(8,128)}, f32[1024,1024]{1,0:T(8,128)}, f32[1024,1024]{1,0:T(8,128)}, ...) | async-done | bytes 12582928 | tf_op jit(solution)/shard_map/psum | solution.py:250
  692.5 3.0 multiply_reduce_fusion.15
  695.5 3.3 multiply_reduce_fusion.12
  698.8 3.3 multiply_reduce_fusion.11
  702.1 2.4 multiply_reduce_fusion.17
  704.6 2.7 pad_maximum_fusion.8
  707.2 2.7 pad_maximum_fusion.7
  709.9 1.3 multiply_subtract_fusion.6
  711.3 39.2 %all-reduce = (f32[4]{0:T(128)S(1)}, f32[4]{0:T(128)S(1)}) all-reduce(f32[4]{0:T(128)S(1)} %pad_maximum_fusion.7, f32[4]{0:T(128)S(1)} %pad_maximum_fusion.8), channel_id=1, replica_groups=mesh['dp'=8,'tensor'=4] {'dp','tensor'}, use_global_device_ids=true, to_apply=%region_27.28 | all-reduce | flops 8 | bytes 64 | tf_op jit(solution)/shard_map/psum | solution.py:266
  750.4 0.7 fusion.91
  751.1 0.6 fusion.92
  757.6 1.9 multiply_subtract_fusion
  759.5 1.9 multiply_subtract_fusion.1
  761.4 1.6 multiply_subtract_fusion.5
  762.9 1.8 multiply_subtract_fusion.2
  (193 shorter events, 7.5 us)
Async XLA Ops:
  7.2 4.4 copy-start.43
  7.2 69.6 %all-reduce.8.cloned.1.call-start = ((), (), s32[]{:S(2)}) async-start(), calls=%async_computation | async-start | bytes 4194304 | tf_op jit(solution)/shard_map/psum | solution.py:164
  9.9 5.1 copy-start.52
  11.6 3.4 copy-start.61
  12.2 2.8 copy-start.47
  12.2 2.8 copy-start.73
  12.2 70.7 %copy-start.44 = (f32[1,1024]{1,0:T(1,128)}, f32[1,1024]{1,0:T(1,128)S(1)}, u32[]{:S(2)}) copy-start(f32[1,1024]{1,0:T(1,128)S(1)} %get-tuple-element.86) | copy-start | bytes 12292
  12.7 2.3 copy-start.6
  16.2 1.9 copy-start.19
  17.5 1.9 copy-start
  17.5 2.0 copy-start.56
  22.6 123.2 %all-reduce.10.cloned.1.call-start = ((), (), s32[]{:S(2)}) async-start(), calls=%async_computation.1 | async-start | bytes 4194304 | tf_op jit(solution)/shard_map/psum | solution.py:171
  76.8 3.3 copy-start.2
  79.3 1.6 copy-start.3
  80.5 2.0 copy-start.54
  80.9 2.2 copy-start.13
  82.5 8.1 %copy-start.49 = (f32[512]{0:T(512)}, f32[512]{0:T(512)S(1)}, u32[]{:S(2)}) copy-start(f32[512]{0:T(512)S(1)} %broadcast_multiply_fusion.9) | copy-start | bytes 6148
  82.9 7.7 copy-start.58
  83.3 8.2 %copy-start.39 = (f32[1024,1024]{1,0:T(8,128)S(1)}, f32[1024,1024]{1,0:T(8,128)}, u32[]{:S(2)}) copy-start(f32[1024,1024]{1,0:T(8,128)} %param.24) | copy-start | bytes 12582916
  94.2 120.4 %all-reduce.12.cloned.1.call-start = ((), (), s32[]{:S(2)}) async-start(), calls=%async_computation.2 | async-start | bytes 4194304 | tf_op jit(solution)/shard_map/psum | solution.py:184
  148.2 2.8 copy-start.5
  150.9 3.0 copy-start.9
  150.9 3.0 copy-start.63
  151.0 4.8 copy-start.78
  153.9 2.6 copy-start.40
  153.9 3.6 copy-start.77
  155.8 3.5 copy-start.17
  157.5 2.8 copy-start.14
  163.0 123.7 %all-reduce.14.cloned.1.call-start = ((), (), s32[]{:S(2)}) async-start(), calls=%async_computation.3 | async-start | bytes 4194304 | tf_op jit(solution)/shard_map/psum | solution.py:231
  214.6 3.3 copy-start.4
  214.6 3.3 copy-start.10
  214.6 3.3 copy-start.45
  214.6 3.3 copy-start.50
  214.6 3.3 copy-start.55
  214.7 3.3 copy-start.59
  222.0 2.0 copy-start.16
  222.0 3.6 copy-start.1
  224.0 2.4 copy-start.11
  224.0 1.7 copy-start.70
  231.1 1.7 copy-start.21
  235.1 5.2 copy-start.46
  235.1 5.2 copy-start.51
  235.1 5.2 copy-start.60
  235.1 5.2 copy-start.76
  235.1 457.4 %all-reduce.16.cloned.1.call-start = ((), (), s32[]{:S(2)}) async-start(), calls=%async_computation.4 | async-start | bytes 25165824 | tf_op jit(solution)/shard_map/psum | solution.py:250
  235.4 4.9 copy-start.23
  240.3 3.5 copy-start.12
  243.7 1.5 copy-start.53
  248.3 40.9 %copy-start.64 = (f32[1024]{0:T(1024)S(1)}, f32[1024]{0:T(1024)}, u32[]{:S(2)}) copy-start(f32[1024]{0:T(1024)} %get-tuple-element.22) | copy-start | bytes 12292
  248.3 40.9 %copy-start.65 = (f32[1024]{0:T(1024)S(1)}, f32[1024]{0:T(1024)}, u32[]{:S(2)}) copy-start(f32[1024]{0:T(1024)} %get-tuple-element.33) | copy-start | bytes 12292
  248.4 40.9 %copy-start.66 = (f32[1024]{0:T(1024)S(1)}, f32[1024]{0:T(1024)}, u32[]{:S(2)}) copy-start(f32[1024]{0:T(1024)} %get-tuple-element.18) | copy-start | bytes 12292
  248.4 40.9 %copy-start.67 = (f32[1024]{0:T(1024)S(1)}, f32[1024]{0:T(1024)}, u32[]{:S(2)}) copy-start(f32[1024]{0:T(1024)} %get-tuple-element.29) | copy-start | bytes 12292
  248.4 40.9 %copy-start.68 = (f32[1024]{0:T(1024)S(1)}, f32[1024]{0:T(1024)}, u32[]{:S(2)}) copy-start(f32[1024]{0:T(1024)} %get-tuple-element.20) | copy-start | bytes 12292
  248.4 40.9 %copy-start.69 = (f32[1024]{0:T(1024)S(1)}, f32[1024]{0:T(1024)}, u32[]{:S(2)}) copy-start(f32[1024]{0:T(1024)} %get-tuple-element.30) | copy-start | bytes 12292
  248.4 80.3 %copy-start.8 = (f32[512,1024]{1,0:T(8,128)S(1)}, f32[512,1024]{1,0:T(8,128)}, u32[]{:S(2)}) copy-start(f32[512,1024]{1,0:T(8,128)} %copy-done.7) | copy-start | bytes 6291460
  328.7 363.8 %copy-start.38 = (f32[128,3,256]{2,0,1:T(8,128)S(1)}, f32[128,3,256]{2,0,1:T(8,128)}, u32[]{:S(2)}) copy-start(f32[128,3,256]{2,0,1:T(8,128)} %param.25) | copy-start | bytes 1179652
  332.1 363.5 %copy-start.26 = (f32[128,1024]{1,0:T(8,128)S(1)}, f32[128,1024]{1,0:T(8,128)}, u32[]{:S(2)}) copy-start(f32[128,1024]{1,0:T(8,128)} %param.29) | copy-start | bytes 1572868
  332.1 363.5 %copy-start.27 = (f32[128,1024]{1,0:T(8,128)S(1)}, f32[128,1024]{1,0:T(8,128)}, u32[]{:S(2)}) copy-start(f32[128,1024]{1,0:T(8,128)} %param.30) | copy-start | bytes 1572868
  695.5 3.3 copy-start.28
  695.5 3.3 copy-start.29
  698.8 3.3 copy-start.41
  698.8 3.3 copy-start.42
  698.8 11.1 %copy-start.71 = (f32[8,128]{1,0:T(8,128)S(1)}, f32[8,128]{1,0:T(8,128)}, u32[]{:S(2)}) copy-start(f32[8,128]{1,0:T(8,128)} %param.33) | copy-start | bytes 12292
  698.8 11.1 %copy-start.72 = (f32[8,128]{1,0:T(8,128)S(1)}, f32[8,128]{1,0:T(8,128)}, u32[]{:S(2)}) copy-start(f32[8,128]{1,0:T(8,128)} %param.34) | copy-start | bytes 12292
  (20 other events, 22.7 us)
Sparse Core Ops, SparseCore 0:
  22.7 54.0 all-reduce.7
  94.3 51.4 all-reduce.9
  163.1 51.4 all-reduce.11
  235.2 51.4 all-reduce.13
  291.3 401.1 all-reduce.15
where the time goes:
time: 772 us; the launch traced here: 771 us
  waiting for transfers between devices  555 us (72%)
  blocking collectives  78.5 us (10%)
  other arithmetic  62.8 us (8%)
  matrix products  38.6 us (5%)
  between operations  20.6 us (3%)
  local copies, waits for them, and re-layouts  14.9 us (2%)
    psum x1, waiting for transfers between devices, shards(): lax.psum((grad_qkv, grad_out, grad_up, grad_down, grad_norms), 'dp')  360 us
    psum x1, waiting for transfers between devices, shards(): lax.psum(jnp.dot(attn_low, out_low, preferred_element_type=jnp.float32),...  54.2 us
    psum x1, waiting for transfers between devices, shards(): lax.psum(jnp.dot(active_low, down_low, preferred_element_type=jnp.float32...  51.4 us
    psum x1, waiting for transfers between devices, shards(): lax.psum(jnp.dot(grad_up_low, up_low.T, preferred_element_type=jnp.float3...  50.8 us
    psum x1, blocking collectives, shards(): lax.psum((grad_qkv, grad_out, grad_up, grad_down, grad_norms), 'dp')  39.4 us
    psum x1, blocking collectives, shards(): lax.psum((weight_local, update_local), ('dp', 'tensor'))  39.2 us
    psum x1, waiting for transfers between devices, shards(): lax.psum(jnp.dot(grad_rows_low, qkv_low.T, preferred_element_type=jnp.flo...  38.3 us
  transfers between devices with their start and end apart: 5, of which 5 were waited for; matrix products, arithmetic and copies ran while one was open for 3% of the time, Pallas kernels for 0%

commit v1 on v0

v1 whole, which is shorter than its diff:
```python
import functools

import jax
import jax.numpy as jnp
import numpy as np
from jax import lax
from jax.experimental import pallas as pl
from jax.experimental.pallas import tpu as pltpu
from jax.sharding import PartitionSpec as P

HEAD_DIM = 64
STEP = 10
CHUNKS = 2
LANES = 128

norm_epsilon = 1e-05
rotary_base = 10000.0
mask_fill = -1000000000.0
first_decay = 0.9
second_decay = 0.999
adam_epsilon = 1e-06
trust_epsilon = 1e-06
decay_rate = 0.01
learn_rate = 0.25

LOW = jnp.bfloat16
WIDE = jnp.float32
VMEM = pl.BlockSpec(memory_space=pltpu.VMEM)
SMEM = pl.BlockSpec(memory_space=pltpu.SMEM)
ANY = pl.BlockSpec(memory_space=pl.ANY)


def log2_of(count):
    bits = 0
    while (1 << bits) < count:
        bits += 1
    return bits


def after(values, *earlier):
    return lax.optimization_barrier((values,) + earlier)[0]


def swap(values, axis, distance):
    count = lax.axis_size(axis)
    return lax.ppermute(values, axis, [(i, i ^ distance) for i in range(count)])


def sum_rows(send, keep):
    mine, theirs = keep, swap(send, "tensor", 1)
    for bit in range(1, log2_of(lax.axis_size("tensor"))):
        mine = mine + theirs
        theirs = swap(mine, "tensor", 1 << bit)
    return mine, theirs


def sum_all(values, axis, most=2):
    bits = log2_of(lax.axis_size(axis))
    start = 0
    while start < bits:
        taken = min(most, bits - start)
        terms = [values] + [
            swap(values, axis, distance << start) for distance in range(1, 1 << taken)
        ]
        while len(terms) > 1:
            terms = [terms[i] + terms[i + 1] for i in range(0, len(terms), 2)]
        values = terms[0]
        start += taken
    return values


def chunk_order(count, bits):
    order = [0]
    for bit in reversed(bits):
        order = order + [distance ^ (1 << bit) for distance in order]
    return order


def scatter_terms(send, keep, bits):
    terms = [keep, swap(send, "dp", 1 << bits[0])]
    size = keep.shape[0]
    for bit in bits[1:]:
        size //= 2
        outgoing = terms[0][size : 2 * size]
        for term in terms[1:]:
            outgoing = outgoing + term[size : 2 * size]
        terms.append(swap(outgoing, "dp", 1 << bit))
    return terms


def normalize(values):
    center = values - jnp.mean(values, axis=-1, keepdims=True)
    inverse = lax.rsqrt(jnp.mean(center * center, axis=-1, keepdims=True) + norm_epsilon)
    return center * inverse, inverse


def norm_back(incoming, normed, inverse, gain):
    scaled = incoming * gain
    inner = (
        scaled
        - jnp.mean(scaled, axis=-1, keepdims=True)
        - normed * jnp.mean(scaled * normed, axis=-1, keepdims=True)
    )
    gain_grad = jnp.sum(incoming * normed, axis=0, keepdims=True)
    return inner * inverse, gain_grad, jnp.sum(incoming, axis=0, keepdims=True)


def rotary_tables(length):
    half = HEAD_DIM // 2
    lane = np.arange(LANES)
    frequency = (rotary_base ** (-((lane % half).astype(np.float32) * 2.0 / HEAD_DIM))).astype(np.float32)
    angles = np.arange(length, dtype=np.float32)[:, None] * frequency[None, :]
    sign = np.where(lane % HEAD_DIM < half, -1.0, 1.0)
    cosine = np.cos(angles.astype(np.float64)).astype(np.float32)
    sine = (np.sin(angles.astype(np.float64)) * sign[None, :]).astype(np.float32)
    return jnp.asarray(cosine), jnp.asarray(sine)


def turn(values, cosine, sine):
    half = HEAD_DIM // 2
    lane = lax.broadcasted_iota(jnp.int32, (1, LANES), 1)
    first = lax.rem(lane, HEAD_DIM) < half
    tiles = []
    for start in range(0, values.shape[1], LANES):
        tile = values[:, start : start + LANES]
        other = jnp.where(
            first, pltpu.roll(tile, LANES - half, 1), pltpu.roll(tile, half, 1)
        )
        tiles.append(tile * cosine + other * sine)
    return tiles[0] if len(tiles) == 1 else jnp.concatenate(tiles, axis=1)


def gelu_mass(up):
    return 0.5 * (1.0 + lax.erf(up * (0.5**0.5)))


def dot(left, right):
    return jnp.dot(left, right, preferred_element_type=WIDE)


def dot_rows(left, right):
    return lax.dot_general(left, right, (((0,), (0,)), ((), ())), preferred_element_type=WIDE)


def dot_wide(left, right):
    return lax.dot_general(left, right, (((1,), (1,)), ((), ())), preferred_element_type=WIDE)


def of_head(values, head):
    lane = lax.broadcasted_iota(jnp.int32, (1, values.shape[1]), 1)
    mine = (lane >= head * HEAD_DIM) & (lane < (head + 1) * HEAD_DIM)
    return jnp.where(mine, values, jnp.zeros_like(values))


def core_index():
    return lax.rem(lax.axis_index("tensor"), 2)


def shaped(*shape, kind=WIDE):
    return jax.ShapeDtypeStruct(shape, kind)


def call(kernel, outs, args, specs=None, flops=0, scratch=(), megabytes=40, name=None):
    moved = sum(a.size * a.dtype.itemsize for a in args) + sum(
        int(np.prod(o.shape)) * jnp.dtype(o.dtype).itemsize for o in outs
    )
    blocks = any(spec.block_shape is not None for spec in specs or [])
    return pl.pallas_call(
        kernel,
        grid=(1,) if blocks else (),
        out_shape=tuple(outs),
        in_specs=specs or [VMEM] * len(args),
        out_specs=tuple([VMEM] * len(outs)),
        scratch_shapes=list(scratch),
        compiler_params=pltpu.CompilerParams(vmem_limit_bytes=megabytes * 1024 * 1024),
        cost_estimate=pl.CostEstimate(flops=int(flops), bytes_accessed=int(moved), transcendentals=0),
        name=name,
    )(*args)


def project(normed, weights, cosine, sine):
    query = turn(dot(normed, weights[0]), cosine, sine).astype(LOW)
    keys = turn(dot(normed, weights[1]), cosine, sine).astype(LOW)
    return query, keys, dot(normed, weights[2]).astype(LOW)


def attend(query, keys, values, first_row, live_len):
    rows, reach = query.shape[0], keys.shape[0]
    row = first_row + lax.broadcasted_iota(jnp.int32, (rows, reach), 0)
    column = lax.broadcasted_iota(jnp.int32, (rows, reach), 1)
    visible = (column <= row) & (column < live_len)
    lane = lax.broadcasted_iota(jnp.int32, (1, LANES), 1)
    mixed = jnp.zeros((rows, query.shape[1]), WIDE)
    masses = jnp.zeros((rows, LANES), WIDE)
    for head in range(query.shape[1] // HEAD_DIM):
        scores = dot_wide(of_head(query, head), keys) * HEAD_DIM ** (-0.5)
        scores = jnp.where(visible, scores, mask_fill)
        top = jnp.max(scores, axis=-1, keepdims=True)
        expo = jnp.exp(scores - top)
        total = jnp.sum(expo, axis=-1, keepdims=True)
        probs = (expo * (1.0 / total)).astype(LOW)
        mixed = mixed + dot(probs, of_head(values, head))
        masses = jnp.where(lane == head, top + jnp.log(total), masses)
    live = first_row + lax.broadcasted_iota(jnp.int32, (rows, 1), 0) < live_len
    return jnp.where(live, mixed, 0.0).astype(LOW), masses


def split_rows(left_ref, right, send_ref, keep_ref, how):
    half = send_ref.shape[0]
    core = core_index()
    send_ref[...] = how(left_ref[pl.ds((1 - core) * half, half), :], right)
    keep_ref[...] = how(left_ref[pl.ds(core * half, half), :], right)


def first_kernel(
    live_ref, x_ref, norm_ref, cos_ref, sin_ref, qkv_ref, out_ref,
    qkv_low_ref, out_low_ref, normed_ref, q_ref, k_ref, v_ref, attn_ref, mass_ref, send_ref, keep_ref,
    qkv_in, out_in, arrived,
):
    copies = [
        pltpu.make_async_copy(qkv_ref.at[j], qkv_in.at[j], arrived.at[j]) for j in range(3)
    ]
    copies.append(pltpu.make_async_copy(out_ref, out_in, arrived.at[3]))
    for copy in copies:
        copy.start()
    stat, _ = normalize(x_ref[...].astype(WIDE))
    normed = (stat * norm_ref[0:1, :] + norm_ref[1:2, :]).astype(LOW)
    normed_ref[...] = normed
    weights = []
    for j in range(3):
        copies[j].wait()
        weights.append(qkv_in[j].astype(LOW))
        qkv_low_ref[j] = weights[j]
    query, keys, values = project(normed, weights, cos_ref[...], sin_ref[...])
    q_ref[...], k_ref[...], v_ref[...] = query, keys, values
    attn_ref[...], mass_ref[...] = attend(query, keys, values, 0, live_ref[0])
    copies[3].wait()
    out_low = out_in[...].astype(LOW)
    out_low_ref[...] = out_low
    split_rows(attn_ref, out_low, send_ref, keep_ref, dot)


def next_kernel(
    live_ref, x_ref, norm_ref, cos_ref, sin_ref, qkv_low_ref, out_low_ref, *refs, first_row
):
    earlier = first_row // x_ref.shape[0]
    k_before, v_before = refs[:earlier], refs[earlier : 2 * earlier]
    normed_ref, q_ref, k_ref, v_ref, attn_ref, mass_ref, send_ref, keep_ref = refs[2 * earlier :]
    stat, _ = normalize(x_ref[...].astype(WIDE))
    normed = (stat * norm_ref[0:1, :] + norm_ref[1:2, :]).astype(LOW)
    normed_ref[...] = normed
    weights = [qkv_low_ref[j] for j in range(3)]
    query, keys, values = project(normed, weights, cos_ref[...], sin_ref[...])
    q_ref[...], k_ref[...], v_ref[...] = query, keys, values
    keys = jnp.concatenate([ref[...] for ref in k_before] + [keys], axis=0)
    values = jnp.concatenate([ref[...] for ref in v_before] + [values], axis=0)
    attn_ref[...], mass_ref[...] = attend(query, keys, values, first_row, live_ref[0])
    split_rows(attn_ref, out_low_ref[...], send_ref, keep_ref, dot)


def middle_kernel(first_row, x_ref, norm_ref, mine_ref, theirs_ref, branch_ref, hidden_ref, normed_ref):
    half = mine_ref.shape[0]
    branch = mine_ref[...] + theirs_ref[...]
    branch_ref[...] = branch
    stat, _ = normalize(branch)
    inputs = x_ref[pl.ds(first_row + core_index() * half, half), :].astype(WIDE)
    hidden = inputs + stat * norm_ref[2:3, :] + norm_ref[3:4, :]
    hidden_ref[...] = hidden
    stat, _ = normalize(hidden)
    normed_ref[...] = stat * norm_ref[4:5, :] + norm_ref[5:6, :]


def mlp_kernel(own_ref, other_ref, up_w_ref, down_w_ref, normed_ref, up_ref, active_ref, send_ref, keep_ref):
    half = own_ref.shape[0]
    normed = jnp.concatenate([own_ref[...].astype(LOW), other_ref[...].astype(LOW)], axis=0)
    normed_ref[...] = normed
    step = min(256, up_w_ref.shape[1])
    total = None
    for start in range(0, up_w_ref.shape[1], step):
        block = slice(start, start + step)
        up = dot(normed, up_w_ref[:, block])
        up_ref[:, block] = up
        active = (up * gelu_mass(up)).astype(LOW)
        active_ref[:, block] = active
        product = dot(active, down_w_ref[block, :])
        total = product if total is None else total + product
    keep_ref[...] = total[:half]
    send_ref[...] = total[half:]


def loss_kernel(
    first_row, grad_ref, norm_ref, hidden_ref, mine_ref, theirs_ref, block_ref, back_ref, sums_ref
):
    half = mine_ref.shape[0]
    stat, inverse = normalize(mine_ref[...] + theirs_ref[...])
    block_ref[...] = hidden_ref[...] + stat * norm_ref[6:7, :] + norm_ref[7:8, :]
    incoming = grad_ref[pl.ds(first_row + core_index() * half, half), :].astype(WIDE)
    back, gain, offset = norm_back(incoming, stat, inverse, norm_ref[6:7, :])
    back_ref[...] = back
    sums_ref[0:1, :] = gain
    sums_ref[1:2, :] = offset


def mlp_back_kernel(
    own_ref, other_ref, up_ref, up_w_ref, down_w_ref, grad_mlp_ref, grad_up_ref, send_ref, keep_ref
):
    half = own_ref.shape[0]
    grad_mlp = jnp.concatenate([own_ref[...].astype(LOW), other_ref[...].astype(LOW)], axis=0)
    grad_mlp_ref[...] = grad_mlp
    step = min(256, up_w_ref.shape[1])
    total = None
    for start in range(0, up_w_ref.shape[1], step):
        block = slice(start, start + step)
        up = up_ref[:, block]
        slope = gelu_mass(up) + up * jnp.exp(-0.5 * up * up) * float((2.0 * np.pi) ** -0.5)
        grad_up = (dot_wide(grad_mlp, down_w_ref[block, :]) * slope).astype(LOW)
        grad_up_ref[:, block] = grad_up
        product = dot_wide(grad_up, up_w_ref[:, block])
        total = product if total is None else total + product
    keep_ref[...] = total[:half]
    send_ref[...] = total[half:]


def norms_back_kernel(
    first_row, grad_ref, norm_ref, hidden_ref, branch_ref, mine_ref, theirs_ref,
    grad_hidden_ref, back_ref, sums_ref,
):
    half = mine_ref.shape[0]
    stat, inverse = normalize(hidden_ref[...])
    back, gain, offset = norm_back(
        mine_ref[...] + theirs_ref[...], stat, inverse, norm_ref[4:5, :]
    )
    incoming = grad_ref[pl.ds(first_row + core_index() * half, half), :].astype(WIDE)
    grad_hidden = incoming + back
    grad_hidden_ref[...] = grad_hidden
    sums_ref[2:3, :] = gain
    sums_ref[3:4, :] = offset
    stat, inverse = normalize(branch_ref[...])
    back, gain, offset = norm_back(grad_hidden, stat, inverse, norm_ref[2:3, :])
    back_ref[...] = back
    sums_ref[0:1, :] = gain
    sums_ref[1:2, :] = offset


def attention_back_kernel(live_ref, out_low_ref, cos_ref, sin_ref, *refs, chunks):
    groups = [refs[i * chunks : (i + 1) * chunks] for i in range(6)]
    own, other, query_refs, key_refs, value_refs, mass_refs = groups
    grad_branch_ref, rows_ref = refs[6 * chunks : 6 * chunks + 2]
    keys_sum, values_sum = refs[6 * chunks + 2 :]
    half = own[0].shape[0]
    part = 2 * half
    core = core_index()
    live_len = live_ref[0]
    local = rows_ref.shape[1] // 3
    heads = local // HEAD_DIM
    for c in range(chunks):
        grad_branch_ref[pl.ds(c * part + core * half, half), :] = own[c][...].astype(LOW)
        grad_branch_ref[pl.ds(c * part + (1 - core) * half, half), :] = other[c][...].astype(LOW)
    keys_all = jnp.concatenate([ref[...] for ref in key_refs], axis=0)
    values_all = jnp.concatenate([ref[...] for ref in value_refs], axis=0)
    for c in range(chunks):
        reach = (c + 1) * part
        first_row = c * part
        row = first_row + lax.broadcasted_iota(jnp.int32, (part, reach), 0)
        column = lax.broadcasted_iota(jnp.int32, (part, reach), 1)
        visible = (column <= row) & (column < live_len)
        live = first_row + lax.broadcasted_iota(jnp.int32, (part, 1), 0) < live_len
        grad_attn = dot_wide(grad_branch_ref[first_row : first_row + part, :], out_low_ref[...])
        grad_mixed = jnp.where(live, grad_attn, 0.0).astype(LOW)
        query, masses = query_refs[c][...], mass_refs[c][...]
        keys, values = keys_all[:reach], values_all[:reach]
        grad_query = jnp.zeros((part, local), WIDE)
        grad_keys = jnp.zeros((reach, local), WIDE)
        grad_values = jnp.zeros((reach, local), WIDE)
        for head in range(heads):
            query_h, grad_h = of_head(query, head), of_head(grad_mixed, head)
            scores = dot_wide(query_h, keys) * HEAD_DIM ** (-0.5)
            scores = jnp.where(visible, scores, mask_fill)
            probs = jnp.exp(scores - masses[:, head : head + 1])
            grad_values = grad_values + dot_rows(probs.astype(LOW), grad_h)
            grad_probs = dot_wide(grad_h, values)
            inner = jnp.sum(grad_probs * probs, axis=-1, keepdims=True)
            grad_scores = (probs * (grad_probs - inner)).astype(LOW)
            grad_query = grad_query + dot(grad_scores, of_head(keys, head))
            grad_keys = grad_keys + dot_rows(grad_scores, query_h)
        cosine = cos_ref[first_row : first_row + part, :]
        sine = sin_ref[first_row : first_row + part, :]
        grad_query = turn(grad_query * HEAD_DIM ** (-0.5), cosine, -sine)
        rows_ref[first_row : first_row + part, 0:local] = grad_query.astype(LOW)
        if c == 0:
            keys_sum[0:reach, :] = grad_keys
            values_sum[0:reach, :] = grad_values
        else:
            keys_sum[0:first_row, :] += grad_keys[:first_row]
            keys_sum[first_row:reach, :] = grad_keys[first_row:]
            values_sum[0:first_row, :] += grad_values[:first_row]
            values_sum[first_row:reach, :] = grad_values[first_row:]
    grad_keys = turn(keys_sum[...] * HEAD_DIM ** (-0.5), cos_ref[...], -sin_ref[...])
    rows_ref[:, local : 2 * local] = grad_keys.astype(LOW)
    rows_ref[:, 2 * local : 3 * local] = values_sum[...].astype(LOW)


def picked_columns(refs, distances, own):
    rank = lax.axis_index("dp")
    blocks = []
    for distance in distances:
        start = pl.multiple_of(lax.bitwise_xor(rank, distance) * own, own)
        pieces = [ref[:, pl.ds(start, own)].astype(LOW) for ref in refs]
        blocks.append(pieces[0] if len(pieces) == 1 else jnp.concatenate(pieces, axis=0))
    return blocks[0] if len(blocks) == 1 else jnp.concatenate(blocks, axis=1)


def whole_rows(refs, window):
    pieces = [ref[:, window[0] : window[1]].astype(LOW) for ref in refs]
    return pieces[0] if len(pieces) == 1 else jnp.concatenate(pieces, axis=0)


def owned_columns_kernel(*refs, pairs, jobs, own):
    (lefts, rights), outs = pairs, refs[sum(pairs) :]
    left, right = refs[:lefts], refs[lefts : lefts + rights]
    for (distances, window), out_ref in zip(jobs, outs):
        rows = whole_rows(left, window)
        product = dot_rows(rows, picked_columns(right, distances, own))
        for place in range(len(distances)):
            out_ref[place] = product[:, place * own : (place + 1) * own]


def owned_rows_kernel(*refs, pairs, jobs, own):
    (lefts, rights), outs = pairs, refs[sum(pairs) :]
    left, right = refs[:lefts], refs[lefts : lefts + rights]
    for (distances, window), out_ref in zip(jobs, outs):
        product = dot_rows(picked_columns(left, distances, own), whole_rows(right, window))
        for place in range(len(distances)):
            out_ref[place] = product[place * own : (place + 1) * own, :]


def owned_parts_kernel(*refs, pairs, jobs, own):
    (lefts, rights), outs = pairs, refs[sum(pairs) :]
    left, right = refs[:lefts], refs[lefts : lefts + rights]
    for (distances, window), out_ref in zip(jobs, outs):
        local = out_ref.shape[3]
        columns = (window[0] * local, window[1] * local)
        product = dot_rows(picked_columns(left, distances, own), whole_rows(right, columns))
        for place in range(len(distances)):
            for j in range(window[1] - window[0]):
                out_ref[place, j] = product[
                    place * own : (place + 1) * own, j * local : (j + 1) * local
                ]


def rounded_kernel(*refs):
    refs[-1][...] = whole_rows(refs[:-1], (0, refs[0].shape[1]))


def narrow_products(kernel, left, right, jobs, outs, own):
    rank = lax.axis_index("dp")
    joined = []
    for arrays in (left, right):
        rows = sum(array.shape[0] for array in arrays)
        joined.append(call(rounded_kernel, [shaped(rows, arrays[0].shape[1], kind=LOW)], arrays)[0])
    results = []
    for (distances, window), out in zip(jobs, outs):
        pick = lambda array: jnp.concatenate(
            [lax.dynamic_slice_in_dim(array, (rank ^ d) * own, own, 1) for d in distances], axis=1
        )
        if kernel is owned_columns_kernel:
            product = dot_rows(joined[0][:, window[0] : window[1]], pick(joined[1]))
            product = product.reshape(-1, len(distances), own).transpose(1, 0, 2)
        elif kernel is owned_rows_kernel:
            product = dot_rows(pick(joined[0]), joined[1][:, window[0] : window[1]])
            product = product.reshape(out.shape)
        else:
            local = out.shape[3]
            columns = joined[1][:, window[0] * local : window[1] * local]
            product = dot_rows(pick(joined[0]), columns)
            product = product.reshape(len(distances), own, -1, local).transpose(0, 2, 1, 3)
        results.append(product)
    return results


def owner_products(kernel, left, right, pieces, own, send, name):
    count = lax.axis_size("dp")
    jobs, outs = [], []
    for window, bits in pieces:
        order = chunk_order(count, bits)
        order = order[count // 2 :] if send else order[: count // 2]
        jobs.append((order, window))
        size = window[1] - window[0]
        if kernel is owned_columns_kernel:
            outs.append(shaped(len(order), size, own))
        elif kernel is owned_rows_kernel:
            outs.append(shaped(len(order), own, size))
        else:
            outs.append(shaped(len(order), size, own, right[0].shape[1] // 3))
    if own % LANES:
        return narrow_products(kernel, left, right, jobs, outs, own)
    rows = sum(array.shape[0] for array in left)
    flops = 2 * rows * sum(int(np.prod(out.shape)) for out in outs)
    return call(
        functools.partial(kernel, pairs=(len(left), len(right)), jobs=jobs, own=own),
        outs,
        [*left, *right],
        flops=flops,
        name=name,
    )


def cut_windows(size):
    cut = size // 4 * 3
    return [(0, cut), (cut, size)]


def first_block(array):
    return pl.BlockSpec((1,) + array.shape[1:], lambda i: (0,) * array.ndim)


def input_back_kernel(rows_ref, qkv_low_ref, send_ref, keep_ref, *, chunks):
    half = send_ref.shape[0] // chunks
    local = qkv_low_ref.shape[2]
    core = core_index()
    for c in range(chunks):
        for target, which in ((send_ref, 1 - core), (keep_ref, core)):
            rows = rows_ref[pl.ds(c * 2 * half + which * half, half), :]
            total = None
            for j in range(3):
                product = dot_wide(rows[:, j * local : (j + 1) * local], qkv_low_ref[j])
                total = product if total is None else total + product
            target[c * half : (c + 1) * half, :] = total


def input_norm_kernel(x_ref, norm_ref, mine_ref, theirs_ref, *refs, chunks):
    grad_hidden = refs[:chunks]
    rows_ref, sums_ref = refs[chunks:]
    half = mine_ref.shape[0] // chunks
    core = core_index()
    gains = offsets = None
    for c in range(chunks):
        rows = slice(c * half, (c + 1) * half)
        inputs = x_ref[pl.ds(c * 2 * half + core * half, half), :].astype(WIDE)
        stat, inverse = normalize(inputs)
        back, gain, offset = norm_back(
            mine_ref[rows, :] + theirs_ref[rows, :], stat, inverse, norm_ref[0:1, :]
        )
        rows_ref[rows, :] = grad_hidden[c][...] + back
        gains = gain if gains is None else gains + gain
        offsets = offset if offsets is None else offsets + offset
    sums_ref[0:1, :] = gains
    sums_ref[1:2, :] = offsets


def place_kernel(mine_ref, theirs_ref, out_ref, *, chunks):
    half = theirs_ref.shape[0] // chunks
    core = core_index()
    for c in range(chunks):
        rows = slice(c * half, (c + 1) * half)
        out_ref[pl.ds((2 * c + core) * half, half), :] = mine_ref[rows, :].astype(LOW)
        out_ref[pl.ds((2 * c + 1 - core) * half, half), :] = theirs_ref[rows, :].astype(LOW)


def moment_step(gradient, first_state, second_state):
    first_new = first_decay * first_state + (1.0 - first_decay) * gradient
    second_new = second_decay * second_state + (1.0 - second_decay) * gradient * gradient
    direction = (
        first_new
        / (1.0 - first_decay**STEP)
        / (jnp.sqrt(second_new / (1.0 - second_decay**STEP)) + adam_epsilon)
    )
    return (first_new, second_new, direction)


def total_of(values):
    rows = values.reshape(-1, values.shape[-1])
    return jnp.sum(jnp.sum(rows, axis=0, keepdims=True), axis=1, keepdims=True)


def moments_kernel(master_ref, first_ref, second_ref, squares_ref, *refs, row, regions, counts):
    update_ref, first_new_ref, second_new_ref, table_ref = refs[-4:]
    at = 0
    sizes = []
    for region, count in zip(regions, counts):
        gradient = refs[at][0]
        for term in refs[at + 1 : at + count]:
            gradient = gradient + term[0]
        at += count
        first_new, second_new, direction = moment_step(
            gradient, first_ref[region], second_ref[region]
        )
        first_new_ref[region] = first_new
        second_new_ref[region] = second_new
        master = master_ref[region]
        update = direction + decay_rate * master
        update_ref[region] = update
        sizes.append((total_of(master * master), total_of(update * update)))
    table_ref[...] = squares_ref[...]
    for place, size in ((row, 0), (row + 4, 1)):
        amount = sizes[0][size]
        for other in sizes[1:]:
            amount = amount + other[size]
        table_ref[place : place + 1, :] = jnp.broadcast_to(amount, (1, LANES))


def masters_kernel(squares_ref, *refs):
    masters, updates = refs[:4], refs[4:8]
    outs, norms_ref = refs[8:12], refs[12]
    sizes = jnp.sqrt(squares_ref[0:4, :])
    steps = jnp.sqrt(squares_ref[4:8, :] + trust_epsilon)
    norms_ref[0:4, :] = sizes
    norms_ref[4:8, :] = steps
    ratio = learn_rate * (sizes / steps)
    for index in range(4):
        scale = ratio[index : index + 1, 0:1]
        if len(masters[index].shape) == 3:
            scale = scale.reshape(1, 1, 1)
        outs[index][...] = masters[index][...] - scale * updates[index][...]


def shards(
    block_input,
    lengths,
    norm_params,
    qkv_weight,
    out_weight,
    up_weight,
    down_weight,
    qkv_first,
    qkv_second,
    out_first,
    out_second,
    up_first,
    up_second,
    down_first,
    down_second,
    norm_first,
    norm_second,
    out_grad,
):
    row_count, width = block_input.shape
    local = qkv_weight.shape[2]
    hidden_units = up_weight.shape[1]
    group_count = lax.axis_size("dp")
    group_rank = lax.axis_index("dp")
    own = width // group_count
    own_start = group_rank * own
    part = row_count // CHUNKS
    half = part // 2
    chunks = range(CHUNKS)
    bits = list(range(log2_of(group_count)))
    bits_across = [1, 0] + bits[2:] if len(bits) > 1 else bits

    qkv_parts = jnp.transpose(qkv_weight, (1, 0, 2))
    cosine, sine = rotary_tables(row_count)

    weight_shapes = [shaped(3, width, local, kind=LOW), shaped(local, width, kind=LOW)]
    chunk_shapes = [
        shaped(part, width, kind=LOW),
        shaped(part, local, kind=LOW),
        shaped(part, local, kind=LOW),
        shaped(part, local, kind=LOW),
        shaped(part, local, kind=LOW),
        shaped(part, LANES),
        shaped(half, width),
        shaped(half, width),
    ]
    chunk_flops = 2 * part * width * 4 * local + 8 * part * part * local
    parts = []
    for c in chunks:
        rows = slice(c * part, (c + 1) * part)
        common = [lengths, block_input, norm_params, cosine, sine]
        row_block = lambda array, c=c: pl.BlockSpec((part, array.shape[1]), lambda i, c=c: (c, 0))
        specs = [SMEM, row_block(block_input), VMEM, row_block(cosine), row_block(sine)]
        if c == 0:
            outs = call(
                first_kernel,
                weight_shapes + chunk_shapes,
                common + [qkv_parts, out_weight],
                specs + [ANY, ANY],
                flops=chunk_flops,
                scratch=[
                    pltpu.VMEM((3, width, local), WIDE),
                    pltpu.VMEM((local, width), WIDE),
                    pltpu.SemaphoreType.DMA((4,)),
                ],
                name="attention_first",
            )
            qkv_low, out_low = outs[:2]
            parts.append(outs[2:])
        else:
            before = [p[2] for p in parts] + [p[3] for p in parts]
            parts.append(
                call(
                    functools.partial(next_kernel, first_row=c * part),
                    chunk_shapes,
                    common + [qkv_low, out_low] + before,
                    specs + [VMEM] * (2 + len(before)),
                    flops=chunk_flops,
                    name="attention_next",
                )
            )
    normed_in, query, keys, values, attn, masses, sends, keeps = zip(*parts)
    up_low = after(up_weight, sends[-1]).astype(LOW)
    down_low = after(down_weight, sends[-1]).astype(LOW)
    branch_terms = [sum_rows(sends[c], keeps[c]) for c in chunks]

    mlp_flops = 4 * part * width * hidden_units
    branch, hidden, normed_mid, up, active, mlp_terms = [], [], [], [], [], []
    for c in chunks:
        outs = call(
            functools.partial(middle_kernel, c * part),
            [shaped(half, width)] * 3,
            [block_input, norm_params, *branch_terms[c]],
            name="middle",
        )
        branch.append(outs[0])
        hidden.append(outs[1])
        other = swap(outs[2], "tensor", 1)
        outs = call(
            mlp_kernel,
            [
                shaped(part, width, kind=LOW),
                shaped(part, hidden_units),
                shaped(part, hidden_units, kind=LOW),
                shaped(half, width),
                shaped(half, width),
            ],
            [outs[2], other, up_low, down_low],
            flops=mlp_flops,
            name="mlp",
        )
        normed_mid.append(outs[0])
        up.append(outs[1])
        active.append(outs[2])
        mlp_terms.append(sum_rows(outs[3], outs[4]))

    block_rows, loss_sums, grad_final, grad_mlp, grad_up_rows, mid_terms = [], [], [], [], [], []
    down_sends = None

    down_windows = cut_windows(hidden_units)
    up_windows = down_windows
    pieces_of = lambda windows: list(zip(windows, [bits, bits_across]))

    for c in chunks:
        outs = call(
            functools.partial(loss_kernel, c * part),
            [shaped(half, width), shaped(half, width), shaped(2, width)],
            [out_grad, norm_params, hidden[c], *mlp_terms[c]],
            name="loss",
        )
        block_rows.append(outs[0])
        loss_sums.append(outs[2])
        grad_final += [outs[1], swap(outs[1], "tensor", 1)]
        mine, other = grad_final[-2:]
        if c == CHUNKS - 1:
            down_sends = owner_products(
                owned_columns_kernel, active, grad_final, pieces_of(down_windows), own, True, "down_send"
            )
            mine = after(mine, *down_sends)
        outs = call(
            mlp_back_kernel,
            [
                shaped(part, width, kind=LOW),
                shaped(part, hidden_units, kind=LOW),
                shaped(half, width),
                shaped(half, width),
            ],
            [mine, other, up[c], up_low, down_low],
            flops=mlp_flops,
            name="mlp_back",
        )
        grad_mlp.append(outs[0])
        grad_up_rows.append(outs[1])
        mid_terms.append(sum_rows(outs[2], outs[3]))
    down_keeps = owner_products(
        owned_columns_kernel, active, grad_final, pieces_of(down_windows), own, False, "down_keep"
    )
    up_sends = owner_products(
        owned_rows_kernel, normed_mid, grad_up_rows, pieces_of(up_windows), own, True, "up_send"
    )
    up_keeps = owner_products(
        owned_rows_kernel, normed_mid, grad_up_rows, pieces_of(up_windows), own, False, "up_keep"
    )
    down_terms = [
        scatter_terms(s, k, piece[1])
        for s, k, piece in zip(down_sends, down_keeps, pieces_of(down_windows))
    ]
    up_terms = [
        scatter_terms(s, k, piece[1])
        for s, k, piece in zip(up_sends, up_keeps, pieces_of(up_windows))
    ]

    grad_hidden, norms_sums, own_back, other_back = [], [], [], []
    for c in chunks:
        outs = call(
            functools.partial(norms_back_kernel, c * part),
            [shaped(half, width), shaped(half, width), shaped(4, width)],
            [out_grad, norm_params, hidden[c], branch[c], *mid_terms[c]],
            name="norms_back",
        )
        grad_hidden.append(outs[0])
        norms_sums.append(outs[2])
        own_back.append(outs[1])
        other_back.append(swap(outs[1], "tensor", 1))
    grad_branch, grad_rows = call(
        functools.partial(attention_back_kernel, chunks=CHUNKS),
        [shaped(row_count, width, kind=LOW), shaped(row_count, 3 * local, kind=LOW)],
        [lengths, out_low, cosine, sine, *own_back, *other_back, *query, *keys, *values, *masses],
        [SMEM] + [VMEM] * (3 + 6 * CHUNKS),
        flops=2 * row_count * width * local + 10 * row_count * row_count * local,
        scratch=[pltpu.VMEM((row_count, local), WIDE), pltpu.VMEM((row_count, local), WIDE)],
        name="attention_back",
    )
    qkv_pieces = [((1, 3), bits), ((0, 1), bits_across)]
    out_pieces = [((0, local), bits)]
    qkv_sends = owner_products(
        owned_parts_kernel, normed_in, [grad_rows], qkv_pieces, own, True, "qkv_send"
    )
    out_sends = owner_products(
        owned_columns_kernel, attn, [grad_branch], out_pieces, own, True, "out_send"
    )
    qkv_keeps = owner_products(
        owned_parts_kernel, normed_in, [grad_rows], qkv_pieces, own, False, "qkv_keep"
    )
    out_keeps = owner_products(
        owned_columns_kernel, attn, [grad_branch], out_pieces, own, False, "out_keep"
    )
    qkv_terms = [
        scatter_terms(s, k, piece[1]) for s, k, piece in zip(qkv_sends, qkv_keeps, qkv_pieces)
    ]
    out_terms = [
        scatter_terms(s, k, piece[1]) for s, k, piece in zip(out_sends, out_keeps, out_pieces)
    ]

    send, keep = call(
        functools.partial(input_back_kernel, chunks=CHUNKS),
        [shaped(row_count // 2, width)] * 2,
        [grad_rows, qkv_low],
        flops=2 * row_count * width * 3 * local,
        name="input_back",
    )
    in_terms = sum_rows(send, keep)
    input_rows, input_sums = call(
        functools.partial(input_norm_kernel, chunks=CHUNKS),
        [shaped(row_count // 2, width), shaped(2, width)],
        [block_input, norm_params, *in_terms, *grad_hidden],
        name="input_norm",
    )

    def place(mine, name):
        stacked = mine[0] if len(mine) == 1 else jnp.concatenate(mine, axis=0)
        theirs = swap(stacked, "tensor", 1)
        return call(
            functools.partial(place_kernel, chunks=CHUNKS),
            [shaped(row_count, width, kind=LOW)],
            [stacked, theirs],
            name=name,
        )[0]

    block_output = place(block_rows, "place_output")
    input_grad = place([input_rows], "place_input")

    def total(arrays):
        result = arrays[0]
        for array in arrays[1:]:
            result = result + array
        return result

    grad_norms = jnp.concatenate([input_sums, total(norms_sums), total(loss_sums)], axis=0)
    grad_norms = grad_norms + swap(grad_norms, "tensor", 1)
    norm_chunks = jnp.stack(
        [
            lax.dynamic_slice_in_dim(grad_norms, (group_rank ^ distance) * own, own, 1)
            for distance in chunk_order(group_count, bits)
        ]
    )
    middle = group_count // 2
    norm_gradient = total(
        [term[0] for term in scatter_terms(norm_chunks[middle:], norm_chunks[:middle], bits)]
    )
    norm_own = lax.dynamic_slice_in_dim(norm_params, own_start, own, 1)
    norm_first_new, norm_second_new, norm_direction = moment_step(
        norm_gradient, norm_first, norm_second
    )
    norm_new = norm_own - learn_rate * norm_direction

    masters = [
        jnp.transpose(lax.dynamic_slice_in_dim(qkv_weight, own_start, own, 0), (1, 0, 2)),
        lax.dynamic_slice_in_dim(out_weight, own_start, own, 1),
        lax.dynamic_slice_in_dim(up_weight, own_start, own, 0),
        lax.dynamic_slice_in_dim(down_weight, own_start, own, 1),
    ]
    states = [
        (jnp.transpose(qkv_first, (1, 0, 2)), jnp.transpose(qkv_second, (1, 0, 2))),
        (out_first, out_second),
        (up_first, up_second),
        (down_first, down_second),
    ]
    everything = slice(None)
    regions = [
        [(slice(*w), everything, everything) for w, _ in qkv_pieces],
        [(slice(*w), everything) for w, _ in out_pieces],
        [(everything, slice(*w)) for w in up_windows],
        [(slice(*w), everything) for w in down_windows],
    ]
    table = jnp.zeros((8, LANES), WIDE)
    stepped = [None] * 4
    for index, terms in ((3, down_terms), (2, up_terms), (1, out_terms), (0, qkv_terms)):
        flat = [term for piece in terms for term in piece]
        counts = [len(piece) for piece in terms]
        shape = masters[index].shape
        outs = call(
            functools.partial(moments_kernel, row=index, regions=regions[index], counts=counts),
            [shaped(*shape)] * 3 + [shaped(8, LANES)],
            [masters[index], *states[index], table, *flat],
            [VMEM] * 4 + [first_block(term) for term in flat],
            name="moments_" + ("qkv", "out", "up", "down")[index],
        )
        stepped[index] = outs[:3]
        table = outs[3]
    squares = sum_all(sum_all(table, "tensor"), "dp")
    outs = call(
        masters_kernel,
        [shaped(*master.shape) for master in masters] + [shaped(8, LANES)],
        [squares, *masters, *[entry[0] for entry in stepped]],
        name="masters",
    )
    back = lambda array: jnp.transpose(array, (1, 0, 2))
    matrix_norms = jnp.stack([outs[4][0:4, 0], outs[4][4:8, 0]])
    return (
        block_output,
        input_grad,
        back(outs[0]),
        back(stepped[0][1]),
        back(stepped[0][2]),
        outs[1],
        stepped[1][1],
        stepped[1][2],
        outs[2],
        stepped[2][1],
        stepped[2][2],
        outs[3],
        stepped[3][1],
        stepped[3][2],
        norm_new,
        norm_first_new,
        norm_second_new,
        matrix_norms,
    )


def solution(mesh):
    in_specs = (
        P("dp", None),
        P("dp"),
        P(),
        P(None, None, "tensor"),
        P("tensor", None),
        P(None, "tensor"),
        P("tensor", None),
        P("dp", None, "tensor"),
        P("dp", None, "tensor"),
        P("tensor", "dp"),
        P("tensor", "dp"),
        P("dp", "tensor"),
        P("dp", "tensor"),
        P("tensor", "dp"),
        P("tensor", "dp"),
        P(None, "dp"),
        P(None, "dp"),
        P("dp", None),
    )
    out_specs = (
        P("dp", None),
        P("dp", None),
        P("dp", None, "tensor"),
        P("dp", None, "tensor"),
        P("dp", None, "tensor"),
        P("tensor", "dp"),
        P("tensor", "dp"),
        P("tensor", "dp"),
        P("dp", "tensor"),
        P("dp", "tensor"),
        P("dp", "tensor"),
        P("tensor", "dp"),
        P("tensor", "dp"),
        P("tensor", "dp"),
        P(None, "dp"),
        P(None, "dp"),
        P(None, "dp"),
        P(),
    )
    return jax.shard_map(shards, mesh=mesh, in_specs=in_specs, out_specs=out_specs, check_vma=False)
```

time: 772 us -> 345 us (0.45)
  waiting for transfers between devices: 555 us -> 195 us
  blocking collectives: 78.5 us -> 0 us
  other arithmetic: 62.8 us -> 9.77 us
  Pallas kernels: 0 us -> 47.1 us
  starting transfers between devices: 0.61 us -> 45.9 us
  matrix products: 38.6 us -> 0 us
  local copies, waits for them, and re-layouts: 14.9 us -> 43.1 us
  between operations: 20.6 us -> 2.95 us
    psum x5 -> x0, waiting for transfers between devices: 555 us -> none  [the longest x1 360 us: shards(): lax.psum((grad_qkv, grad_out, grad_up, grad_down, grad_norms), 'dp')]
    ppermute x0 -> x54, waiting for transfers between devices: none -> 195 us  [swap(): return lax.ppermute(values, axis, [(i, i ^ distance) for i in range(count)])]
    psum x2 -> x0, blocking collectives: 78.5 us -> none  [the longest x1 39.4 us: shards(): lax.psum((grad_qkv, grad_out, grad_up, grad_down, grad_norms), 'dp')]
    pallas_call x0 -> x30, Pallas kernels: none -> 47.1 us  [call(): pl.pallas_call(kernel, grid=(1,) if blocks else (), out_shape=tuple(outs)...]
    ppermute x0 -> x54, starting transfers between devices: none -> 45.9 us  [swap(): return lax.ppermute(values, axis, [(i, i ^ distance) for i in range(count)])]
    dot_general x18 -> x0, matrix products: 38.6 us -> none  [the longest x1 7.24 us: shards(): jnp.dot(normed_mid_low, up_low, preferred_element_type=jnp.float32)]
    reduce_sum x17 -> x0, other arithmetic: 37.4 us -> none  [the longest x4 12.7 us: norm_back(): jnp.sum(incoming * normed, axis=0)]
    unnamed x159 -> x313, local copies, waits for them, and re-layouts: 12.9 us -> 36.5 us
  transfers between devices with their start and end apart: 5 -> 54, of which waited for: 5 -> 18; matrix products, arithmetic and copies ran while one was open for 3% -> 5% of each run, Pallas kernels for 0% -> 12%
where the time goes in v1:
time: 345 us; the launch traced here: 343 us
  waiting for transfers between devices  195 us (57%)
  Pallas kernels  47.1 us (14%)
  starting transfers between devices  45.9 us (13%)
  local copies, waits for them, and re-layouts  43.1 us (12%)
  other arithmetic  9.77 us (3%)
    ppermute x54, waiting for transfers between devices, swap(): return lax.ppermute(values, axis, [(i, i ^ distance) for i in range(count)])  195 us
    pallas_call x30, Pallas kernels, call(): pl.pallas_call(kernel, grid=(1,) if blocks else (), out_shape=tuple(outs)...  47.1 us
    ppermute x54, starting transfers between devices, swap(): return lax.ppermute(values, axis, [(i, i ^ distance) for i in range(count)])  45.9 us
    unnamed x313, local copies, waits for them, and re-layouts  36.5 us
  transfers between devices with their start and end apart: 54, of which 18 were waited for; matrix products, arithmetic and copies ran while one was open for 5% of the time, Pallas kernels for 12%

profile of v1, /device:TPU:0, one launch (start us, length us, event | category | flops | bytes accessed | tf_op | source)
XLA Modules:
  0.0 343.3 jit_solution(9253527944918739658)
XLA Ops:
  1.3 1.2 copy-done
  2.5 1.9 copy-done.18
  7.1 1.2 copy-done.75
  8.3 2.9 attention_first.1
  11.8 2.7 attention_next.1
  17.3 3.0 collective-permute-start.1
  20.4 1.5 collective-permute-start.6
  21.9 11.2 %collective-permute-done.1.theirs_ref = f32[128,1024]{1,0:T(8,128)S(1)} collective-permute-done((f32[128,1024]{1,0:T(8,128)S(1)}, f32[128,1024]{1,0:T(8,128)S(1)}, u32[]{:S(2)}, u32[]{:S(2)}) %collective-permute-start.1) | collective-permute-done | bytes 524320 | tf_op jit(solution)/shard_map/ppermute | solution.py:46
  34.4 9.3 %collective-permute-done.6.theirs_ref = f32[128,1024]{1,0:T(8,128)S(1)} collective-permute-done((f32[128,1024]{1,0:T(8,128)S(1)}, f32[128,1024]{1,0:T(8,128)S(1)}, u32[]{:S(2)}, u32[]{:S(2)}) %collective-permute-start.6) | collective-permute-done | bytes 524320 | tf_op jit(solution)/shard_map/ppermute | solution.py:46
  45.0 1.8 copy-done.153
  47.1 1.8 mlp.2
  49.1 1.8 mlp.3
  51.6 1.8 collective-permute-start.4
  53.5 1.5 collective-permute-start.9
  54.9 11.5 %collective-permute-done.4.theirs_ref = f32[128,1024]{1,0:T(8,128)S(1)} collective-permute-done((f32[128,1024]{1,0:T(8,128)S(1)}, f32[128,1024]{1,0:T(8,128)S(1)}, u32[]{:S(2)}, u32[]{:S(2)}) %collective-permute-start.4) | collective-permute-done | bytes 524320 | tf_op jit(solution)/shard_map/ppermute | solution.py:46
  68.3 8.4 %collective-permute-done.9.theirs_ref = f32[128,1024]{1,0:T(8,128)S(1)} collective-permute-done((f32[128,1024]{1,0:T(8,128)S(1)}, f32[128,1024]{1,0:T(8,128)S(1)}, u32[]{:S(2)}, u32[]{:S(2)}) %collective-permute-start.9) | collective-permute-done | bytes 524320 | tf_op jit(solution)/shard_map/ppermute | solution.py:46
  77.4 2.9 mlp_back.2
  80.8 1.6 down_send.1
  82.4 2.7 mlp_back.3
  86.8 1.8 collective-permute-start.25
  88.6 1.1 constant_dynamic-slice_fusion.1.master_ref.refs_2_
  89.7 1.9 constant_dynamic-slice_fusion.master_ref.refs_3_
  91.6 1.5 collective-permute-start.22
  97.5 1.2 add.177.mine_ref
  98.7 1.6 collective-permute-start.13
  100.3 1.3 add.178.mine_ref
  105.3 8.3 %collective-permute-done.13.theirs_ref = f32[128,1024]{1,0:T(8,128)S(1)} collective-permute-done((f32[128,1024]{1,0:T(8,128)S(1)}, f32[128,1024]{1,0:T(8,128)S(1)}, u32[]{:S(2)}, u32[]{:S(2)}) %collective-permute-start.13) | collective-permute-done | bytes 524320 | tf_op jit(solution)/shard_map/ppermute | solution.py:46
  115.5 7.9 %collective-permute-done.16.theirs_ref = f32[128,1024]{1,0:T(8,128)S(1)} collective-permute-done((f32[128,1024]{1,0:T(8,128)S(1)}, f32[128,1024]{1,0:T(8,128)S(1)}, u32[]{:S(2)}, u32[]{:S(2)}) %collective-permute-start.16) | collective-permute-done | bytes 524320 | tf_op jit(solution)/shard_map/ppermute | solution.py:46
  127.3 40.4 %collective-permute-done.26.refs_6_ = f32[2,256,128]{2,1,0:T(8,128)S(1)} collective-permute-done((f32[2,256,128]{2,1,0:T(8,128)S(1)}, f32[2,256,128]{2,1,0:T(8,128)S(1)}, u32[]{:S(2)}, u32[]{:S(2)}) %collective-permute-start.26) | collective-permute-done | bytes 262176 | tf_op jit(solution)/shard_map/ppermute | solution.py:46
  167.6 1.5 collective-permute-start.32
  170.0 4.5 %attention_back.1 = (bf16[512,1024]{1,0:T(8,128)(2,1)S(1)}, bf16[512,768]{1,0:T(8,128)(2,1)S(1)}) custom-call(s32[1]{0:T(128)S(6)} %copy.39.live_ref, bf16[256,1024]{1,0:T(8,128)(2,1)S(1)} %copy-done.35, f32[512,128]{1,0:T(8,128)S(1)} %copy-done.27, f32[512,128]{1,0:T(8,128)S(1)} %copy-done.29, f32[128,1024]{1,0:T(8,128)S(1)} %get-tuple-element.137.refs_0_, ...), custom_call_target="tpu_custom_call" | custom-call | flops 939524096 | bytes 6029316 | tf_op jit(solution)/shard_map/attention_back/pallas_call | solution.py:168
  176.5 2.1 input_back.1
  179.4 1.6 collective-permute-start.37
  182.6 7.5 %collective-permute-done.34.refs_1_ = f32[4,256,128]{2,1,0:T(8,128)S(1)} collective-permute-done((f32[4,256,128]{2,1,0:T(8,128)S(1)}, f32[4,256,128]{2,1,0:T(8,128)S(1)}, u32[]{:S(2)}, u32[]{:S(2)}) %collective-permute-start.34) | collective-permute-done | bytes 524320 | tf_op jit(solution)/shard_map/ppermute | solution.py:46
  190.6 1.6 collective-permute-start.35
  192.3 4.5 %collective-permute-done.40.refs_5_ = f32[4,1,128,256]{3,2,1,0:T(8,128)S(1)} collective-permute-done((f32[4,1,128,256]{3,2,1,0:T(8,128)S(1)}, f32[4,1,128,256]{3,2,1,0:T(8,128)S(1)}, u32[]{:S(2)}, u32[]{:S(2)}) %collective-permute-start.40) | collective-permute-done | bytes 524320 | tf_op jit(solution)/shard_map/ppermute | solution.py:46
  197.3 22.0 %collective-permute-done.35.refs_2_ = f32[2,256,128]{2,1,0:T(8,128)S(1)} collective-permute-done((f32[2,256,128]{2,1,0:T(8,128)S(1)}, f32[2,256,128]{2,1,0:T(8,128)S(1)}, u32[]{:S(2)}, u32[]{:S(2)}) %collective-permute-start.35) | collective-permute-done | bytes 262176 | tf_op jit(solution)/shard_map/ppermute | solution.py:46
  219.3 2.6 collective-permute-start.27
  223.1 1.2 add.179.mine_ref
  224.3 1.5 collective-permute-start.20
  226.5 12.4 %collective-permute-done.29.refs_2_ = f32[2,128,768]{2,1,0:T(8,128)S(1)} collective-permute-done((f32[2,128,768]{2,1,0:T(8,128)S(1)}, f32[2,128,768]{2,1,0:T(8,128)S(1)}, u32[]{:S(2)}, u32[]{:S(2)}) %collective-permute-start.29) | collective-permute-done | bytes 786464 | tf_op jit(solution)/shard_map/ppermute | solution.py:46
  239.7 18.2 %collective-permute-done.38.refs_2_ = f32[2,2,128,256]{3,2,1,0:T(8,128)S(1)} collective-permute-done((f32[2,2,128,256]{3,2,1,0:T(8,128)S(1)}, f32[2,2,128,256]{3,2,1,0:T(8,128)S(1)}, u32[]{:S(2)}, u32[]{:S(2)}) %collective-permute-start.38) | collective-permute-done | bytes 524320 | tf_op jit(solution)/shard_map/ppermute | solution.py:46
  258.9 2.7 collective-permute-start.33
  262.5 25.9 %collective-permute-done.33.refs_7_ = f32[1,128,256]{2,1,0:T(8,128)S(1)} collective-permute-done((f32[1,128,256]{2,1,0:T(8,128)S(1)}, f32[1,128,256]{2,1,0:T(8,128)S(1)}, u32[]{:S(2)}, u32[]{:S(2)}) %collective-permute-start.33) | collective-permute-done | bytes 131104 | tf_op jit(solution)/shard_map/ppermute | solution.py:46
  288.5 3.0 collective-permute-start.42
  293.0 1.6 constant_dynamic-slice_fusion.2.master_ref.refs_1_
  296.1 1.4 copy-done.4
  297.5 1.1 copy-done.56
  305.7 1.4 moments_down.1
  309.2 1.4 moments_up.1
  310.6 2.0 moments_out.1
  313.5 2.4 moments_qkv.1
  315.8 1.5 collective-permute-start.44
  318.0 2.4 input_norm.1
  320.8 1.9 collective-permute-start.48
  322.7 1.6 collective-permute-start.46
  326.3 1.4 collective-permute-start.49
  327.7 2.7 place_output.1
  330.9 1.3 masters.1
  332.2 1.2 collective-permute-start.52
  333.5 2.4 collective-permute-done.52
  335.9 1.4 collective-permute-start.53
  337.8 2.6 collective-permute-done.53
  341.0 2.3 place_input.1
  (430 shorter events, 56.0 us)
Async XLA Ops:
  11.3 6.0 %collective-permute-start = (f32[128,1024]{1,0:T(8,128)S(1)}, f32[128,1024]{1,0:T(8,128)S(1)}, u32[]{:S(2)}, u32[]{:S(2)}) collective-permute-start(f32[128,1024]{1,0:T(8,128)S(1)} %get-tuple-element.113), channel_id=1, source_target_pairs={{0,1},{1,0},{2,3},{3,2},{4,5},{5,4},{6,7},{7,6},{8,9},{9,8},{10,11... | collective-permute-start | bytes 1572872 | tf_op jit(solution)/shard_map/ppermute | solution.py:46
  17.2 3.1 collective-permute-start.5
  17.3 15.7 %collective-permute-start.1 = (f32[128,1024]{1,0:T(8,128)S(1)}, f32[128,1024]{1,0:T(8,128)S(1)}, u32[]{:S(2)}, u32[]{:S(2)}) collective-permute-start(f32[128,1024]{1,0:T(8,128)S(1)} %add.173.mine_ref), channel_id=1, source_target_pairs={{0,2},{1,3},{2,0},{3,1},{4,6},{5,7},{6,4},{7,5},{8,10},{9,11},{10,... | collective-permute-start | bytes 1572872 | tf_op jit(solution)/shard_map/ppermute | solution.py:46
  20.4 23.3 %collective-permute-start.6 = (f32[128,1024]{1,0:T(8,128)S(1)}, f32[128,1024]{1,0:T(8,128)S(1)}, u32[]{:S(2)}, u32[]{:S(2)}) collective-permute-start(f32[128,1024]{1,0:T(8,128)S(1)} %add.175.mine_ref), channel_id=1, source_target_pairs={{0,2},{1,3},{2,0},{3,1},{4,6},{5,7},{6,4},{7,5},{8,10},{9,11},{10,... | collective-permute-start | bytes 1572872 | tf_op jit(solution)/shard_map/ppermute | solution.py:46
  34.4 12.7 %collective-permute-start.2 = (f32[128,1024]{1,0:T(8,128)S(1)}, f32[128,1024]{1,0:T(8,128)S(1)}, u32[]{:S(2)}, u32[]{:S(2)}) collective-permute-start(f32[128,1024]{1,0:T(8,128)S(1)} %get-tuple-element.115.own_ref), channel_id=1, source_target_pairs={{0,1},{1,0},{2,3},{3,2},{4,5},{5,4},{6,7},{7,6},{8,9},{9,8},{10,11... | collective-permute-start | bytes 1572872 | tf_op jit(solution)/shard_map/ppermute | solution.py:46
  44.2 4.8 %collective-permute-start.7 = (f32[128,1024]{1,0:T(8,128)S(1)}, f32[128,1024]{1,0:T(8,128)S(1)}, u32[]{:S(2)}, u32[]{:S(2)}) collective-permute-start(f32[128,1024]{1,0:T(8,128)S(1)} %get-tuple-element.128.own_ref), channel_id=1, source_target_pairs={{0,1},{1,0},{2,3},{3,2},{4,5},{5,4},{6,7},{7,6},{8,9},{9,8},{10,11... | collective-permute-start | bytes 1572872 | tf_op jit(solution)/shard_map/ppermute | solution.py:46
  49.0 2.5 collective-permute-start.3
  50.9 2.4 collective-permute-start.8
  51.6 14.9 %collective-permute-start.4 = (f32[128,1024]{1,0:T(8,128)S(1)}, f32[128,1024]{1,0:T(8,128)S(1)}, u32[]{:S(2)}, u32[]{:S(2)}) collective-permute-start(f32[128,1024]{1,0:T(8,128)S(1)} %add.174.mine_ref), channel_id=1, source_target_pairs={{0,2},{1,3},{2,0},{3,1},{4,6},{5,7},{6,4},{7,5},{8,10},{9,11},{10,... | collective-permute-start | bytes 1572872 | tf_op jit(solution)/shard_map/ppermute | solution.py:46
  53.5 23.3 %collective-permute-start.9 = (f32[128,1024]{1,0:T(8,128)S(1)}, f32[128,1024]{1,0:T(8,128)S(1)}, u32[]{:S(2)}, u32[]{:S(2)}) collective-permute-start(f32[128,1024]{1,0:T(8,128)S(1)} %add.176.mine_ref), channel_id=1, source_target_pairs={{0,2},{1,3},{2,0},{3,1},{4,6},{5,7},{6,4},{7,5},{8,10},{9,11},{10,... | collective-permute-start | bytes 1572872 | tf_op jit(solution)/shard_map/ppermute | solution.py:46
  68.3 9.0 %collective-permute-start.11 = (f32[128,1024]{1,0:T(8,128)S(1)}, f32[128,1024]{1,0:T(8,128)S(1)}, u32[]{:S(2)}, u32[]{:S(2)}) collective-permute-start(f32[128,1024]{1,0:T(8,128)S(1)} %get-tuple-element.133.own_ref.refs_2_), channel_id=1, source_target_pairs={{0,1},{1,0},{2,3},{3,2},{4,5},{5,4},{6,7},{7,6},{8,9},{9,8},{10,11... | collective-permute-start | bytes 1572872 | tf_op jit(solution)/shard_map/ppermute | solution.py:46
  77.3 3.5 %collective-permute-start.14 = (f32[128,1024]{1,0:T(8,128)S(1)}, f32[128,1024]{1,0:T(8,128)S(1)}, u32[]{:S(2)}, u32[]{:S(2)}) collective-permute-start(f32[128,1024]{1,0:T(8,128)S(1)} %get-tuple-element.144.refs_4_.own_ref), channel_id=1, source_target_pairs={{0,1},{1,0},{2,3},{3,2},{4,5},{5,4},{6,7},{7,6},{8,9},{9,8},{10,11... | collective-permute-start | bytes 1572872 | tf_op jit(solution)/shard_map/ppermute | solution.py:46
  80.2 17.3 %collective-permute-start.12 = (f32[128,1024]{1,0:T(8,128)}, f32[128,1024]{1,0:T(8,128)}, u32[]{:S(2)}, u32[]{:S(2)}) collective-permute-start(f32[128,1024]{1,0:T(8,128)} %get-tuple-element.136), channel_id=1, source_target_pairs={{0,1},{1,0},{2,3},{3,2},{4,5},{5,4},{6,7},{7,6},{8,9},{9,8},{10,11... | collective-permute-start | bytes 1572872 | tf_op jit(solution)/shard_map/ppermute | solution.py:46
  86.7 13.5 %collective-permute-start.15 = (f32[128,1024]{1,0:T(8,128)}, f32[128,1024]{1,0:T(8,128)}, u32[]{:S(2)}, u32[]{:S(2)}) collective-permute-start(f32[128,1024]{1,0:T(8,128)} %get-tuple-element.147), channel_id=1, source_target_pairs={{0,1},{1,0},{2,3},{3,2},{4,5},{5,4},{6,7},{7,6},{8,9},{9,8},{10,11... | collective-permute-start | bytes 1572872 | tf_op jit(solution)/shard_map/ppermute | solution.py:46
  86.8 18.2 %collective-permute-start.25 = (f32[4,256,128]{2,1,0:T(8,128)}, f32[4,256,128]{2,1,0:T(8,128)S(1)}, u32[]{:S(2)}, u32[]{:S(2)}) collective-permute-start(f32[4,256,128]{2,1,0:T(8,128)} %get-tuple-element.143), channel_id=1, source_target_pairs={{0,8},{4,12},{8,0},{12,4},{16,24},{20,28},{24,16},{28,20},{1,9},{5... | collective-permute-start | bytes 1572872 | tf_op jit(solution)/shard_map/ppermute | solution.py:46
  91.6 90.4 %collective-permute-start.22 = (f32[4,768,128]{2,1,0:T(8,128)}, f32[4,768,128]{2,1,0:T(8,128)S(1)}, u32[]{:S(2)}, u32[]{:S(2)}) collective-permute-start(f32[4,768,128]{2,1,0:T(8,128)} %copy-done.151), channel_id=1, source_target_pairs={{0,4},{4,0},{8,12},{12,8},{16,20},{20,16},{24,28},{28,24},{1,5},{5... | collective-permute-start | bytes 4718600 | tf_op jit(solution)/shard_map/ppermute | solution.py:46
  97.0 28.7 %collective-permute-start.31 = (f32[4,128,256]{2,1,0:T(8,128)S(1)}, f32[4,128,256]{2,1,0:T(8,128)S(1)}, u32[]{:S(2)}, u32[]{:S(2)}) collective-permute-start(f32[4,128,256]{2,1,0:T(8,128)S(1)} %get-tuple-element.171), channel_id=1, source_target_pairs={{0,8},{4,12},{8,0},{12,4},{16,24},{20,28},{24,16},{28,20},{1,9},{5... | collective-permute-start | bytes 1572872 | tf_op jit(solution)/shard_map/ppermute | solution.py:46
  98.7 14.9 %collective-permute-start.13 = (f32[128,1024]{1,0:T(8,128)S(1)}, f32[128,1024]{1,0:T(8,128)S(1)}, u32[]{:S(2)}, u32[]{:S(2)}) collective-permute-start(f32[128,1024]{1,0:T(8,128)S(1)} %add.177.mine_ref), channel_id=1, source_target_pairs={{0,2},{1,3},{2,0},{3,1},{4,6},{5,7},{6,4},{7,5},{8,10},{9,11},{10,... | collective-permute-start | bytes 1572872 | tf_op jit(solution)/shard_map/ppermute | solution.py:46
  101.6 21.9 %collective-permute-start.16 = (f32[128,1024]{1,0:T(8,128)S(1)}, f32[128,1024]{1,0:T(8,128)S(1)}, u32[]{:S(2)}, u32[]{:S(2)}) collective-permute-start(f32[128,1024]{1,0:T(8,128)S(1)} %add.178.mine_ref), channel_id=1, source_target_pairs={{0,2},{1,3},{2,0},{3,1},{4,6},{5,7},{6,4},{7,5},{8,10},{9,11},{10,... | collective-permute-start | bytes 1572872 | tf_op jit(solution)/shard_map/ppermute | solution.py:46
  104.9 64.2 %copy-start.63 = (f32[4,256,128]{2,1,0:T(8,128)}, f32[4,256,128]{2,1,0:T(8,128)S(1)}, u32[]{:S(2)}) copy-start(f32[4,256,128]{2,1,0:T(8,128)S(1)} %get-tuple-element.162.refs_4_) | copy-start | bytes 1572868
  104.9 121.5 %copy-start.3 = (f32[4,768,128]{2,1,0:T(8,128)}, f32[4,768,128]{2,1,0:T(8,128)S(1)}, u32[]{:S(2)}) copy-start(f32[4,768,128]{2,1,0:T(8,128)S(1)} %get-tuple-element.161.refs_0_) | copy-start | bytes 4718596
  104.9 64.2 %copy-start.59 = (f32[4,256,128]{2,1,0:T(8,128)}, f32[4,256,128]{2,1,0:T(8,128)S(1)}, u32[]{:S(2)}) copy-start(f32[4,256,128]{2,1,0:T(8,128)S(1)} %collective-permute-done.25.refs_5_) | copy-start | bytes 1572868
  104.9 85.7 %collective-permute-start.28 = (f32[4,128,768]{2,1,0:T(8,128)S(1)}, f32[4,128,768]{2,1,0:T(8,128)S(1)}, u32[]{:S(2)}, u32[]{:S(2)}) collective-permute-start(f32[4,128,768]{2,1,0:T(8,128)S(1)} %get-tuple-element.169), channel_id=1, source_target_pairs={{0,4},{4,0},{8,12},{12,8},{16,20},{20,16},{24,28},{28,24},{1,5},{5... | collective-permute-start | bytes 4718600 | tf_op jit(solution)/shard_map/ppermute | solution.py:46
  113.6 54.0 %collective-permute-start.26 = (f32[2,256,128]{2,1,0:T(8,128)S(1)}, f32[2,256,128]{2,1,0:T(8,128)S(1)}, u32[]{:S(2)}, u32[]{:S(2)}) collective-permute-start(f32[2,256,128]{2,1,0:T(8,128)S(1)} %slice_add_fusion.12), channel_id=1, source_target_pairs={{0,4},{4,0},{8,12},{12,8},{16,20},{20,16},{24,28},{28,24},{1,5},{5... | collective-permute-start | bytes 786440 | tf_op jit(solution)/shard_map/ppermute | solution.py:46
  123.5 46.4 %collective-permute-start.17 = (f32[128,1024]{1,0:T(8,128)S(1)}, f32[128,1024]{1,0:T(8,128)S(1)}, u32[]{:S(2)}, u32[]{:S(2)}) collective-permute-start(f32[128,1024]{1,0:T(8,128)S(1)} %get-tuple-element.137.refs_0_), channel_id=1, source_target_pairs={{0,1},{1,0},{2,3},{3,2},{4,5},{5,4},{6,7},{7,6},{8,9},{9,8},{10,11... | collective-permute-start | bytes 1572872 | tf_op jit(solution)/shard_map/ppermute | solution.py:46
  125.7 50.0 %copy-start.61 = (f32[4,128,256]{2,1,0:T(8,128)}, f32[4,128,256]{2,1,0:T(8,128)S(1)}, u32[]{:S(2)}) copy-start(f32[4,128,256]{2,1,0:T(8,128)S(1)} %collective-permute-done.31.refs_5_) | copy-start | bytes 1572868
  125.9 44.0 %collective-permute-start.18 = (f32[128,1024]{1,0:T(8,128)S(1)}, f32[128,1024]{1,0:T(8,128)S(1)}, u32[]{:S(2)}, u32[]{:S(2)}) collective-permute-start(f32[128,1024]{1,0:T(8,128)S(1)} %get-tuple-element.148.refs_1_), channel_id=1, source_target_pairs={{0,1},{1,0},{2,3},{3,2},{4,5},{5,4},{6,7},{7,6},{8,9},{9,8},{10,11... | collective-permute-start | bytes 1572872 | tf_op jit(solution)/shard_map/ppermute | solution.py:46
  127.2 112.4 %copy-start.7 = (f32[4,128,768]{2,1,0:T(8,128)}, f32[4,128,768]{2,1,0:T(8,128)S(1)}, u32[]{:S(2)}) copy-start(f32[4,128,768]{2,1,0:T(8,128)S(1)} %get-tuple-element.168.refs_0_) | copy-start | bytes 4718596
  167.6 8.1 %collective-permute-start.32 = (f32[2,128,256]{2,1,0:T(8,128)S(1)}, f32[2,128,256]{2,1,0:T(8,128)S(1)}, u32[]{:S(2)}, u32[]{:S(2)}) collective-permute-start(f32[2,128,256]{2,1,0:T(8,128)S(1)} %slice_add_fusion.11), channel_id=1, source_target_pairs={{0,4},{4,0},{8,12},{12,8},{16,20},{20,16},{24,28},{28,24},{1,5},{5... | collective-permute-start | bytes 786440 | tf_op jit(solution)/shard_map/ppermute | solution.py:46
  175.2 14.9 %collective-permute-start.34 = (f32[4,256,128]{2,1,0:T(8,128)S(1)}, f32[4,256,128]{2,1,0:T(8,128)S(1)}, u32[]{:S(2)}, u32[]{:S(2)}) collective-permute-start(f32[4,256,128]{2,1,0:T(8,128)S(1)} %out_send.1), channel_id=1, source_target_pairs={{0,4},{4,0},{8,12},{12,8},{16,20},{20,16},{24,28},{28,24},{1,5},{5... | collective-permute-start | bytes 1572872 | tf_op jit(solution)/shard_map/ppermute | solution.py:46
  178.6 44.0 %collective-permute-start.19 = (f32[256,1024]{1,0:T(8,128)S(1)}, f32[256,1024]{1,0:T(8,128)S(1)}, u32[]{:S(2)}, u32[]{:S(2)}) collective-permute-start(f32[256,1024]{1,0:T(8,128)S(1)} %get-tuple-element.157), channel_id=1, source_target_pairs={{0,1},{1,0},{2,3},{3,2},{4,5},{5,4},{6,7},{7,6},{8,9},{9,8},{10,11... | collective-permute-start | bytes 3145736 | tf_op jit(solution)/shard_map/ppermute | solution.py:46
  179.4 44.9 %collective-permute-start.37 = (f32[4,2,128,256]{3,2,1,0:T(8,128)S(1)}, f32[4,2,128,256]{3,2,1,0:T(8,128)S(1)}, u32[]{:S(2)}, u32[]{:S(2)}) collective-permute-start(f32[4,2,128,256]{3,2,1,0:T(8,128)S(1)} %get-tuple-element.180), channel_id=1, source_target_pairs={{0,4},{4,0},{8,12},{12,8},{16,20},{20,16},{24,28},{28,24},{1,5},{5... | collective-permute-start | bytes 3145736 | tf_op jit(solution)/shard_map/ppermute | solution.py:46
  182.0 76.1 %copy-start.21 = (f32[4,2,128,256]{3,2,1,0:T(8,128)}, f32[4,2,128,256]{3,2,1,0:T(8,128)S(1)}, u32[]{:S(2)}) copy-start(f32[4,2,128,256]{3,2,1,0:T(8,128)S(1)} %get-tuple-element.179.refs_0_) | copy-start | bytes 3145732
  182.0 79.8 %copy-start.69 = (f32[4,1,128,256]{3,2,1,0:T(8,128)}, f32[4,1,128,256]{3,2,1,0:T(8,128)S(1)}, u32[]{:S(2)}) copy-start(f32[4,1,128,256]{3,2,1,0:T(8,128)S(1)} %get-tuple-element.181.refs_4_) | copy-start | bytes 1572868
  182.0 14.8 %collective-permute-start.40 = (f32[4,1,128,256]{3,2,1,0:T(8,128)S(1)}, f32[4,1,128,256]{3,2,1,0:T(8,128)S(1)}, u32[]{:S(2)}, u32[]{:S(2)}) collective-permute-start(f32[4,1,128,256]{3,2,1,0:T(8,128)S(1)} %get-tuple-element.182), channel_id=1, source_target_pairs={{0,8},{4,12},{8,0},{12,4},{16,24},{20,28},{24,16},{28,20},{1,9},{5... | collective-permute-start | bytes 1572872 | tf_op jit(solution)/shard_map/ppermute | solution.py:46
  190.1 35.8 %collective-permute-start.23 = (f32[2,768,128]{2,1,0:T(8,128)S(1)}, f32[2,768,128]{2,1,0:T(8,128)S(1)}, u32[]{:S(2)}, u32[]{:S(2)}) collective-permute-start(f32[2,768,128]{2,1,0:T(8,128)S(1)} %slice_add_fusion.1), channel_id=1, source_target_pairs={{0,8},{4,12},{8,0},{12,4},{16,24},{20,28},{24,16},{28,20},{1,9},{5... | collective-permute-start | bytes 2359304 | tf_op jit(solution)/shard_map/ppermute | solution.py:46
  190.6 28.7 %collective-permute-start.35 = (f32[2,256,128]{2,1,0:T(8,128)S(1)}, f32[2,256,128]{2,1,0:T(8,128)S(1)}, u32[]{:S(2)}, u32[]{:S(2)}) collective-permute-start(f32[2,256,128]{2,1,0:T(8,128)S(1)} %slice_add_fusion.10), channel_id=1, source_target_pairs={{0,8},{4,12},{8,0},{12,4},{16,24},{20,28},{24,16},{28,20},{1,9},{5... | collective-permute-start | bytes 786440 | tf_op jit(solution)/shard_map/ppermute | solution.py:46
  196.8 65.0 %copy-start.71 = (f32[4,1,128,256]{3,2,1,0:T(8,128)}, f32[4,1,128,256]{3,2,1,0:T(8,128)S(1)}, u32[]{:S(2)}) copy-start(f32[4,1,128,256]{3,2,1,0:T(8,128)S(1)} %collective-permute-done.40.refs_5_) | copy-start | bytes 1572868
  196.8 42.1 %collective-permute-start.29 = (f32[2,128,768]{2,1,0:T(8,128)S(1)}, f32[2,128,768]{2,1,0:T(8,128)S(1)}, u32[]{:S(2)}, u32[]{:S(2)}) collective-permute-start(f32[2,128,768]{2,1,0:T(8,128)S(1)} %slice_add_fusion), channel_id=1, source_target_pairs={{0,8},{4,12},{8,0},{12,4},{16,24},{20,28},{24,16},{28,20},{1,9},{5... | collective-permute-start | bytes 2359304 | tf_op jit(solution)/shard_map/ppermute | solution.py:46
  219.3 39.6 %collective-permute-start.27 = (f32[1,256,128]{2,1,0:T(8,128)S(1)}, f32[1,256,128]{2,1,0:T(8,128)S(1)}, u32[]{:S(2)}, u32[]{:S(2)}) collective-permute-start(f32[1,256,128]{2,1,0:T(8,128)S(1)} %slice_add_fusion.19), channel_id=1, source_target_pairs={{0,16},{4,20},{8,24},{12,28},{16,0},{20,4},{24,8},{28,12},{1,17},{... | collective-permute-start | bytes 393224 | tf_op jit(solution)/shard_map/ppermute | solution.py:46
  222.6 39.0 %collective-permute-start.41 = (f32[2,1,128,256]{3,2,1,0:T(8,128)S(1)}, f32[2,1,128,256]{3,2,1,0:T(8,128)S(1)}, u32[]{:S(2)}, u32[]{:S(2)}) collective-permute-start(f32[2,1,128,256]{3,2,1,0:T(8,128)S(1)} %slice_add_fusion.7), channel_id=1, source_target_pairs={{0,4},{4,0},{8,12},{12,8},{16,20},{20,16},{24,28},{28,24},{1,5},{5... | collective-permute-start | bytes 786440 | tf_op jit(solution)/shard_map/ppermute | solution.py:46
  224.3 93.7 %collective-permute-start.20 = (f32[256,1024]{1,0:T(8,128)}, f32[256,1024]{1,0:T(8,128)}, u32[]{:S(2)}, u32[]{:S(2)}) collective-permute-start(f32[256,1024]{1,0:T(8,128)} %add.179.mine_ref), channel_id=1, source_target_pairs={{0,2},{1,3},{2,0},{3,1},{4,6},{5,7},{6,4},{7,5},{8,10},{9,11},{10,... | collective-permute-start | bytes 3145736 | tf_op jit(solution)/shard_map/ppermute | solution.py:46
  225.9 32.0 %collective-permute-start.38 = (f32[2,2,128,256]{3,2,1,0:T(8,128)S(1)}, f32[2,2,128,256]{3,2,1,0:T(8,128)S(1)}, u32[]{:S(2)}, u32[]{:S(2)}) collective-permute-start(f32[2,2,128,256]{3,2,1,0:T(8,128)S(1)} %slice_add_fusion.2), channel_id=1, source_target_pairs={{0,8},{4,12},{8,0},{12,4},{16,24},{20,28},{24,16},{28,20},{1,9},{5... | collective-permute-start | bytes 1572872 | tf_op jit(solution)/shard_map/ppermute | solution.py:46
  226.5 64.9 %copy-start.109 = (f32[128,1024]{1,0:T(8,128)S(1)}, f32[128,1024]{1,0:T(8,128)}, u32[]{:S(2)}) copy-start(f32[128,1024]{1,0:T(8,128)} %copy-done.108) | copy-start | bytes 1572868
  239.0 49.5 %collective-permute-start.24 = (f32[1,768,128]{2,1,0:T(8,128)S(1)}, f32[1,768,128]{2,1,0:T(8,128)S(1)}, u32[]{:S(2)}, u32[]{:S(2)}) collective-permute-start(f32[1,768,128]{2,1,0:T(8,128)S(1)} %slice_add_fusion.5), channel_id=1, source_target_pairs={{0,16},{4,20},{8,24},{12,28},{16,0},{20,4},{24,8},{28,12},{1,17},{... | collective-permute-start | bytes 1179656 | tf_op jit(solution)/shard_map/ppermute | solution.py:46
  239.7 56.4 %copy-start.9 = (f32[1024,128]{1,0:T(8,128)S(1)}, f32[1024,128]{1,0:T(8,128)}, u32[]{:S(2)}) copy-start(f32[1024,128]{1,0:T(8,128)} %constant_dynamic-slice_fusion.master_ref.refs_3_) | copy-start | bytes 1572868
  257.9 34.4 %collective-permute-start.30 = (f32[1,128,768]{2,1,0:T(8,128)S(1)}, f32[1,128,768]{2,1,0:T(8,128)S(1)}, u32[]{:S(2)}, u32[]{:S(2)}) collective-permute-start(f32[1,128,768]{2,1,0:T(8,128)S(1)} %slice_add_fusion.3), channel_id=1, source_target_pairs={{0,16},{4,20},{8,24},{12,28},{16,0},{20,4},{24,8},{28,12},{1,17},{... | collective-permute-start | bytes 1179656 | tf_op jit(solution)/shard_map/ppermute | solution.py:46
  258.9 29.6 %collective-permute-start.33 = (f32[1,128,256]{2,1,0:T(8,128)S(1)}, f32[1,128,256]{2,1,0:T(8,128)S(1)}, u32[]{:S(2)}, u32[]{:S(2)}) collective-permute-start(f32[1,128,256]{2,1,0:T(8,128)S(1)} %slice_add_fusion.17), channel_id=1, source_target_pairs={{0,16},{4,20},{8,24},{12,28},{16,0},{20,4},{24,8},{28,12},{1,17},{... | collective-permute-start | bytes 393224 | tf_op jit(solution)/shard_map/ppermute | solution.py:46
  261.6 51.7 %collective-permute-start.39 = (f32[1,2,128,256]{3,2,1,0:T(8,128)}, f32[1,2,128,256]{3,2,1,0:T(8,128)}, u32[]{:S(2)}, u32[]{:S(2)}) collective-permute-start(f32[1,2,128,256]{3,2,1,0:T(8,128)} %slice_add_fusion.8), channel_id=1, source_target_pairs={{0,16},{4,20},{8,24},{12,28},{16,0},{20,4},{24,8},{28,12},{1,17},{... | collective-permute-start | bytes 786440 | tf_op jit(solution)/shard_map/ppermute | solution.py:46
  288.4 22.1 %collective-permute-start.36 = (f32[1,256,128]{2,1,0:T(8,128)}, f32[1,256,128]{2,1,0:T(8,128)}, u32[]{:S(2)}, u32[]{:S(2)}) collective-permute-start(f32[1,256,128]{2,1,0:T(8,128)} %slice_add_fusion.15), channel_id=1, source_target_pairs={{0,16},{4,20},{8,24},{12,28},{16,0},{20,4},{24,8},{28,12},{1,17},{... | collective-permute-start | bytes 393224 | tf_op jit(solution)/shard_map/ppermute | solution.py:46
  288.5 24.8 %collective-permute-start.42 = (f32[1,1,128,256]{3,2,1,0:T(8,128)}, f32[1,1,128,256]{3,2,1,0:T(8,128)}, u32[]{:S(2)}, u32[]{:S(2)}) collective-permute-start(f32[1,1,128,256]{3,2,1,0:T(8,128)} %slice_add_fusion.13), channel_id=1, source_target_pairs={{0,16},{4,20},{8,24},{12,28},{16,0},{20,4},{24,8},{28,12},{1,17},{... | collective-permute-start | bytes 393224 | tf_op jit(solution)/shard_map/ppermute | solution.py:46
  293.0 34.6 %collective-permute-start.10 = (f32[256,1024]{1,0:T(8,128)}, f32[256,1024]{1,0:T(8,128)}, u32[]{:S(2)}, u32[]{:S(2)}) collective-permute-start(f32[256,1024]{1,0:T(8,128)} %constant_dynamic-update-slice_fusion.mine_ref), channel_id=1, source_target_pairs={{0,1},{1,0},{2,3},{3,2},{4,5},{5,4},{6,7},{7,6},{8,9},{9,8},{10,11... | collective-permute-start | bytes 3145736 | tf_op jit(solution)/shard_map/ppermute | solution.py:46
  315.8 4.9 %collective-permute-start.44 = (f32[8,128]{1,0:T(8,128)S(1)}, f32[8,128]{1,0:T(8,128)S(1)}, u32[]{:S(2)}, u32[]{:S(2)}) collective-permute-start(f32[8,128]{1,0:T(8,128)S(1)} %get-tuple-element.183), channel_id=1, source_target_pairs={{0,2},{1,3},{2,0},{3,1},{4,6},{5,7},{6,4},{7,5},{8,10},{9,11},{10,... | collective-permute-start | bytes 12296 | tf_op jit(solution)/shard_map/ppermute | solution.py:46
  317.3 3.4 collective-permute-start.45
  317.7 3.0 collective-permute-start.43
  320.4 3.9 %collective-permute-start.50 = (f32[8,1024]{1,0:T(8,128)S(1)}, f32[8,1024]{1,0:T(8,128)S(1)}, u32[]{:S(2)}, u32[]{:S(2)}) collective-permute-start(f32[8,1024]{1,0:T(8,128)S(1)} %pad_maximum_fusion), channel_id=1, source_target_pairs={{0,1},{1,0},{2,3},{3,2},{4,5},{5,4},{6,7},{7,6},{8,9},{9,8},{10,11... | collective-permute-start | bytes 98312 | tf_op jit(solution)/shard_map/ppermute | solution.py:46
  320.7 3.7 %collective-permute-start.47 = (f32[8,128]{1,0:T(8,128)S(1)}, f32[8,128]{1,0:T(8,128)S(1)}, u32[]{:S(2)}, u32[]{:S(2)}) collective-permute-start(f32[8,128]{1,0:T(8,128)S(1)} %add_add_fusion.1), channel_id=1, source_target_pairs={{0,8},{4,12},{8,0},{12,4},{16,24},{20,28},{24,16},{28,20},{1,9},{5... | collective-permute-start | bytes 12296 | tf_op jit(solution)/shard_map/ppermute | solution.py:46
  320.8 4.6 %collective-permute-start.48 = (f32[8,128]{1,0:T(8,128)S(1)}, f32[8,128]{1,0:T(8,128)S(1)}, u32[]{:S(2)}, u32[]{:S(2)}) collective-permute-start(f32[8,128]{1,0:T(8,128)S(1)} %add_add_fusion.1), channel_id=1, source_target_pairs={{0,12},{4,8},{8,4},{12,0},{16,28},{20,24},{24,20},{28,16},{1,13},{... | collective-permute-start | bytes 12296 | tf_op jit(solution)/shard_map/ppermute | solution.py:46
  322.7 3.6 %collective-permute-start.46 = (f32[8,128]{1,0:T(8,128)S(1)}, f32[8,128]{1,0:T(8,128)S(1)}, u32[]{:S(2)}, u32[]{:S(2)}) collective-permute-start(f32[8,128]{1,0:T(8,128)S(1)} %add_add_fusion.1), channel_id=1, source_target_pairs={{0,4},{4,0},{8,12},{12,8},{16,20},{20,16},{24,28},{28,24},{1,5},{5... | collective-permute-start | bytes 12296 | tf_op jit(solution)/shard_map/ppermute | solution.py:46
  324.3 16.7 %collective-permute-start.21 = (f32[256,1024]{1,0:T(8,128)S(1)}, f32[256,1024]{1,0:T(8,128)}, u32[]{:S(2)}, u32[]{:S(2)}) collective-permute-start(f32[256,1024]{1,0:T(8,128)S(1)} %get-tuple-element.160.mine_ref), channel_id=1, source_target_pairs={{0,1},{1,0},{2,3},{3,2},{4,5},{5,4},{6,7},{7,6},{8,9},{9,8},{10,11... | collective-permute-start | bytes 3145736 | tf_op jit(solution)/shard_map/ppermute | solution.py:46
  324.4 7.8 %collective-permute-start.51 = (f32[4,8,128]{2,1,0:T(8,128)S(1)}, f32[4,8,128]{2,1,0:T(8,128)S(1)}, u32[]{:S(2)}, u32[]{:S(2)}) collective-permute-start(f32[4,8,128]{2,1,0:T(8,128)S(1)} %pad_maximum_fusion.1), channel_id=1, source_target_pairs={{0,4},{4,0},{8,12},{12,8},{16,20},{20,16},{24,28},{28,24},{1,5},{5... | collective-permute-start | bytes 49160 | tf_op jit(solution)/shard_map/ppermute | solution.py:46
  326.3 4.5 %collective-permute-start.49 = (f32[8,128]{1,0:T(8,128)S(1)}, f32[8,128]{1,0:T(8,128)S(1)}, u32[]{:S(2)}, u32[]{:S(2)}) collective-permute-start(f32[8,128]{1,0:T(8,128)S(1)} %add_add_fusion), channel_id=1, source_target_pairs={{0,16},{4,20},{8,24},{12,28},{16,0},{20,4},{24,8},{28,12},{1,17},{... | collective-permute-start | bytes 12296 | tf_op jit(solution)/shard_map/ppermute | solution.py:46
  332.2 3.7 %collective-permute-start.52 = (f32[2,8,128]{2,1,0:T(8,128)S(1)}, f32[2,8,128]{2,1,0:T(8,128)S(1)}, u32[]{:S(2)}, u32[]{:S(2)}) collective-permute-start(f32[2,8,128]{2,1,0:T(8,128)S(1)} %slice_add_fusion.21), channel_id=1, source_target_pairs={{0,8},{4,12},{8,0},{12,4},{16,24},{20,28},{24,16},{28,20},{1,9},{5... | collective-permute-start | bytes 24584 | tf_op jit(solution)/shard_map/ppermute | solution.py:46
  335.9 4.5 %collective-permute-start.53 = (f32[1,8,128]{2,1,0:T(8,128)S(1)}, f32[1,8,128]{2,1,0:T(8,128)S(1)}, u32[]{:S(2)}, u32[]{:S(2)}) collective-permute-start(f32[1,8,128]{2,1,0:T(8,128)S(1)} %slice_add_fusion.22), channel_id=1, source_target_pairs={{0,16},{4,20},{8,24},{12,28},{16,0},{20,4},{24,8},{28,12},{1,17},{... | collective-permute-start | bytes 12296 | tf_op jit(solution)/shard_map/ppermute | solution.py:46
  (146 other events, 1300.7 us)

commit v2 on v1

--- a/solution.py
+++ b/solution.py
@@ -27,7 +27,7 @@
 WIDE = jnp.float32
 VMEM = pl.BlockSpec(memory_space=pltpu.VMEM)
 SMEM = pl.BlockSpec(memory_space=pltpu.SMEM)
-ANY = pl.BlockSpec(memory_space=pl.ANY)
+HBM = pl.BlockSpec(memory_space=pltpu.HBM)
 
 
 def log2_of(count):
@@ -37,36 +37,9 @@
     return bits
 
 
-def after(values, *earlier):
-    return lax.optimization_barrier((values,) + earlier)[0]
-
-
 def swap(values, axis, distance):
     count = lax.axis_size(axis)
     return lax.ppermute(values, axis, [(i, i ^ distance) for i in range(count)])
-
-
-def sum_rows(send, keep):
-    mine, theirs = keep, swap(send, "tensor", 1)
-    for bit in range(1, log2_of(lax.axis_size("tensor"))):
-        mine = mine + theirs
-        theirs = swap(mine, "tensor", 1 << bit)
-    return mine, theirs
-
-
-def sum_all(values, axis, most=2):
-    bits = log2_of(lax.axis_size(axis))
-    start = 0
-    while start < bits:
-        taken = min(most, bits - start)
-        terms = [values] + [
-            swap(values, axis, distance << start) for distance in range(1, 1 << taken)
-        ]
-        while len(terms) > 1:
-            terms = [terms[i] + terms[i + 1] for i in range(0, len(terms), 2)]
-        values = terms[0]
-        start += taken
-    return values
 
 
 def chunk_order(count, bits):
@@ -74,18 +47,6 @@
     for bit in reversed(bits):
         order = order + [distance ^ (1 << bit) for distance in order]
     return order
-
-
-def scatter_terms(send, keep, bits):
-    terms = [keep, swap(send, "dp", 1 << bits[0])]
-    size = keep.shape[0]
-    for bit in bits[1:]:
-        size //= 2
-        outgoing = terms[0][size : 2 * size]
-        for term in terms[1:]:
-            outgoing = outgoing + term[size : 2 * size]
-        terms.append(swap(outgoing, "dp", 1 << bit))
-    return terms
 
 
 def normalize(values):
@@ -160,22 +121,187 @@
     return jax.ShapeDtypeStruct(shape, kind)
 
 
-def call(kernel, outs, args, specs=None, flops=0, scratch=(), megabytes=40, name=None):
-    moved = sum(a.size * a.dtype.itemsize for a in args) + sum(
-        int(np.prod(o.shape)) * jnp.dtype(o.dtype).itemsize for o in outs
-    )
-    blocks = any(spec.block_shape is not None for spec in specs or [])
-    return pl.pallas_call(
-        kernel,
-        grid=(1,) if blocks else (),
-        out_shape=tuple(outs),
-        in_specs=specs or [VMEM] * len(args),
-        out_specs=tuple([VMEM] * len(outs)),
-        scratch_shapes=list(scratch),
-        compiler_params=pltpu.CompilerParams(vmem_limit_bytes=megabytes * 1024 * 1024),
-        cost_estimate=pl.CostEstimate(flops=int(flops), bytes_accessed=int(moved), transcendentals=0),
-        name=name,
-    )(*args)
+def cut(rows, width, count=4):
+    return [shaped(rows // count, width)] * count
+
+
+def near(values):
+    return [swap(piece, "tensor", 1) for piece in values]
+
+
+class Take:
+    def __init__(self, array, shape=None, index=None):
+        self.array = array
+        self.shape = array.shape if shape is None else shape
+        self.index = index
+
+
+class Raw:
+    def __init__(self, array, spec):
+        self.array = array
+        self.spec = spec
+
+
+class Rows:
+    def __init__(self, refs):
+        self.refs = refs
+        self.step = refs[0].shape[0]
+        self.shape = (self.step * len(refs), refs[0].shape[1])
+
+    def spans(self, key):
+        first, last = 0, self.shape[0]
+        if key is not Ellipsis and key[0] != slice(None):
+            first, last = key[0].start, key[0].stop
+        for place, ref in enumerate(self.refs):
+            start, stop = max(first, place * self.step), min(last, (place + 1) * self.step)
+            if start < stop:
+                inside = slice(start - place * self.step, stop - place * self.step)
+                yield ref, inside, slice(start - first, stop - first)
+
+    def __getitem__(self, key):
+        pieces = [ref[inside, :] for ref, inside, _ in self.spans(key)]
+        return pieces[0] if len(pieces) == 1 else jnp.concatenate(pieces, axis=0)
+
+    def __setitem__(self, key, value):
+        for ref, inside, outside in self.spans(key):
+            ref[inside, :] = value[outside]
+
+
+class Line:
+    def __init__(self):
+        self.token = jnp.zeros((8, LANES), WIDE)
+
+    def call(self, kernel, outs, args, scratch=(), megabytes=12, name=None):
+        arrays, specs, buffers, layout, takes = [], [], [], [], []
+        for arg in args:
+            if isinstance(arg, Take):
+                layout.append(0)
+                takes.append((len(arrays), arg))
+                arrays.append(arg.array)
+                specs.append(HBM)
+                buffers.append(pltpu.VMEM(arg.shape, arg.array.dtype))
+            elif isinstance(arg, Raw):
+                layout.append(0)
+                arrays.append(arg.array)
+                specs.append(arg.spec)
+            elif isinstance(arg, (list, tuple)):
+                layout.append(len(arg))
+                arrays += arg
+                specs += [VMEM] * len(arg)
+            else:
+                layout.append(0)
+                arrays.append(arg)
+                specs.append(VMEM)
+        if takes:
+            buffers.append(pltpu.SemaphoreType.DMA((len(takes),)))
+        out_layout = [len(out) if isinstance(out, list) else 0 for out in outs]
+        out_shapes = [o for out in outs for o in (out if isinstance(out, list) else [out])]
+
+        def joined(refs, layout):
+            refs = list(refs)
+            return [
+                Rows([refs.pop(0) for _ in range(count)]) if count else refs.pop(0)
+                for count in layout
+            ]
+
+        def body(*refs):
+            inputs = list(refs[: len(arrays)])
+            rest = refs[len(arrays) + 1 :]
+            results, rest = rest[: len(out_shapes)], rest[len(out_shapes) + 1 :]
+            own, rest = rest[: len(scratch)], rest[len(scratch) :]
+            copies = []
+            for place, (i, take) in enumerate(takes):
+                source = inputs[i]
+                if take.index is not None:
+                    source = source.at[take.index()]
+                copies.append(pltpu.make_async_copy(source, rest[place], rest[-1].at[place]))
+                inputs[i] = rest[place]
+            for copy in copies:
+                copy.start()
+            for copy in copies:
+                copy.wait()
+            kernel(*joined(inputs, layout), *joined(results, out_layout), *own)
+
+        results = pl.pallas_call(
+            body,
+            out_shape=(*out_shapes, shaped(8, LANES)),
+            in_specs=[*specs, HBM],
+            out_specs=tuple([VMEM] * len(out_shapes) + [HBM]),
+            scratch_shapes=[*scratch, *buffers],
+            input_output_aliases={len(arrays): len(out_shapes)},
+            compiler_params=pltpu.CompilerParams(vmem_limit_bytes=megabytes * 1024 * 1024),
+            cost_estimate=pl.CostEstimate(flops=0, bytes_accessed=0, transcendentals=0),
+            name=name,
+        )(*arrays, self.token)
+        self.token = results[-1]
+        found = list(results[:-1])
+        return [
+            [found.pop(0) for _ in range(count)] if count else found.pop(0) for count in out_layout
+        ]
+
+
+def sum_kernel(*refs):
+    total = refs[0][...]
+    for ref in refs[1:-1]:
+        total = total + ref[...]
+    refs[-1][...] = total
+
+
+def pairs_kernel(*refs):
+    terms = [ref[...] for ref in refs[:-1]]
+    while len(terms) > 1:
+        terms = [terms[i] + terms[i + 1] for i in range(0, len(terms), 2)]
+    refs[-1][...] = terms[0]
+
+
+def add_rows(line, terms, name):
+    return line.call(sum_kernel, [shaped(*terms[0].shape)], terms, name=name)[0]
+
+
+def sum_rows(line, keep, arrived, name):
+    mine, theirs = keep, arrived
+    for bit in range(1, log2_of(lax.axis_size("tensor"))):
+        mine = add_rows(line, [mine, theirs], name)
+        theirs = swap(mine, "tensor", 1 << bit)
+    return mine, theirs
+
+
+def sum_all(line, values, axis, name, most=2):
+    bits = log2_of(lax.axis_size(axis))
+    for start in range(0, bits, most):
+        taken = min(most, bits - start)
+        terms = [values] + [
+            swap(values, axis, distance << start) for distance in range(1, 1 << taken)
+        ]
+        values = line.call(pairs_kernel, [shaped(*values.shape)], terms, name=name)[0]
+    return values
+
+
+class Piece:
+    def __init__(self, name, window, bits):
+        self.name, self.window, self.bits = name, window, bits
+        self.terms, self.stage = [], 0
+
+    def start(self, send):
+        self.terms = [swap(send, "dp", 1 << self.bits[0])]
+        self.stage = 1
+
+    def hold(self, keep):
+        self.terms.insert(0, keep)
+        self.size = keep.shape[0]
+
+    def advance(self, line):
+        self.size //= 2
+        shape = (self.size,) + self.terms[0].shape[1:]
+        index = lambda size=self.size: (pl.ds(size, size),)
+        outgoing = line.call(
+            sum_kernel,
+            [shaped(*shape)],
+            [Take(term, shape, index) for term in self.terms],
+            name="sum_" + self.name,
+        )[0]
+        self.terms.append(swap(outgoing, "dp", 1 << self.bits[self.stage]))
+        self.stage += 1
 
 
 def project(normed, weights, cosine, sine):
@@ -213,49 +339,63 @@
 
 
 def first_kernel(
-    live_ref, x_ref, norm_ref, cos_ref, sin_ref, qkv_ref, out_ref,
+    live_ref, x_any, norm_any, cos_any, sin_any, qkv_any, out_any,
     qkv_low_ref, out_low_ref, normed_ref, q_ref, k_ref, v_ref, attn_ref, mass_ref, send_ref, keep_ref,
-    qkv_in, out_in, arrived,
+    x_ref, norm_ref, cos_ref, sin_ref, qkv_in, out_in, arrived,
 ):
+    part = x_ref.shape[0]
+    sources = [x_any.at[pl.ds(0, part)], norm_any, cos_any.at[pl.ds(0, part)], sin_any.at[pl.ds(0, part)]]
+    targets = [x_ref, norm_ref, cos_ref, sin_ref]
+    sources += [qkv_any.at[j] for j in range(3)] + [out_any]
+    targets += [qkv_in.at[j] for j in range(3)] + [out_in]
     copies = [
-        pltpu.make_async_copy(qkv_ref.at[j], qkv_in.at[j], arrived.at[j]) for j in range(3)
+        pltpu.make_async_copy(source, target, arrived.at[i])
+        for i, (source, target) in enumerate(zip(sources, targets))
     ]
-    copies.append(pltpu.make_async_copy(out_ref, out_in, arrived.at[3]))
     for copy in copies:
         copy.start()
+    copies[0].wait()
+    copies[1].wait()
     stat, _ = normalize(x_ref[...].astype(WIDE))
     normed = (stat * norm_ref[0:1, :] + norm_ref[1:2, :]).astype(LOW)
     normed_ref[...] = normed
+    copies[2].wait()
+    copies[3].wait()
     weights = []
     for j in range(3):
-        copies[j].wait()
+        copies[4 + j].wait()
         weights.append(qkv_in[j].astype(LOW))
         qkv_low_ref[j] = weights[j]
     query, keys, values = project(normed, weights, cos_ref[...], sin_ref[...])
     q_ref[...], k_ref[...], v_ref[...] = query, keys, values
     attn_ref[...], mass_ref[...] = attend(query, keys, values, 0, live_ref[0])
-    copies[3].wait()
+    copies[7].wait()
     out_low = out_in[...].astype(LOW)
     out_low_ref[...] = out_low
     split_rows(attn_ref, out_low, send_ref, keep_ref, dot)
 
 
 def next_kernel(
-    live_ref, x_ref, norm_ref, cos_ref, sin_ref, qkv_low_ref, out_low_ref, *refs, first_row
+    live_ref, x_ref, norm_ref, cos_ref, sin_ref, qkv_low_ref, out_low_ref, *refs, first_row, part
 ):
-    earlier = first_row // x_ref.shape[0]
+    earlier = first_row // part
+    rows = slice(first_row, first_row + part)
     k_before, v_before = refs[:earlier], refs[earlier : 2 * earlier]
     normed_ref, q_ref, k_ref, v_ref, attn_ref, mass_ref, send_ref, keep_ref = refs[2 * earlier :]
-    stat, _ = normalize(x_ref[...].astype(WIDE))
+    stat, _ = normalize(x_ref[rows, :].astype(WIDE))
     normed = (stat * norm_ref[0:1, :] + norm_ref[1:2, :]).astype(LOW)
     normed_ref[...] = normed
     weights = [qkv_low_ref[j] for j in range(3)]
-    query, keys, values = project(normed, weights, cos_ref[...], sin_ref[...])
+    query, keys, values = project(normed, weights, cos_ref[rows, :], sin_ref[rows, :])
     q_ref[...], k_ref[...], v_ref[...] = query, keys, values
     keys = jnp.concatenate([ref[...] for ref in k_before] + [keys], axis=0)
     values = jnp.concatenate([ref[...] for ref in v_before] + [values], axis=0)
     attn_ref[...], mass_ref[...] = attend(query, keys, values, first_row, live_ref[0])
     split_rows(attn_ref, out_low_ref[...], send_ref, keep_ref, dot)
+
+
+def cast_kernel(wide_ref, low_ref):
+    low_ref[...] = wide_ref[...].astype(LOW)
 
 
 def middle_kernel(first_row, x_ref, norm_ref, mine_ref, theirs_ref, branch_ref, hidden_ref, normed_ref):
@@ -452,12 +592,13 @@
     refs[-1][...] = whole_rows(refs[:-1], (0, refs[0].shape[1]))
 
 
-def narrow_products(kernel, left, right, jobs, outs, own):
+def narrow_products(line, kernel, left, right, jobs, outs, own):
     rank = lax.axis_index("dp")
     joined = []
     for arrays in (left, right):
         rows = sum(array.shape[0] for array in arrays)
-        joined.append(call(rounded_kernel, [shaped(rows, arrays[0].shape[1], kind=LOW)], arrays)[0])
+        low = shaped(rows, arrays[0].shape[1], kind=LOW)
+        joined.append(line.call(rounded_kernel, [low], arrays, name="rounded")[0])
     results = []
     for (distances, window), out in zip(jobs, outs):
         pick = lambda array: jnp.concatenate(
@@ -478,14 +619,14 @@
     return results
 
 
-def owner_products(kernel, left, right, pieces, own, send, name):
+def owner_products(line, kernel, left, right, pieces, own, send, name):
     count = lax.axis_size("dp")
     jobs, outs = [], []
-    for window, bits in pieces:
-        order = chunk_order(count, bits)
+    for piece in pieces:
+        order = chunk_order(count, piece.bits)
         order = order[count // 2 :] if send else order[: count // 2]
-        jobs.append((order, window))
-        size = window[1] - window[0]
+        jobs.append((order, piece.window))
+        size = piece.window[1] - piece.window[0]
         if kernel is owned_columns_kernel:
             outs.append(shaped(len(order), size, own))
         elif kernel is owned_rows_kernel:
@@ -493,25 +634,14 @@
         else:
             outs.append(shaped(len(order), size, own, right[0].shape[1] // 3))
     if own % LANES:
-        return narrow_products(kernel, left, right, jobs, outs, own)
-    rows = sum(array.shape[0] for array in left)
-    flops = 2 * rows * sum(int(np.prod(out.shape)) for out in outs)
-    return call(
+        return narrow_products(line, kernel, left, right, jobs, outs, own)
+    return line.call(
         functools.partial(kernel, pairs=(len(left), len(right)), jobs=jobs, own=own),
         outs,
         [*left, *right],
-        flops=flops,
+        megabytes=20,
         name=name,
     )
-
-
-def cut_windows(size):
-    cut = size // 4 * 3
-    return [(0, cut), (cut, size)]
-
-
-def first_block(array):
-    return pl.BlockSpec((1,) + array.shape[1:], lambda i: (0,) * array.ndim)
 
 
 def input_back_kernel(rows_ref, qkv_low_ref, send_ref, keep_ref, *, chunks):
@@ -549,12 +679,28 @@
 
 
 def place_kernel(mine_ref, theirs_ref, out_ref, *, chunks):
-    half = theirs_ref.shape[0] // chunks
+    half = mine_ref.shape[0] // chunks
     core = core_index()
     for c in range(chunks):
         rows = slice(c * half, (c + 1) * half)
         out_ref[pl.ds((2 * c + core) * half, half), :] = mine_ref[rows, :].astype(LOW)
         out_ref[pl.ds((2 * c + 1 - core) * half, half), :] = theirs_ref[rows, :].astype(LOW)
+
+
+def norm_sums_kernel(*refs, chunks):
+    input_ref, norms, losses, out_ref = refs[0], refs[1 : 1 + chunks], refs[1 + chunks : -1], refs[-1]
+    out_ref[0:2, :] = input_ref[...]
+    out_ref[2:6, :] = sum(ref[...] for ref in norms[1:]) + norms[0][...]
+    out_ref[6:8, :] = sum(ref[...] for ref in losses[1:]) + losses[0][...]
+
+
+def norm_step_kernel(
+    norm_ref, grad_ref, first_ref, second_ref, norm_new_ref, first_new_ref, second_new_ref
+):
+    first_new, second_new, direction = moment_step(grad_ref[...], first_ref[...], second_ref[...])
+    first_new_ref[...] = first_new
+    second_new_ref[...] = second_new
+    norm_new_ref[...] = norm_ref[...] - learn_rate * direction
 
 
 def moment_step(gradient, first_state, second_state):
@@ -574,13 +720,13 @@
 
 
 def moments_kernel(master_ref, first_ref, second_ref, squares_ref, *refs, row, regions, counts):
-    update_ref, first_new_ref, second_new_ref, table_ref = refs[-4:]
+    kept_ref, update_ref, first_new_ref, second_new_ref, table_ref = refs[-5:]
     at = 0
     sizes = []
     for region, count in zip(regions, counts):
-        gradient = refs[at][0]
+        gradient = refs[at][...]
         for term in refs[at + 1 : at + count]:
-            gradient = gradient + term[0]
+            gradient = gradient + term[...]
         at += count
         first_new, second_new, direction = moment_step(
             gradient, first_ref[region], second_ref[region]
@@ -588,6 +734,7 @@
         first_new_ref[region] = first_new
         second_new_ref[region] = second_new
         master = master_ref[region]
+        kept_ref[region] = master
         update = direction + decay_rate * master
         update_ref[region] = update
         sizes.append((total_of(master * master), total_of(update * update)))
@@ -638,17 +785,18 @@
     local = qkv_weight.shape[2]
     hidden_units = up_weight.shape[1]
     group_count = lax.axis_size("dp")
-    group_rank = lax.axis_index("dp")
     own = width // group_count
-    own_start = group_rank * own
+    own_start = lax.axis_index("dp") * own
     part = row_count // CHUNKS
     half = part // 2
     chunks = range(CHUNKS)
     bits = list(range(log2_of(group_count)))
-    bits_across = [1, 0] + bits[2:] if len(bits) > 1 else bits
-
+    along = {"A": bits, "B": [1, 0] + bits[2:], "C": bits[1:] + [0]}
+
+    line = Line()
     qkv_parts = jnp.transpose(qkv_weight, (1, 0, 2))
     cosine, sine = rotary_tables(row_count)
+    live = Raw(lengths, SMEM)
 
     weight_shapes = [shaped(3, width, local, kind=LOW), shaped(local, width, kind=LOW)]
     chunk_shapes = [
@@ -658,234 +806,233 @@
         shaped(part, local, kind=LOW),
         shaped(part, local, kind=LOW),
         shaped(part, LANES),
-        shaped(half, width),
+        cut(half, width),
         shaped(half, width),
     ]
-    chunk_flops = 2 * part * width * 4 * local + 8 * part * part * local
-    parts = []
-    for c in chunks:
-        rows = slice(c * part, (c + 1) * part)
-        common = [lengths, block_input, norm_params, cosine, sine]
-        row_block = lambda array, c=c: pl.BlockSpec((part, array.shape[1]), lambda i, c=c: (c, 0))
-        specs = [SMEM, row_block(block_input), VMEM, row_block(cosine), row_block(sine)]
-        if c == 0:
-            outs = call(
-                first_kernel,
-                weight_shapes + chunk_shapes,
-                common + [qkv_parts, out_weight],
-                specs + [ANY, ANY],
-                flops=chunk_flops,
-                scratch=[
-                    pltpu.VMEM((3, width, local), WIDE),
-                    pltpu.VMEM((local, width), WIDE),
-                    pltpu.SemaphoreType.DMA((4,)),
-                ],
-                name="attention_first",
+    outs = line.call(
+        first_kernel,
+        weight_shapes + chunk_shapes,
+        [live]
+        + [Raw(a, HBM) for a in (block_input, norm_params, cosine, sine, qkv_parts, out_weight)],
+        scratch=[
+            pltpu.VMEM((part, width), LOW),
+            pltpu.VMEM(norm_params.shape, WIDE),
+            pltpu.VMEM((part, LANES), WIDE),
+            pltpu.VMEM((part, LANES), WIDE),
+            pltpu.VMEM((3, width, local), WIDE),
+            pltpu.VMEM((local, width), WIDE),
+            pltpu.SemaphoreType.DMA((8,)),
+        ],
+        name="attention_first",
+    )
+    qkv_low, out_low = outs[:2]
+    parts = [outs[2:]]
+    arrived = [near(parts[0][6])]
+    for c in chunks[1:]:
+        before = [p[2] for p in parts] + [p[3] for p in parts]
+        parts.append(
+            line.call(
+                functools.partial(next_kernel, first_row=c * part, part=part),
+                chunk_shapes,
+                [live, block_input, norm_params, cosine, sine, qkv_low, out_low] + before,
+                name="attention_next",
             )
-            qkv_low, out_low = outs[:2]
-            parts.append(outs[2:])
-        else:
-            before = [p[2] for p in parts] + [p[3] for p in parts]
-            parts.append(
-                call(
-                    functools.partial(next_kernel, first_row=c * part),
-                    chunk_shapes,
-                    common + [qkv_low, out_low] + before,
-                    specs + [VMEM] * (2 + len(before)),
-                    flops=chunk_flops,
-                    name="attention_next",
-                )
-            )
+        )
+        arrived.append(near(parts[c][6]))
     normed_in, query, keys, values, attn, masses, sends, keeps = zip(*parts)
-    up_low = after(up_weight, sends[-1]).astype(LOW)
-    down_low = after(down_weight, sends[-1]).astype(LOW)
-    branch_terms = [sum_rows(sends[c], keeps[c]) for c in chunks]
-
-    mlp_flops = 4 * part * width * hidden_units
+    branch_terms = [sum_rows(line, keeps[c], arrived[c], "sum_branch") for c in chunks]
+    up_low = line.call(
+        cast_kernel, [shaped(*up_weight.shape, kind=LOW)], [Take(up_weight)], name="cast_up"
+    )[0]
+    down_low = line.call(
+        cast_kernel, [shaped(*down_weight.shape, kind=LOW)], [Take(down_weight)], name="cast_down"
+    )[0]
+
     branch, hidden, normed_mid, up, active, mlp_terms = [], [], [], [], [], []
     for c in chunks:
-        outs = call(
+        outs = line.call(
             functools.partial(middle_kernel, c * part),
-            [shaped(half, width)] * 3,
+            [shaped(half, width), shaped(half, width), cut(half, width)],
             [block_input, norm_params, *branch_terms[c]],
             name="middle",
         )
         branch.append(outs[0])
         hidden.append(outs[1])
-        other = swap(outs[2], "tensor", 1)
-        outs = call(
+        other = near(outs[2])
+        outs = line.call(
             mlp_kernel,
             [
                 shaped(part, width, kind=LOW),
                 shaped(part, hidden_units),
                 shaped(part, hidden_units, kind=LOW),
-                shaped(half, width),
+                cut(half, width),
                 shaped(half, width),
             ],
             [outs[2], other, up_low, down_low],
-            flops=mlp_flops,
             name="mlp",
         )
         normed_mid.append(outs[0])
         up.append(outs[1])
         active.append(outs[2])
-        mlp_terms.append(sum_rows(outs[3], outs[4]))
-
-    block_rows, loss_sums, grad_final, grad_mlp, grad_up_rows, mid_terms = [], [], [], [], [], []
-    down_sends = None
-
-    down_windows = cut_windows(hidden_units)
-    up_windows = down_windows
-    pieces_of = lambda windows: list(zip(windows, [bits, bits_across]))
-
+        mlp_terms.append(sum_rows(line, outs[4], near(outs[3]), "sum_mlp"))
+
+    middle = hidden_units // 2
+    pieces = {
+        "d0": Piece("d0", (0, middle), along["A"]),
+        "d1": Piece("d1", (middle, hidden_units), along["C"]),
+        "u0": Piece("u0", (0, middle), along["A"]),
+        "u1": Piece("u1", (middle, hidden_units), along["A"]),
+        "q0": Piece("q0", (0, 1), along["A"]),
+        "q1": Piece("q1", (1, 2), along["A"]),
+        "q2": Piece("q2", (2, 3), along["B"]),
+        "o0": Piece("o0", (0, local), along["A"]),
+    }
+    of = lambda letter: [piece for name, piece in pieces.items() if name[0] == letter]
+
+    def begin(letter, kernel, left, right, name):
+        for piece, send in zip(
+            of(letter), owner_products(line, kernel, left, right, of(letter), own, True, name)
+        ):
+            piece.start(send)
+
+    def hold(letter, kernel, left, right, name):
+        for piece, keep in zip(
+            of(letter), owner_products(line, kernel, left, right, of(letter), own, False, name)
+        ):
+            piece.hold(keep)
+
+    def advance(*names):
+        for name in names:
+            if pieces[name].stage < len(bits):
+                pieces[name].advance(line)
+
+    block_rows, block_other, loss_sums, grad_final, grad_up_rows, mid_terms = [], [], [], [], [], []
+    grad_blocks = lambda: [block for blocks in grad_final for block in blocks]
     for c in chunks:
-        outs = call(
+        outs = line.call(
             functools.partial(loss_kernel, c * part),
-            [shaped(half, width), shaped(half, width), shaped(2, width)],
+            [cut(half, width), cut(half, width), shaped(2, width)],
             [out_grad, norm_params, hidden[c], *mlp_terms[c]],
             name="loss",
         )
         block_rows.append(outs[0])
         loss_sums.append(outs[2])
-        grad_final += [outs[1], swap(outs[1], "tensor", 1)]
-        mine, other = grad_final[-2:]
+        grad_final += [outs[1], near(outs[1])]
         if c == CHUNKS - 1:
-            down_sends = owner_products(
-                owned_columns_kernel, active, grad_final, pieces_of(down_windows), own, True, "down_send"
-            )
-            mine = after(mine, *down_sends)
-        outs = call(
+            begin("d", owned_columns_kernel, active, grad_blocks(), "down_send")
+        outs = line.call(
             mlp_back_kernel,
             [
                 shaped(part, width, kind=LOW),
                 shaped(part, hidden_units, kind=LOW),
-                shaped(half, width),
+                cut(half, width),
                 shaped(half, width),
             ],
-            [mine, other, up[c], up_low, down_low],
-            flops=mlp_flops,
+            [*grad_final[-2:], up[c], up_low, down_low],
             name="mlp_back",
         )
-        grad_mlp.append(outs[0])
         grad_up_rows.append(outs[1])
-        mid_terms.append(sum_rows(outs[2], outs[3]))
-    down_keeps = owner_products(
-        owned_columns_kernel, active, grad_final, pieces_of(down_windows), own, False, "down_keep"
-    )
-    up_sends = owner_products(
-        owned_rows_kernel, normed_mid, grad_up_rows, pieces_of(up_windows), own, True, "up_send"
-    )
-    up_keeps = owner_products(
-        owned_rows_kernel, normed_mid, grad_up_rows, pieces_of(up_windows), own, False, "up_keep"
-    )
-    down_terms = [
-        scatter_terms(s, k, piece[1])
-        for s, k, piece in zip(down_sends, down_keeps, pieces_of(down_windows))
-    ]
-    up_terms = [
-        scatter_terms(s, k, piece[1])
-        for s, k, piece in zip(up_sends, up_keeps, pieces_of(up_windows))
-    ]
+        crossing = near(outs[2])
+        if c == CHUNKS - 1:
+            begin("u", owned_rows_kernel, normed_mid, grad_up_rows, "up_send")
+        mid_terms.append(sum_rows(line, outs[3], crossing, "sum_mid"))
+        block_other.append(near(block_rows[c]))
+    hold("d", owned_columns_kernel, active, grad_blocks(), "down_keep")
+    hold("u", owned_rows_kernel, normed_mid, grad_up_rows, "up_keep")
+    block_output = line.call(
+        functools.partial(place_kernel, chunks=CHUNKS),
+        [shaped(row_count, width, kind=LOW)],
+        [sum(block_rows, []), sum(block_other, [])],
+        name="place_output",
+    )[0]
 
     grad_hidden, norms_sums, own_back, other_back = [], [], [], []
     for c in chunks:
-        outs = call(
+        outs = line.call(
             functools.partial(norms_back_kernel, c * part),
-            [shaped(half, width), shaped(half, width), shaped(4, width)],
+            [shaped(half, width), cut(half, width), shaped(4, width)],
             [out_grad, norm_params, hidden[c], branch[c], *mid_terms[c]],
             name="norms_back",
         )
         grad_hidden.append(outs[0])
         norms_sums.append(outs[2])
         own_back.append(outs[1])
-        other_back.append(swap(outs[1], "tensor", 1))
-    grad_branch, grad_rows = call(
+        other_back.append(near(outs[1]))
+    advance("d1")
+    grad_branch, grad_rows = line.call(
         functools.partial(attention_back_kernel, chunks=CHUNKS),
         [shaped(row_count, width, kind=LOW), shaped(row_count, 3 * local, kind=LOW)],
-        [lengths, out_low, cosine, sine, *own_back, *other_back, *query, *keys, *values, *masses],
-        [SMEM] + [VMEM] * (3 + 6 * CHUNKS),
-        flops=2 * row_count * width * local + 10 * row_count * row_count * local,
+        [live, out_low, cosine, sine, *own_back, *other_back, *query, *keys, *values, *masses],
         scratch=[pltpu.VMEM((row_count, local), WIDE), pltpu.VMEM((row_count, local), WIDE)],
         name="attention_back",
     )
-    qkv_pieces = [((1, 3), bits), ((0, 1), bits_across)]
-    out_pieces = [((0, local), bits)]
-    qkv_sends = owner_products(
-        owned_parts_kernel, normed_in, [grad_rows], qkv_pieces, own, True, "qkv_send"
-    )
-    out_sends = owner_products(
-        owned_columns_kernel, attn, [grad_branch], out_pieces, own, True, "out_send"
-    )
-    qkv_keeps = owner_products(
-        owned_parts_kernel, normed_in, [grad_rows], qkv_pieces, own, False, "qkv_keep"
-    )
-    out_keeps = owner_products(
-        owned_columns_kernel, attn, [grad_branch], out_pieces, own, False, "out_keep"
-    )
-    qkv_terms = [
-        scatter_terms(s, k, piece[1]) for s, k, piece in zip(qkv_sends, qkv_keeps, qkv_pieces)
-    ]
-    out_terms = [
-        scatter_terms(s, k, piece[1]) for s, k, piece in zip(out_sends, out_keeps, out_pieces)
-    ]
-
-    send, keep = call(
+    begin("q", owned_parts_kernel, normed_in, [grad_rows], "qkv_send")
+    begin("o", owned_columns_kernel, attn, [grad_branch], "out_send")
+    send, keep = line.call(
         functools.partial(input_back_kernel, chunks=CHUNKS),
-        [shaped(row_count // 2, width)] * 2,
+        [cut(row_count // 2, width), shaped(row_count // 2, width)],
         [grad_rows, qkv_low],
-        flops=2 * row_count * width * 3 * local,
         name="input_back",
     )
-    in_terms = sum_rows(send, keep)
-    input_rows, input_sums = call(
+    crossing = near(send)
+    advance("d0")
+    hold("q", owned_parts_kernel, normed_in, [grad_rows], "qkv_keep")
+    hold("o", owned_columns_kernel, attn, [grad_branch], "out_keep")
+    in_terms = sum_rows(line, keep, crossing, "sum_in")
+    advance("d1", "u0", "d0")
+
+    input_rows, input_sums = line.call(
         functools.partial(input_norm_kernel, chunks=CHUNKS),
-        [shaped(row_count // 2, width), shaped(2, width)],
+        [cut(row_count // 2, width), shaped(2, width)],
         [block_input, norm_params, *in_terms, *grad_hidden],
         name="input_norm",
     )
-
-    def place(mine, name):
-        stacked = mine[0] if len(mine) == 1 else jnp.concatenate(mine, axis=0)
-        theirs = swap(stacked, "tensor", 1)
-        return call(
-            functools.partial(place_kernel, chunks=CHUNKS),
-            [shaped(row_count, width, kind=LOW)],
-            [stacked, theirs],
-            name=name,
-        )[0]
-
-    block_output = place(block_rows, "place_output")
-    input_grad = place([input_rows], "place_input")
-
-    def total(arrays):
-        result = arrays[0]
-        for array in arrays[1:]:
-            result = result + array
-        return result
-
-    grad_norms = jnp.concatenate([input_sums, total(norms_sums), total(loss_sums)], axis=0)
-    grad_norms = grad_norms + swap(grad_norms, "tensor", 1)
-    norm_chunks = jnp.stack(
-        [
-            lax.dynamic_slice_in_dim(grad_norms, (group_rank ^ distance) * own, own, 1)
-            for distance in chunk_order(group_count, bits)
+    input_other = near(input_rows)
+    advance("q2")
+    input_grad = line.call(
+        functools.partial(place_kernel, chunks=CHUNKS),
+        [shaped(row_count, width, kind=LOW)],
+        [input_rows, input_other],
+        name="place_input",
+    )[0]
+    grad_norms = line.call(
+        functools.partial(norm_sums_kernel, chunks=CHUNKS),
+        [shaped(8, width)],
+        [input_sums, *norms_sums, *loss_sums],
+        name="norm_sums",
+    )[0]
+    grad_norms = line.call(
+        sum_kernel,
+        [shaped(8, width)],
+        [grad_norms, swap(grad_norms, "tensor", 1)],
+        name="sum_norms",
+    )[0]
+    advance("u1", "u0")
+    grad_norms = sum_all(line, grad_norms, "dp", "sum_norms")
+    advance("u1", "q0", "q1")
+    columns = lambda: (slice(None), pl.ds(pl.multiple_of(lax.axis_index("dp") * own, own), own))
+    mine = lambda array, axis: lax.dynamic_slice_in_dim(array, own_start, own, axis)
+    if own % LANES:
+        norm_args = [mine(norm_params, 1), mine(grad_norms, 1)]
+    else:
+        norm_args = [
+            Take(norm_params, (8, own), columns),
+            Take(grad_norms, (8, own), columns),
         ]
-    )
-    middle = group_count // 2
-    norm_gradient = total(
-        [term[0] for term in scatter_terms(norm_chunks[middle:], norm_chunks[:middle], bits)]
-    )
-    norm_own = lax.dynamic_slice_in_dim(norm_params, own_start, own, 1)
-    norm_first_new, norm_second_new, norm_direction = moment_step(
-        norm_gradient, norm_first, norm_second
-    )
-    norm_new = norm_own - learn_rate * norm_direction
-
+    norm_new, norm_first_new, norm_second_new = line.call(
+        norm_step_kernel,
+        [shaped(8, own)] * 3,
+        [*norm_args, Take(norm_first), Take(norm_second)],
+        name="norm_step",
+    )
+
+    rows = lambda: (pl.ds(pl.multiple_of(lax.axis_index("dp") * own, own), own),)
+    part_rows = lambda: (slice(None), *rows())
     masters = [
-        jnp.transpose(lax.dynamic_slice_in_dim(qkv_weight, own_start, own, 0), (1, 0, 2)),
-        lax.dynamic_slice_in_dim(out_weight, own_start, own, 1),
-        lax.dynamic_slice_in_dim(up_weight, own_start, own, 0),
-        lax.dynamic_slice_in_dim(down_weight, own_start, own, 1),
+        Take(qkv_parts, (3, own, local), part_rows),
+        Take(mine(out_weight, 1)) if own % LANES else Take(out_weight, (local, own), columns),
+        Take(up_weight, (own, hidden_units), rows),
+        Take(mine(down_weight, 1)) if own % LANES else Take(down_weight, (hidden_units, own), columns),
     ]
     states = [
         (jnp.transpose(qkv_first, (1, 0, 2)), jnp.transpose(qkv_second, (1, 0, 2))),
@@ -894,32 +1041,50 @@
         (down_first, down_second),
     ]
     everything = slice(None)
-    regions = [
-        [(slice(*w), everything, everything) for w, _ in qkv_pieces],
-        [(slice(*w), everything) for w, _ in out_pieces],
-        [(everything, slice(*w)) for w in up_windows],
-        [(slice(*w), everything) for w in down_windows],
-    ]
     table = jnp.zeros((8, LANES), WIDE)
     stepped = [None] * 4
-    for index, terms in ((3, down_terms), (2, up_terms), (1, out_terms), (0, qkv_terms)):
-        flat = [term for piece in terms for term in piece]
-        counts = [len(piece) for piece in terms]
+
+    def step(index, letter):
+        nonlocal table
+        found = of(letter)
+        for piece in found:
+            while piece.stage < len(bits):
+                piece.advance(line)
+        if letter == "u":
+            regions = [(everything, slice(*piece.window)) for piece in found]
+        else:
+            regions = [(slice(*piece.window),) for piece in found]
+        terms = [
+            Take(term, term.shape[1:], lambda: (0,)) for piece in found for term in piece.terms
+        ]
         shape = masters[index].shape
-        outs = call(
-            functools.partial(moments_kernel, row=index, regions=regions[index], counts=counts),
-            [shaped(*shape)] * 3 + [shaped(8, LANES)],
-            [masters[index], *states[index], table, *flat],
-            [VMEM] * 4 + [first_block(term) for term in flat],
-            name="moments_" + ("qkv", "out", "up", "down")[index],
+        outs = line.call(
+            functools.partial(
+                moments_kernel,
+                row=index,
+                regions=regions,
+                counts=[len(piece.terms) for piece in found],
+            ),
+            [shaped(*shape)] * 4 + [shaped(8, LANES)],
+            [masters[index], *[Take(state) for state in states[index]], table, *terms],
+            megabytes=16,
+            name="moments_" + letter,
         )
-        stepped[index] = outs[:3]
-        table = outs[3]
-    squares = sum_all(sum_all(table, "tensor"), "dp")
-    outs = call(
+        stepped[index] = outs[:4]
+        table = outs[4]
+
+    step(3, "d")
+    advance("u1", "q0", "q1", "q2", "o0")
+    step(2, "u")
+    advance("q0", "q1", "q2", "o0")
+    step(1, "o")
+    step(0, "q")
+    squares = sum_all(line, table, "tensor", "sum_squares")
+    squares = sum_all(line, squares, "dp", "sum_squares")
+    outs = line.call(
         masters_kernel,
-        [shaped(*master.shape) for master in masters] + [shaped(8, LANES)],
-        [squares, *masters, *[entry[0] for entry in stepped]],
+        [shaped(*entry[0].shape) for entry in stepped] + [shaped(8, LANES)],
+        [squares, *[entry[0] for entry in stepped], *[entry[1] for entry in stepped]],
         name="masters",
     )
     back = lambda array: jnp.transpose(array, (1, 0, 2))
@@ -928,17 +1093,17 @@
         block_output,
         input_grad,
         back(outs[0]),
-        back(stepped[0][1]),
         back(stepped[0][2]),
+        back(stepped[0][3]),
         outs[1],
-        stepped[1][1],
         stepped[1][2],
+        stepped[1][3],
         outs[2],
-        stepped[2][1],
         stepped[2][2],
+        stepped[2][3],
         outs[3],
-        stepped[3][1],
         stepped[3][2],
+        stepped[3][3],
         norm_new,
         norm_first_new,
         norm_second_new,

time: 345 us -> 286 us (0.83); the launches traced: 343 us -> 281 us
  waiting for transfers between devices: 195 us -> 153 us
  local copies, waits for them, and re-layouts: 43.1 us -> 7.24 us
  starting transfers between devices: 45.9 us -> 66.2 us
  other arithmetic: 9.77 us -> 0.58 us
  Pallas kernels: 47.1 us -> 51.3 us
    ppermute x54 -> x107, waiting for transfers between devices: 195 us -> 153 us  [swap(): return lax.ppermute(values, axis, [(i, i ^ distance) for i in range(count)])]
    unnamed x313 -> x50, local copies, waits for them, and re-layouts: 36.5 us -> 7.1 us
    ppermute x54 -> x107, starting transfers between devices: 45.9 us -> 66.2 us  [swap(): return lax.ppermute(values, axis, [(i, i ^ distance) for i in range(count)])]
    add x29 -> x0, other arithmetic: 7.9 us -> none  [the longest x7 3.8 us: sum_rows(): mine = mine + theirs]
    dynamic_slice x3 -> x0, local copies, waits for them, and re-layouts: 4.59 us -> none  [the longest x1 1.94 us: shards(): lax.dynamic_slice_in_dim(down_weight, own_start, own, 1)]
    pallas_call x30 -> x63, Pallas kernels: 47.1 us -> 51.3 us  [call(): pl.pallas_call(body, out_shape=(*out_shapes, shaped(8, LANES)), in_specs=...]
  transfers between devices with their start and end apart: 54 -> 107, of which waited for: 18 -> 69; matrix products, arithmetic and copies ran while one was open for 5% -> 0% of each run, Pallas kernels for 12% -> 15%
where the time goes in v2:
time: 286 us; the launch traced here: 281 us
  waiting for transfers between devices  153 us (53%)
  starting transfers between devices  66.2 us (23%)
  Pallas kernels  51.3 us (18%)
  local copies, waits for them, and re-layouts  7.24 us (3%)
    ppermute x107, waiting for transfers between devices, swap(): return lax.ppermute(values, axis, [(i, i ^ distance) for i in range(count)])  153 us
    ppermute x107, starting transfers between devices, swap(): return lax.ppermute(values, axis, [(i, i ^ distance) for i in range(count)])  66.2 us
    pallas_call x63, Pallas kernels, call(): pl.pallas_call(body, out_shape=(*out_shapes, shaped(8, LANES)), in_specs=...  51.3 us
    unnamed x50, local copies, waits for them, and re-layouts  7.1 us
  transfers between devices with their start and end apart: 107, of which 69 were waited for; matrix products, arithmetic and copies ran while one was open for 0% of the time, Pallas kernels for 15%

profile of v2, /device:TPU:0, one launch (start us, length us, event | category | flops | bytes accessed | tf_op | source)
XLA Modules:
  0.0 280.6 jit_solution(4213187949604638184)
XLA Ops:
  1.3 1.2 copy-done
  2.5 1.9 copy-done.5
  4.4 1.2 copy-done.7
  8.3 3.4 %attention_first.1 = (bf16[3,1024,256]{2,1,0:T(8,128)(2,1)S(1)}, bf16[256,1024]{1,0:T(8,128)(2,1)S(1)}, bf16[256,1024]{1,0:T(8,128)(2,1)S(1)}, bf16[256,256]{1,0...) custom-call(s32[1]{0:T(128)S(6)} %copy.164.refs_0_, ...), custom_call_target="tpu_custom_call", output_to_operand_aliasing={{13}: (7, {})} | custom-call | tf_op jit(solution)/shard_map/attention_first/pallas_call | solution.py:225
  12.8 2.8 attention_next.1
  15.7 3.0 %collective-permute-start.4 = (f32[128,1024]{1,0:T(8,128)S(1)}, f32[128,1024]{1,0:T(8,128)S(1)}, u32[]{:S(2)}, u32[]{:S(2)}) collective-permute-start(f32[128,1024]{1,0:T(8,128)S(1)} %get-tuple-element.275.refs_2_), channel_id=1, source_target_pairs={{0,2},{1,3},{2,0},{3,1},{4,6},{5,7},{6,4},{7,5},{8,10},{9,11},{10,... | collective-permute-start | bytes 1572872 | tf_op jit(solution)/shard_map/ppermute | solution.py:42
  22.2 9.3 %collective-permute-done.4.refs_3_ = f32[128,1024]{1,0:T(8,128)S(1)} collective-permute-done((f32[128,1024]{1,0:T(8,128)S(1)}, f32[128,1024]{1,0:T(8,128)S(1)}, u32[]{:S(2)}, u32[]{:S(2)}) %collective-permute-start.4) | collective-permute-done | bytes 524320 | tf_op jit(solution)/shard_map/ppermute | solution.py:42
  34.0 1.9 mlp.2
  38.2 2.1 collective-permute-start.17
  40.4 2.3 collective-permute-done.18.refs_3_
  45.3 1.9 mlp.3
  49.4 1.9 collective-permute-start.27
  51.4 2.6 collective-permute-done.17.refs_4_
  56.6 2.5 mlp_back.2
  61.3 3.3 %collective-permute-done.27.refs_4_ = f32[128,1024]{1,0:T(8,128)S(1)} collective-permute-done((f32[128,1024]{1,0:T(8,128)S(1)}, f32[128,1024]{1,0:T(8,128)S(1)}, u32[]{:S(2)}, u32[]{:S(2)}) %collective-permute-start.27) | collective-permute-done | bytes 524320 | tf_op jit(solution)/shard_map/ppermute | solution.py:42
  68.0 1.9 collective-permute-start.62
  70.4 2.5 mlp_back.3
  74.2 1.5 collective-permute-start.52
  78.0 1.5 collective-permute-start.67
  79.5 1.3 collective-permute-done.42.refs_14_
  82.6 1.1 place_output.1
  83.7 5.3 %collective-permute-done.52.refs_5_ = f32[128,1024]{1,0:T(8,128)S(1)} collective-permute-done((f32[128,1024]{1,0:T(8,128)S(1)}, f32[128,1024]{1,0:T(8,128)S(1)}, u32[]{:S(2)}, u32[]{:S(2)}) %collective-permute-start.52) | collective-permute-done | bytes 524320 | tf_op jit(solution)/shard_map/ppermute | solution.py:42
  91.4 8.0 %collective-permute-done.53.refs_5_ = f32[128,1024]{1,0:T(8,128)S(1)} collective-permute-done((f32[128,1024]{1,0:T(8,128)S(1)}, f32[128,1024]{1,0:T(8,128)S(1)}, u32[]{:S(2)}, u32[]{:S(2)}) %collective-permute-start.53) | collective-permute-done | bytes 524320 | tf_op jit(solution)/shard_map/ppermute | solution.py:42
  102.7 4.6 %attention_back.1 = (bf16[512,1024]{1,0:T(8,128)(2,1)S(1)}, bf16[512,768]{1,0:T(8,128)(2,1)S(1)}, f32[8,128]{1,0:T(8,128)S(1)}) custom-call(s32[1]{0:T(128)S(6)} %copy.164.refs_0_, bf16[256,1024]{1,0:T(8,128)(2,1)S(1)} %get-tuple-element.270.refs_6_.refs_1_, f32[512,128]{1,0:T(8,128)S(1)} %copy-done.12, ...), custom_call_target="tpu_custom_call", output_to_operand_aliasing={{2}: (28, {})} | custom-call | tf_op jit(solution)/shard_map/attention_back/pallas_call | solution.py:225
  108.4 2.2 input_back.1
  111.7 1.5 collective-permute-start.70
  114.8 1.6 collective-permute-start.68
  116.4 2.6 collective-permute-start.71
  119.9 22.0 %collective-permute-done.71.refs_2_.refs_10_ = f32[2,512,128]{2,1,0:T(8,128)S(1)} collective-permute-done((f32[2,512,128]{2,1,0:T(8,128)S(1)}, f32[2,512,128]{2,1,0:T(8,128)S(1)}, u32[]{:S(2)}, u32[]{:S(2)}) %collective-permute-start.71) | collective-permute-done | bytes 524320 | tf_op jit(solution)/shard_map/ppermute | solution.py:42
  144.4 1.1 collective-permute-start.83
  145.7 11.1 %collective-permute-done.76.refs_1_.refs_13_ = f32[4,1,128,256]{3,2,1,0:T(8,128)S(1)} collective-permute-done((f32[4,1,128,256]{3,2,1,0:T(8,128)S(1)}, f32[4,1,128,256]{3,2,1,0:T(8,128)S(1)}, u32[]{:S(2)}, u32[]{:S(2)}) %collective-permute-start.76) | collective-permute-done | bytes 524320 | tf_op jit(solution)/shard_map/ppermute | solution.py:42
  158.7 1.1 place_input.1
  160.0 1.1 collective-permute-done.79.refs_1_
  161.9 1.5 collective-permute-start.86
  163.9 4.1 %collective-permute-done.83.refs_2_.refs_6_ = f32[2,128,512]{2,1,0:T(8,128)S(1)} collective-permute-done((f32[2,128,512]{2,1,0:T(8,128)S(1)}, f32[2,128,512]{2,1,0:T(8,128)S(1)}, u32[]{:S(2)}, u32[]{:S(2)}) %collective-permute-start.83) | collective-permute-done | bytes 524320 | tf_op jit(solution)/shard_map/ppermute | solution.py:42
  168.0 19.3 %collective-permute-done.80.refs_1_ = f32[8,1024]{1,0:T(8,128)S(1)} collective-permute-done((f32[8,1024]{1,0:T(8,128)S(1)}, f32[8,1024]{1,0:T(8,128)S(1)}, u32[]{:S(2)}, u32[]{:S(2)}) %collective-permute-start.80) | collective-permute-done | bytes 32800 | tf_op jit(solution)/shard_map/ppermute | solution.py:42
  187.3 1.6 collective-permute-start.82
  189.1 3.0 %collective-permute-done.82.refs_3_ = f32[8,1024]{1,0:T(8,128)S(1)} collective-permute-done((f32[8,1024]{1,0:T(8,128)S(1)}, f32[8,1024]{1,0:T(8,128)S(1)}, u32[]{:S(2)}, u32[]{:S(2)}) %collective-permute-start.82) | collective-permute-done | bytes 32800 | tf_op jit(solution)/shard_map/ppermute | solution.py:42
  192.1 2.8 %collective-permute-start.85 = (f32[8,1024]{1,0:T(8,128)S(1)}, f32[8,1024]{1,0:T(8,128)S(1)}, u32[]{:S(2)}, u32[]{:S(2)}) collective-permute-start(f32[8,1024]{1,0:T(8,128)S(1)} %get-tuple-element.442.refs_0_), channel_id=1, source_target_pairs={{0,16},{4,20},{8,24},{12,28},{16,0},{20,4},{24,8},{28,12},{1,17},{... | collective-permute-start | bytes 98312 | tf_op jit(solution)/shard_map/ppermute | solution.py:42
  195.1 6.8 %collective-permute-done.85.refs_1_ = f32[8,1024]{1,0:T(8,128)S(1)} collective-permute-done((f32[8,1024]{1,0:T(8,128)S(1)}, f32[8,1024]{1,0:T(8,128)S(1)}, u32[]{:S(2)}, u32[]{:S(2)}) %collective-permute-start.85) | collective-permute-done | bytes 32800 | tf_op jit(solution)/shard_map/ppermute | solution.py:42
  201.9 2.1 collective-permute-start.78
  204.4 2.1 collective-permute-start.93
  206.5 1.6 collective-permute-done.77.refs_7_
  209.0 7.7 %collective-permute-done.78.refs_11_ = f32[1,512,128]{2,1,0:T(8,128)S(1)} collective-permute-done((f32[1,512,128]{2,1,0:T(8,128)S(1)}, f32[1,512,128]{2,1,0:T(8,128)S(1)}, u32[]{:S(2)}, u32[]{:S(2)}) %collective-permute-start.78) | collective-permute-done | bytes 262176 | tf_op jit(solution)/shard_map/ppermute | solution.py:42
  216.7 2.0 collective-permute-start.89
  218.7 2.1 moments_d.1
  224.6 7.2 %collective-permute-done.89.refs_7_ = f32[1,128,512]{2,1,0:T(8,128)S(1)} collective-permute-done((f32[1,128,512]{2,1,0:T(8,128)S(1)}, f32[1,128,512]{2,1,0:T(8,128)S(1)}, u32[]{:S(2)}, u32[]{:S(2)}) %collective-permute-start.89) | collective-permute-done | bytes 262176 | tf_op jit(solution)/shard_map/ppermute | solution.py:42
  231.7 2.8 %collective-permute-done.90.refs_11_ = f32[1,128,512]{2,1,0:T(8,128)S(1)} collective-permute-done((f32[1,128,512]{2,1,0:T(8,128)S(1)}, f32[1,128,512]{2,1,0:T(8,128)S(1)}, u32[]{:S(2)}, u32[]{:S(2)}) %collective-permute-start.90) | collective-permute-done | bytes 262176 | tf_op jit(solution)/shard_map/ppermute | solution.py:42
  234.6 2.0 moments_u.1
  237.3 2.9 %collective-permute-start.99 = (f32[1,1,128,256]{3,2,1,0:T(8,128)S(1)}, f32[1,1,128,256]{3,2,1,0:T(8,128)S(1)}, u32[]{:S(2)}, u32[]{:S(2)}) collective-permute-start(f32[1,1,128,256]{3,2,1,0:T(8,128)S(1)} %get-tuple-element.476), channel_id=1, source_target_pairs={{0,16},{4,20},{8,24},{12,28},{16,0},{20,4},{24,8},{28,12},{1,17},{... | collective-permute-start | bytes 393224 | tf_op jit(solution)/shard_map/ppermute | solution.py:42
  240.3 2.8 %collective-permute-start.97 = (f32[1,1,128,256]{3,2,1,0:T(8,128)S(1)}, f32[1,1,128,256]{3,2,1,0:T(8,128)S(1)}, u32[]{:S(2)}, u32[]{:S(2)}) collective-permute-start(f32[1,1,128,256]{3,2,1,0:T(8,128)S(1)} %get-tuple-element.474), channel_id=1, source_target_pairs={{0,16},{4,20},{8,24},{12,28},{16,0},{20,4},{24,8},{28,12},{1,17},{... | collective-permute-start | bytes 393224 | tf_op jit(solution)/shard_map/ppermute | solution.py:42
  243.1 8.0 %collective-permute-done.96.refs_7_ = f32[1,256,128]{2,1,0:T(8,128)S(1)} collective-permute-done((f32[1,256,128]{2,1,0:T(8,128)S(1)}, f32[1,256,128]{2,1,0:T(8,128)S(1)}, u32[]{:S(2)}, u32[]{:S(2)}) %collective-permute-start.96) | collective-permute-done | bytes 131104 | tf_op jit(solution)/shard_map/ppermute | solution.py:42
  251.2 1.9 moments_o.1
  254.0 2.8 %collective-permute-done.98.refs_11_ = f32[1,1,128,256]{3,2,1,0:T(8,128)S(1)} collective-permute-done((f32[1,1,128,256]{3,2,1,0:T(8,128)S(1)}, f32[1,1,128,256]{3,2,1,0:T(8,128)S(1)}, u32[]{:S(2)}, u32[]{:S(2)}) %collective-permute-start.98) | collective-permute-done | bytes 131104 | tf_op jit(solution)/shard_map/ppermute | solution.py:42
  256.8 1.7 collective-permute-done.97.refs_7_
  258.5 4.1 %moments_q.1 = (f32[3,128,256]{2,1,0:T(8,128)S(1)}, f32[3,128,256]{2,1,0:T(8,128)S(1)}, f32[3,128,256]{2,1,0:T(8,128)}, f32[3,128,256]{2,1,0:T(8,128)}, f32[8,128]{1,0:T(8,128)S(1)}, /*index=5*/f32[8,128]{1,0:T(8,128)S(1)}) custom-call(f32[3,1024,256]{2,1,0:T(8,128)S(1)} %bitcast.9, f32[3,128,256]{2,1,0:T(8,128)S(1)} %bitcast.10, ...), custom_call_target="tpu_custom_call", output_to_operand_aliasing={{5}: (16, {})} | custom-call | tf_op jit(solution)/shard_map/moments_q/pallas_call | solution.py:225
  262.7 1.7 collective-permute-start.101
  264.5 1.8 collective-permute-done.101.refs_2_
  267.4 1.8 collective-permute-start.103
  269.1 1.7 collective-permute-start.105
  271.0 1.8 collective-permute-done.104.refs_2_
  273.7 2.7 collective-permute-start.106
  276.4 1.8 collective-permute-done.106.refs_1_
  278.2 1.3 masters.1
  (267 shorter events, 57.4 us)
Async XLA Ops:
  11.7 3.9 %collective-permute-start = (f32[32,1024]{1,0:T(8,128)S(1)}, f32[32,1024]{1,0:T(8,128)S(1)}, u32[]{:S(2)}, u32[]{:S(2)}) collective-permute-start(f32[32,1024]{1,0:T(8,128)S(1)} %get-tuple-element.265), channel_id=1, source_target_pairs={{0,1},{1,0},{2,3},{3,2},{4,5},{5,4},{6,7},{7,6},{8,9},{9,8},{10,11... | collective-permute-start | bytes 393224 | tf_op jit(solution)/shard_map/ppermute | solution.py:42
  12.2 3.4 %collective-permute-start.1 = (f32[32,1024]{1,0:T(8,128)S(1)}, f32[32,1024]{1,0:T(8,128)S(1)}, u32[]{:S(2)}, u32[]{:S(2)}) collective-permute-start(f32[32,1024]{1,0:T(8,128)S(1)} %get-tuple-element.266), channel_id=1, source_target_pairs={{0,1},{1,0},{2,3},{3,2},{4,5},{5,4},{6,7},{7,6},{8,9},{9,8},{10,11... | collective-permute-start | bytes 393224 | tf_op jit(solution)/shard_map/ppermute | solution.py:42
  12.3 3.3 %collective-permute-start.2 = (f32[32,1024]{1,0:T(8,128)S(1)}, f32[32,1024]{1,0:T(8,128)S(1)}, u32[]{:S(2)}, u32[]{:S(2)}) collective-permute-start(f32[32,1024]{1,0:T(8,128)S(1)} %get-tuple-element.267), channel_id=1, source_target_pairs={{0,1},{1,0},{2,3},{3,2},{4,5},{5,4},{6,7},{7,6},{8,9},{9,8},{10,11... | collective-permute-start | bytes 393224 | tf_op jit(solution)/shard_map/ppermute | solution.py:42
  12.8 2.9 %collective-permute-start.3 = (f32[32,1024]{1,0:T(8,128)S(1)}, f32[32,1024]{1,0:T(8,128)S(1)}, u32[]{:S(2)}, u32[]{:S(2)}) collective-permute-start(f32[32,1024]{1,0:T(8,128)S(1)} %get-tuple-element.268), channel_id=1, source_target_pairs={{0,1},{1,0},{2,3},{3,2},{4,5},{5,4},{6,7},{7,6},{8,9},{9,8},{10,11... | collective-permute-start | bytes 393224 | tf_op jit(solution)/shard_map/ppermute | solution.py:42
  15.7 15.7 %collective-permute-start.4 = (f32[128,1024]{1,0:T(8,128)S(1)}, f32[128,1024]{1,0:T(8,128)S(1)}, u32[]{:S(2)}, u32[]{:S(2)}) collective-permute-start(f32[128,1024]{1,0:T(8,128)S(1)} %get-tuple-element.275.refs_2_), channel_id=1, source_target_pairs={{0,2},{1,3},{2,0},{3,1},{4,6},{5,7},{6,4},{7,5},{8,10},{9,11},{10,... | collective-permute-start | bytes 1572872 | tf_op jit(solution)/shard_map/ppermute | solution.py:42
  20.8 21.8 %collective-permute-start.18 = (f32[128,1024]{1,0:T(8,128)S(1)}, f32[128,1024]{1,0:T(8,128)S(1)}, u32[]{:S(2)}, u32[]{:S(2)}) collective-permute-start(f32[128,1024]{1,0:T(8,128)S(1)} %get-tuple-element.300.refs_2_), channel_id=1, source_target_pairs={{0,2},{1,3},{2,0},{3,1},{4,6},{5,7},{6,4},{7,5},{8,10},{9,11},{10,... | collective-permute-start | bytes 1572872 | tf_op jit(solution)/shard_map/ppermute | solution.py:42
  38.2 15.7 %collective-permute-start.17 = (f32[128,1024]{1,0:T(8,128)S(1)}, f32[128,1024]{1,0:T(8,128)S(1)}, u32[]{:S(2)}, u32[]{:S(2)}) collective-permute-start(f32[128,1024]{1,0:T(8,128)S(1)} %get-tuple-element.299.refs_3_), channel_id=1, source_target_pairs={{0,2},{1,3},{2,0},{3,1},{4,6},{5,7},{6,4},{7,5},{8,10},{9,11},{10,... | collective-permute-start | bytes 1572872 | tf_op jit(solution)/shard_map/ppermute | solution.py:42
  49.4 15.2 %collective-permute-start.27 = (f32[128,1024]{1,0:T(8,128)S(1)}, f32[128,1024]{1,0:T(8,128)S(1)}, u32[]{:S(2)}, u32[]{:S(2)}) collective-permute-start(f32[128,1024]{1,0:T(8,128)S(1)} %get-tuple-element.319.refs_3_), channel_id=1, source_target_pairs={{0,2},{1,3},{2,0},{3,1},{4,6},{5,7},{6,4},{7,5},{8,10},{9,11},{10,... | collective-permute-start | bytes 1572872 | tf_op jit(solution)/shard_map/ppermute | solution.py:42
  66.2 6.8 %collective-permute-start.36 = (f32[32,1024]{1,0:T(8,128)S(1)}, f32[32,1024]{1,0:T(8,128)S(1)}, u32[]{:S(2)}, u32[]{:S(2)}) collective-permute-start(f32[32,1024]{1,0:T(8,128)S(1)} %get-tuple-element.314.refs_0_), channel_id=1, source_target_pairs={{0,1},{1,0},{2,3},{3,2},{4,5},{5,4},{6,7},{7,6},{8,9},{9,8},{10,11... | collective-permute-start | bytes 393224 | tf_op jit(solution)/shard_map/ppermute | solution.py:42
  68.0 33.4 %collective-permute-start.62 = (f32[4,512,128]{2,1,0:T(8,128)S(1)}, f32[4,512,128]{2,1,0:T(8,128)S(1)}, u32[]{:S(2)}, u32[]{:S(2)}) collective-permute-start(f32[4,512,128]{2,1,0:T(8,128)S(1)} %get-tuple-element.382), channel_id=1, source_target_pairs={{0,8},{4,12},{8,0},{12,4},{16,24},{20,28},{24,16},{28,20},{1,9},{5... | collective-permute-start | bytes 3145736 | tf_op jit(solution)/shard_map/ppermute | solution.py:42
  69.9 3.5 %collective-permute-start.37 = (f32[32,1024]{1,0:T(8,128)S(1)}, f32[32,1024]{1,0:T(8,128)S(1)}, u32[]{:S(2)}, u32[]{:S(2)}) collective-permute-start(f32[32,1024]{1,0:T(8,128)S(1)} %get-tuple-element.315.refs_1_), channel_id=1, source_target_pairs={{0,1},{1,0},{2,3},{3,2},{4,5},{5,4},{6,7},{7,6},{8,9},{9,8},{10,11... | collective-permute-start | bytes 393224 | tf_op jit(solution)/shard_map/ppermute | solution.py:42
  69.9 3.6 %collective-permute-start.38 = (f32[32,1024]{1,0:T(8,128)S(1)}, f32[32,1024]{1,0:T(8,128)S(1)}, u32[]{:S(2)}, u32[]{:S(2)}) collective-permute-start(f32[32,1024]{1,0:T(8,128)S(1)} %get-tuple-element.316.refs_2_), channel_id=1, source_target_pairs={{0,1},{1,0},{2,3},{3,2},{4,5},{5,4},{6,7},{7,6},{8,9},{9,8},{10,11... | collective-permute-start | bytes 393224 | tf_op jit(solution)/shard_map/ppermute | solution.py:42
  73.0 2.8 collective-permute-start.49
  73.4 2.3 collective-permute-start.50
  73.5 2.8 collective-permute-start.51
  74.2 14.8 %collective-permute-start.52 = (f32[128,1024]{1,0:T(8,128)S(1)}, f32[128,1024]{1,0:T(8,128)S(1)}, u32[]{:S(2)}, u32[]{:S(2)}) collective-permute-start(f32[128,1024]{1,0:T(8,128)S(1)} %get-tuple-element.362.refs_4_), channel_id=1, source_target_pairs={{0,2},{1,3},{2,0},{3,1},{4,6},{5,7},{6,4},{7,5},{8,10},{9,11},{10,... | collective-permute-start | bytes 1572872 | tf_op jit(solution)/shard_map/ppermute | solution.py:42
  75.8 2.2 collective-permute-start.40
  76.3 3.2 %collective-permute-start.41 = (f32[32,1024]{1,0:T(8,128)S(1)}, f32[32,1024]{1,0:T(8,128)S(1)}, u32[]{:S(2)}, u32[]{:S(2)}) collective-permute-start(f32[32,1024]{1,0:T(8,128)S(1)} %get-tuple-element.334.refs_5_), channel_id=1, source_target_pairs={{0,1},{1,0},{2,3},{3,2},{4,5},{5,4},{6,7},{7,6},{8,9},{9,8},{10,11... | collective-permute-start | bytes 393224 | tf_op jit(solution)/shard_map/ppermute | solution.py:42
  77.4 22.1 %collective-permute-start.53 = (f32[128,1024]{1,0:T(8,128)S(1)}, f32[128,1024]{1,0:T(8,128)S(1)}, u32[]{:S(2)}, u32[]{:S(2)}) collective-permute-start(f32[128,1024]{1,0:T(8,128)S(1)} %get-tuple-element.369.refs_4_), channel_id=1, source_target_pairs={{0,2},{1,3},{2,0},{3,1},{4,6},{5,7},{6,4},{7,5},{8,10},{9,11},{10,... | collective-permute-start | bytes 1572872 | tf_op jit(solution)/shard_map/ppermute | solution.py:42
  78.0 33.7 %collective-permute-start.67 = (f32[4,512,128]{2,1,0:T(8,128)S(1)}, f32[4,512,128]{2,1,0:T(8,128)S(1)}, u32[]{:S(2)}, u32[]{:S(2)}) collective-permute-start(f32[4,512,128]{2,1,0:T(8,128)S(1)} %get-tuple-element.400), channel_id=1, source_target_pairs={{0,4},{4,0},{8,12},{12,8},{16,20},{20,16},{24,28},{28,24},{1,5},{5... | collective-permute-start | bytes 3145736 | tf_op jit(solution)/shard_map/ppermute | solution.py:42
  80.9 1.7 collective-permute-start.43
  89.9 10.3 %collective-permute-start.55 = (f32[32,1024]{1,0:T(8,128)S(1)}, f32[32,1024]{1,0:T(8,128)S(1)}, u32[]{:S(2)}, u32[]{:S(2)}) collective-permute-start(f32[32,1024]{1,0:T(8,128)S(1)} %get-tuple-element.365.refs_5_), channel_id=1, source_target_pairs={{0,1},{1,0},{2,3},{3,2},{4,5},{5,4},{6,7},{7,6},{8,9},{9,8},{10,11... | collective-permute-start | bytes 393224 | tf_op jit(solution)/shard_map/ppermute | solution.py:42
  91.3 9.6 %collective-permute-start.56 = (f32[32,1024]{1,0:T(8,128)S(1)}, f32[32,1024]{1,0:T(8,128)S(1)}, u32[]{:S(2)}, u32[]{:S(2)}) collective-permute-start(f32[32,1024]{1,0:T(8,128)S(1)} %get-tuple-element.366.refs_6_), channel_id=1, source_target_pairs={{0,1},{1,0},{2,3},{3,2},{4,5},{5,4},{6,7},{7,6},{8,9},{9,8},{10,11... | collective-permute-start | bytes 393224 | tf_op jit(solution)/shard_map/ppermute | solution.py:42
  110.6 4.1 %collective-permute-start.63 = (f32[64,1024]{1,0:T(8,128)S(1)}, f32[64,1024]{1,0:T(8,128)S(1)}, u32[]{:S(2)}, u32[]{:S(2)}) collective-permute-start(f32[64,1024]{1,0:T(8,128)S(1)} %get-tuple-element.395), channel_id=1, source_target_pairs={{0,1},{1,0},{2,3},{3,2},{4,5},{5,4},{6,7},{7,6},{8,9},{9,8},{10,11... | collective-permute-start | bytes 786440 | tf_op jit(solution)/shard_map/ppermute | solution.py:42
  110.8 3.8 %collective-permute-start.64 = (f32[64,1024]{1,0:T(8,128)S(1)}, f32[64,1024]{1,0:T(8,128)S(1)}, u32[]{:S(2)}, u32[]{:S(2)}) collective-permute-start(f32[64,1024]{1,0:T(8,128)S(1)} %get-tuple-element.396), channel_id=1, source_target_pairs={{0,1},{1,0},{2,3},{3,2},{4,5},{5,4},{6,7},{7,6},{8,9},{9,8},{10,11... | collective-permute-start | bytes 786440 | tf_op jit(solution)/shard_map/ppermute | solution.py:42
  111.2 3.5 %collective-permute-start.65 = (f32[64,1024]{1,0:T(8,128)S(1)}, f32[64,1024]{1,0:T(8,128)S(1)}, u32[]{:S(2)}, u32[]{:S(2)}) collective-permute-start(f32[64,1024]{1,0:T(8,128)S(1)} %get-tuple-element.397), channel_id=1, source_target_pairs={{0,1},{1,0},{2,3},{3,2},{4,5},{5,4},{6,7},{7,6},{8,9},{9,8},{10,11... | collective-permute-start | bytes 786440 | tf_op jit(solution)/shard_map/ppermute | solution.py:42
  111.3 3.3 %collective-permute-start.66 = (f32[64,1024]{1,0:T(8,128)S(1)}, f32[64,1024]{1,0:T(8,128)S(1)}, u32[]{:S(2)}, u32[]{:S(2)}) collective-permute-start(f32[64,1024]{1,0:T(8,128)S(1)} %get-tuple-element.398), channel_id=1, source_target_pairs={{0,1},{1,0},{2,3},{3,2},{4,5},{5,4},{6,7},{7,6},{8,9},{9,8},{10,11... | collective-permute-start | bytes 786440 | tf_op jit(solution)/shard_map/ppermute | solution.py:42
  111.7 30.4 %collective-permute-start.70 = (f32[4,128,512]{2,1,0:T(8,128)S(1)}, f32[4,128,512]{2,1,0:T(8,128)S(1)}, u32[]{:S(2)}, u32[]{:S(2)}) collective-permute-start(f32[4,128,512]{2,1,0:T(8,128)S(1)} %get-tuple-element.410), channel_id=1, source_target_pairs={{0,4},{4,0},{8,12},{12,8},{16,20},{20,16},{24,28},{28,24},{1,5},{5... | collective-permute-start | bytes 3145736 | tf_op jit(solution)/shard_map/ppermute | solution.py:42
  114.8 28.6 %collective-permute-start.68 = (f32[256,1024]{1,0:T(8,128)S(1)}, f32[256,1024]{1,0:T(8,128)S(1)}, u32[]{:S(2)}, u32[]{:S(2)}) collective-permute-start(f32[256,1024]{1,0:T(8,128)S(1)} %get-tuple-element.405.refs_2_), channel_id=1, source_target_pairs={{0,2},{1,3},{2,0},{3,1},{4,6},{5,7},{6,4},{7,5},{8,10},{9,11},{10,... | collective-permute-start | bytes 3145736 | tf_op jit(solution)/shard_map/ppermute | solution.py:42
  116.4 25.6 %collective-permute-start.71 = (f32[2,512,128]{2,1,0:T(8,128)S(1)}, f32[2,512,128]{2,1,0:T(8,128)S(1)}, u32[]{:S(2)}, u32[]{:S(2)}) collective-permute-start(f32[2,512,128]{2,1,0:T(8,128)S(1)} %get-tuple-element.411), channel_id=1, source_target_pairs={{0,16},{4,20},{8,24},{12,28},{16,0},{20,4},{24,8},{28,12},{1,17},{... | collective-permute-start | bytes 1572872 | tf_op jit(solution)/shard_map/ppermute | solution.py:42
  118.9 24.3 %collective-permute-start.69 = (f32[2,512,128]{2,1,0:T(8,128)S(1)}, f32[2,512,128]{2,1,0:T(8,128)S(1)}, u32[]{:S(2)}, u32[]{:S(2)}) collective-permute-start(f32[2,512,128]{2,1,0:T(8,128)S(1)} %get-tuple-element.408), channel_id=1, source_target_pairs={{0,8},{4,12},{8,0},{12,4},{16,24},{20,28},{24,16},{28,20},{1,9},{5... | collective-permute-start | bytes 1572872 | tf_op jit(solution)/shard_map/ppermute | solution.py:42
  119.4 41.6 %collective-permute-start.84 = (f32[4,128,512]{2,1,0:T(8,128)S(1)}, f32[4,128,512]{2,1,0:T(8,128)S(1)}, u32[]{:S(2)}, u32[]{:S(2)}) collective-permute-start(f32[4,128,512]{2,1,0:T(8,128)S(1)} %get-tuple-element.438), channel_id=1, source_target_pairs={{0,4},{4,0},{8,12},{12,8},{16,20},{20,16},{24,28},{28,24},{1,5},{5... | collective-permute-start | bytes 3145736 | tf_op jit(solution)/shard_map/ppermute | solution.py:42
  142.0 14.8 %collective-permute-start.76 = (f32[4,1,128,256]{3,2,1,0:T(8,128)S(1)}, f32[4,1,128,256]{3,2,1,0:T(8,128)S(1)}, u32[]{:S(2)}, u32[]{:S(2)}) collective-permute-start(f32[4,1,128,256]{3,2,1,0:T(8,128)S(1)} %get-tuple-element.421), channel_id=1, source_target_pairs={{0,8},{4,12},{8,0},{12,4},{16,24},{20,28},{24,16},{28,20},{1,9},{5... | collective-permute-start | bytes 1572872 | tf_op jit(solution)/shard_map/ppermute | solution.py:42
  144.3 12.5 %collective-permute-start.72 = (f32[64,1024]{1,0:T(8,128)S(1)}, f32[64,1024]{1,0:T(8,128)S(1)}, u32[]{:S(2)}, u32[]{:S(2)}) collective-permute-start(f32[64,1024]{1,0:T(8,128)S(1)} %get-tuple-element.416.refs_0_), channel_id=1, source_target_pairs={{0,1},{1,0},{2,3},{3,2},{4,5},{5,4},{6,7},{7,6},{8,9},{9,8},{10,11... | collective-permute-start | bytes 786440 | tf_op jit(solution)/shard_map/ppermute | solution.py:42
  144.4 23.6 %collective-permute-start.83 = (f32[2,128,512]{2,1,0:T(8,128)S(1)}, f32[2,128,512]{2,1,0:T(8,128)S(1)}, u32[]{:S(2)}, u32[]{:S(2)}) collective-permute-start(f32[2,128,512]{2,1,0:T(8,128)S(1)} %get-tuple-element.436), channel_id=1, source_target_pairs={{0,8},{4,12},{8,0},{12,4},{16,24},{20,28},{24,16},{28,20},{1,9},{5... | collective-permute-start | bytes 1572872 | tf_op jit(solution)/shard_map/ppermute | solution.py:42
  145.5 11.9 %collective-permute-start.73 = (f32[64,1024]{1,0:T(8,128)S(1)}, f32[64,1024]{1,0:T(8,128)S(1)}, u32[]{:S(2)}, u32[]{:S(2)}) collective-permute-start(f32[64,1024]{1,0:T(8,128)S(1)} %get-tuple-element.417.refs_1_), channel_id=1, source_target_pairs={{0,1},{1,0},{2,3},{3,2},{4,5},{5,4},{6,7},{7,6},{8,9},{9,8},{10,11... | collective-permute-start | bytes 786440 | tf_op jit(solution)/shard_map/ppermute | solution.py:42
  156.8 1.9 collective-permute-start.75
  161.2 40.7 %collective-permute-start.88 = (f32[2,128,512]{2,1,0:T(8,128)S(1)}, f32[2,128,512]{2,1,0:T(8,128)S(1)}, u32[]{:S(2)}, u32[]{:S(2)}) collective-permute-start(f32[2,128,512]{2,1,0:T(8,128)S(1)} %get-tuple-element.449), channel_id=1, source_target_pairs={{0,8},{4,12},{8,0},{12,4},{16,24},{20,28},{24,16},{28,20},{1,9},{5... | collective-permute-start | bytes 1572872 | tf_op jit(solution)/shard_map/ppermute | solution.py:42
  161.3 42.8 %collective-permute-start.87 = (f32[4,1,128,256]{3,2,1,0:T(8,128)S(1)}, f32[4,1,128,256]{3,2,1,0:T(8,128)S(1)}, u32[]{:S(2)}, u32[]{:S(2)}) collective-permute-start(f32[4,1,128,256]{3,2,1,0:T(8,128)S(1)} %get-tuple-element.448), channel_id=1, source_target_pairs={{0,4},{4,0},{8,12},{12,8},{16,20},{20,16},{24,28},{28,24},{1,5},{5... | collective-permute-start | bytes 1572872 | tf_op jit(solution)/shard_map/ppermute | solution.py:42
  161.9 42.4 %collective-permute-start.86 = (f32[4,1,128,256]{3,2,1,0:T(8,128)S(1)}, f32[4,1,128,256]{3,2,1,0:T(8,128)S(1)}, u32[]{:S(2)}, u32[]{:S(2)}) collective-permute-start(f32[4,1,128,256]{3,2,1,0:T(8,128)S(1)} %get-tuple-element.446), channel_id=1, source_target_pairs={{0,4},{4,0},{8,12},{12,8},{16,20},{20,16},{24,28},{28,24},{1,5},{5... | collective-permute-start | bytes 1572872 | tf_op jit(solution)/shard_map/ppermute | solution.py:42
  163.4 23.9 %collective-permute-start.80 = (f32[8,1024]{1,0:T(8,128)S(1)}, f32[8,1024]{1,0:T(8,128)S(1)}, u32[]{:S(2)}, u32[]{:S(2)}) collective-permute-start(f32[8,1024]{1,0:T(8,128)S(1)} %get-tuple-element.435.refs_0_), channel_id=1, source_target_pairs={{0,4},{4,0},{8,12},{12,8},{16,20},{20,16},{24,28},{28,24},{1,5},{5... | collective-permute-start | bytes 98312 | tf_op jit(solution)/shard_map/ppermute | solution.py:42
  168.0 21.1 %collective-permute-start.81 = (f32[8,1024]{1,0:T(8,128)S(1)}, f32[8,1024]{1,0:T(8,128)S(1)}, u32[]{:S(2)}, u32[]{:S(2)}) collective-permute-start(f32[8,1024]{1,0:T(8,128)S(1)} %get-tuple-element.435.refs_0_), channel_id=1, source_target_pairs={{0,8},{4,12},{8,0},{12,4},{16,24},{20,28},{24,16},{28,20},{1,9},{5... | collective-permute-start | bytes 98312 | tf_op jit(solution)/shard_map/ppermute | solution.py:42
  187.3 4.8 %collective-permute-start.82 = (f32[8,1024]{1,0:T(8,128)S(1)}, f32[8,1024]{1,0:T(8,128)S(1)}, u32[]{:S(2)}, u32[]{:S(2)}) collective-permute-start(f32[8,1024]{1,0:T(8,128)S(1)} %get-tuple-element.435.refs_0_), channel_id=1, source_target_pairs={{0,12},{4,8},{8,4},{12,0},{16,28},{20,24},{24,20},{28,16},{1,13},{... | collective-permute-start | bytes 98312 | tf_op jit(solution)/shard_map/ppermute | solution.py:42
  192.1 9.8 %collective-permute-start.85 = (f32[8,1024]{1,0:T(8,128)S(1)}, f32[8,1024]{1,0:T(8,128)S(1)}, u32[]{:S(2)}, u32[]{:S(2)}) collective-permute-start(f32[8,1024]{1,0:T(8,128)S(1)} %get-tuple-element.442.refs_0_), channel_id=1, source_target_pairs={{0,16},{4,20},{8,24},{12,28},{16,0},{20,4},{24,8},{28,12},{1,17},{... | collective-permute-start | bytes 98312 | tf_op jit(solution)/shard_map/ppermute | solution.py:42
  194.9 13.1 %collective-permute-start.77 = (f32[1,512,128]{2,1,0:T(8,128)S(1)}, f32[1,512,128]{2,1,0:T(8,128)S(1)}, u32[]{:S(2)}, u32[]{:S(2)}) collective-permute-start(f32[1,512,128]{2,1,0:T(8,128)S(1)} %get-tuple-element.425), channel_id=1, source_target_pairs={{0,16},{4,20},{8,24},{12,28},{16,0},{20,4},{24,8},{28,12},{1,17},{... | collective-permute-start | bytes 786440 | tf_op jit(solution)/shard_map/ppermute | solution.py:42
  201.9 21.6 %collective-permute-start.91 = (f32[4,256,128]{2,1,0:T(8,128)S(1)}, f32[4,256,128]{2,1,0:T(8,128)S(1)}, u32[]{:S(2)}, u32[]{:S(2)}) collective-permute-start(f32[4,256,128]{2,1,0:T(8,128)S(1)} %get-tuple-element.459), channel_id=1, source_target_pairs={{0,4},{4,0},{8,12},{12,8},{16,20},{20,16},{24,28},{28,24},{1,5},{5... | collective-permute-start | bytes 1572872 | tf_op jit(solution)/shard_map/ppermute | solution.py:42
  201.9 14.8 %collective-permute-start.78 = (f32[1,512,128]{2,1,0:T(8,128)S(1)}, f32[1,512,128]{2,1,0:T(8,128)S(1)}, u32[]{:S(2)}, u32[]{:S(2)}) collective-permute-start(f32[1,512,128]{2,1,0:T(8,128)S(1)} %get-tuple-element.426), channel_id=1, source_target_pairs={{0,4},{4,0},{8,12},{12,8},{16,20},{20,16},{24,28},{28,24},{1,5},{5... | collective-permute-start | bytes 786440 | tf_op jit(solution)/shard_map/ppermute | solution.py:42
  204.2 16.6 %collective-permute-start.94 = (f32[2,1,128,256]{3,2,1,0:T(8,128)S(1)}, f32[2,1,128,256]{3,2,1,0:T(8,128)S(1)}, u32[]{:S(2)}, u32[]{:S(2)}) collective-permute-start(f32[2,1,128,256]{3,2,1,0:T(8,128)S(1)} %get-tuple-element.462), channel_id=1, source_target_pairs={{0,8},{4,12},{8,0},{12,4},{16,24},{20,28},{24,16},{28,20},{1,9},{5... | collective-permute-start | bytes 786440 | tf_op jit(solution)/shard_map/ppermute | solution.py:42
  204.4 17.9 %collective-permute-start.93 = (f32[2,1,128,256]{3,2,1,0:T(8,128)S(1)}, f32[2,1,128,256]{3,2,1,0:T(8,128)S(1)}, u32[]{:S(2)}, u32[]{:S(2)}) collective-permute-start(f32[2,1,128,256]{3,2,1,0:T(8,128)S(1)} %get-tuple-element.461), channel_id=1, source_target_pairs={{0,8},{4,12},{8,0},{12,4},{16,24},{20,28},{24,16},{28,20},{1,9},{5... | collective-permute-start | bytes 786440 | tf_op jit(solution)/shard_map/ppermute | solution.py:42
  208.0 14.8 %collective-permute-start.92 = (f32[2,1,128,256]{3,2,1,0:T(8,128)S(1)}, f32[2,1,128,256]{3,2,1,0:T(8,128)S(1)}, u32[]{:S(2)}, u32[]{:S(2)}) collective-permute-start(f32[2,1,128,256]{3,2,1,0:T(8,128)S(1)} %get-tuple-element.460), channel_id=1, source_target_pairs={{0,4},{4,0},{8,12},{12,8},{16,20},{20,16},{24,28},{28,24},{1,5},{5... | collective-permute-start | bytes 786440 | tf_op jit(solution)/shard_map/ppermute | solution.py:42
  216.7 15.1 %collective-permute-start.89 = (f32[1,128,512]{2,1,0:T(8,128)S(1)}, f32[1,128,512]{2,1,0:T(8,128)S(1)}, u32[]{:S(2)}, u32[]{:S(2)}) collective-permute-start(f32[1,128,512]{2,1,0:T(8,128)S(1)} %get-tuple-element.456), channel_id=1, source_target_pairs={{0,16},{4,20},{8,24},{12,28},{16,0},{20,4},{24,8},{28,12},{1,17},{... | collective-permute-start | bytes 786440 | tf_op jit(solution)/shard_map/ppermute | solution.py:42
  220.8 13.7 %collective-permute-start.90 = (f32[1,128,512]{2,1,0:T(8,128)S(1)}, f32[1,128,512]{2,1,0:T(8,128)S(1)}, u32[]{:S(2)}, u32[]{:S(2)}) collective-permute-start(f32[1,128,512]{2,1,0:T(8,128)S(1)} %get-tuple-element.457), channel_id=1, source_target_pairs={{0,16},{4,20},{8,24},{12,28},{16,0},{20,4},{24,8},{28,12},{1,17},{... | collective-permute-start | bytes 786440 | tf_op jit(solution)/shard_map/ppermute | solution.py:42
  223.6 13.1 %collective-permute-start.95 = (f32[2,256,128]{2,1,0:T(8,128)S(1)}, f32[2,256,128]{2,1,0:T(8,128)S(1)}, u32[]{:S(2)}, u32[]{:S(2)}) collective-permute-start(f32[2,256,128]{2,1,0:T(8,128)S(1)} %get-tuple-element.469), channel_id=1, source_target_pairs={{0,8},{4,12},{8,0},{12,4},{16,24},{20,28},{24,16},{28,20},{1,9},{5... | collective-permute-start | bytes 786440 | tf_op jit(solution)/shard_map/ppermute | solution.py:42
  237.2 14.0 %collective-permute-start.96 = (f32[1,256,128]{2,1,0:T(8,128)S(1)}, f32[1,256,128]{2,1,0:T(8,128)S(1)}, u32[]{:S(2)}, u32[]{:S(2)}) collective-permute-start(f32[1,256,128]{2,1,0:T(8,128)S(1)} %get-tuple-element.471), channel_id=1, source_target_pairs={{0,16},{4,20},{8,24},{12,28},{16,0},{20,4},{24,8},{28,12},{1,17},{... | collective-permute-start | bytes 393224 | tf_op jit(solution)/shard_map/ppermute | solution.py:42
  237.3 16.7 %collective-permute-start.99 = (f32[1,1,128,256]{3,2,1,0:T(8,128)S(1)}, f32[1,1,128,256]{3,2,1,0:T(8,128)S(1)}, u32[]{:S(2)}, u32[]{:S(2)}) collective-permute-start(f32[1,1,128,256]{3,2,1,0:T(8,128)S(1)} %get-tuple-element.476), channel_id=1, source_target_pairs={{0,16},{4,20},{8,24},{12,28},{16,0},{20,4},{24,8},{28,12},{1,17},{... | collective-permute-start | bytes 393224 | tf_op jit(solution)/shard_map/ppermute | solution.py:42
  240.2 16.6 %collective-permute-start.98 = (f32[1,1,128,256]{3,2,1,0:T(8,128)S(1)}, f32[1,1,128,256]{3,2,1,0:T(8,128)S(1)}, u32[]{:S(2)}, u32[]{:S(2)}) collective-permute-start(f32[1,1,128,256]{3,2,1,0:T(8,128)S(1)} %get-tuple-element.475), channel_id=1, source_target_pairs={{0,16},{4,20},{8,24},{12,28},{16,0},{20,4},{24,8},{28,12},{1,17},{... | collective-permute-start | bytes 393224 | tf_op jit(solution)/shard_map/ppermute | solution.py:42
  240.3 18.2 %collective-permute-start.97 = (f32[1,1,128,256]{3,2,1,0:T(8,128)S(1)}, f32[1,1,128,256]{3,2,1,0:T(8,128)S(1)}, u32[]{:S(2)}, u32[]{:S(2)}) collective-permute-start(f32[1,1,128,256]{3,2,1,0:T(8,128)S(1)} %get-tuple-element.474), channel_id=1, source_target_pairs={{0,16},{4,20},{8,24},{12,28},{16,0},{20,4},{24,8},{28,12},{1,17},{... | collective-permute-start | bytes 393224 | tf_op jit(solution)/shard_map/ppermute | solution.py:42
  262.6 1.9 collective-permute-start.100
  262.7 3.7 %collective-permute-start.101 = (f32[8,128]{1,0:T(8,128)S(1)}, f32[8,128]{1,0:T(8,128)S(1)}, u32[]{:S(2)}, u32[]{:S(2)}) collective-permute-start(f32[8,128]{1,0:T(8,128)S(1)} %get-tuple-element.478.refs_0_), channel_id=1, source_target_pairs={{0,2},{1,3},{2,0},{3,1},{4,6},{5,7},{6,4},{7,5},{8,10},{9,11},{10,... | collective-permute-start | bytes 12296 | tf_op jit(solution)/shard_map/ppermute | solution.py:42
  264.3 3.0 %collective-permute-start.102 = (f32[8,128]{1,0:T(8,128)S(1)}, f32[8,128]{1,0:T(8,128)S(1)}, u32[]{:S(2)}, u32[]{:S(2)}) collective-permute-start(f32[8,128]{1,0:T(8,128)S(1)} %get-tuple-element.478.refs_0_), channel_id=1, source_target_pairs={{0,3},{1,2},{2,1},{3,0},{4,7},{5,6},{6,5},{7,4},{8,11},{9,10},{10,... | collective-permute-start | bytes 12296 | tf_op jit(solution)/shard_map/ppermute | solution.py:42
  267.4 3.6 %collective-permute-start.103 = (f32[8,128]{1,0:T(8,128)S(1)}, f32[8,128]{1,0:T(8,128)S(1)}, u32[]{:S(2)}, u32[]{:S(2)}) collective-permute-start(f32[8,128]{1,0:T(8,128)S(1)} %get-tuple-element.480.refs_0_), channel_id=1, source_target_pairs={{0,4},{4,0},{8,12},{12,8},{16,20},{20,16},{24,28},{28,24},{1,5},{5... | collective-permute-start | bytes 12296 | tf_op jit(solution)/shard_map/ppermute | solution.py:42
  269.1 3.6 %collective-permute-start.104 = (f32[8,128]{1,0:T(8,128)S(1)}, f32[8,128]{1,0:T(8,128)S(1)}, u32[]{:S(2)}, u32[]{:S(2)}) collective-permute-start(f32[8,128]{1,0:T(8,128)S(1)} %get-tuple-element.480.refs_0_), channel_id=1, source_target_pairs={{0,8},{4,12},{8,0},{12,4},{16,24},{20,28},{24,16},{28,20},{1,9},{5... | collective-permute-start | bytes 12296 | tf_op jit(solution)/shard_map/ppermute | solution.py:42
  269.1 4.5 %collective-permute-start.105 = (f32[8,128]{1,0:T(8,128)S(1)}, f32[8,128]{1,0:T(8,128)S(1)}, u32[]{:S(2)}, u32[]{:S(2)}) collective-permute-start(f32[8,128]{1,0:T(8,128)S(1)} %get-tuple-element.480.refs_0_), channel_id=1, source_target_pairs={{0,12},{4,8},{8,4},{12,0},{16,28},{20,24},{24,20},{28,16},{1,13},{... | collective-permute-start | bytes 12296 | tf_op jit(solution)/shard_map/ppermute | solution.py:42
  273.7 4.5 %collective-permute-start.106 = (f32[8,128]{1,0:T(8,128)S(1)}, f32[8,128]{1,0:T(8,128)S(1)}, u32[]{:S(2)}, u32[]{:S(2)}) collective-permute-start(f32[8,128]{1,0:T(8,128)S(1)} %get-tuple-element.482.refs_0_), channel_id=1, source_target_pairs={{0,16},{4,20},{8,24},{12,28},{16,0},{20,4},{24,8},{28,12},{1,17},{... | collective-permute-start | bytes 12296 | tf_op jit(solution)/shard_map/ppermute | solution.py:42
  (68 other events, 378.5 us)

commit v3 on v2

--- a/solution.py
+++ b/solution.py
@@ -23,6 +23,9 @@
 decay_rate = 0.01
 learn_rate = 0.25
 
+CUT_ATTENTION, CUT_MIDDLE, CUT_MLP, CUT_LOSS = 2, 4, 4, 2
+CUT_MID, CUT_NORMS, CUT_BACK, CUT_INPUT = 2, 2, 2, 2
+
 LOW = jnp.bfloat16
 WIDE = jnp.float32
 VMEM = pl.BlockSpec(memory_space=pltpu.VMEM)
@@ -171,7 +174,7 @@
     def __init__(self):
         self.token = jnp.zeros((8, LANES), WIDE)
 
-    def call(self, kernel, outs, args, scratch=(), megabytes=12, name=None):
+    def call(self, kernel, outs, args, scratch=(), megabytes=12, first=False):
         arrays, specs, buffers, layout, takes = [], [], [], [], []
         for arg in args:
             if isinstance(arg, Take):
@@ -194,6 +197,7 @@
                 specs.append(VMEM)
         if takes:
             buffers.append(pltpu.SemaphoreType.DMA((len(takes),)))
+        token = [] if first else [self.token]
         out_layout = [len(out) if isinstance(out, list) else 0 for out in outs]
         out_shapes = [o for out in outs for o in (out if isinstance(out, list) else [out])]
 
@@ -206,8 +210,8 @@
 
         def body(*refs):
             inputs = list(refs[: len(arrays)])
-            rest = refs[len(arrays) + 1 :]
-            results, rest = rest[: len(out_shapes)], rest[len(out_shapes) + 1 :]
+            rest = refs[len(arrays) + len(token) :]
+            results, rest = rest[: len(out_shapes)], rest[len(out_shapes) + len(token) :]
             own, rest = rest[: len(scratch)], rest[len(scratch) :]
             copies = []
             for place, (i, take) in enumerate(takes):
@@ -224,17 +228,17 @@
 
         results = pl.pallas_call(
             body,
-            out_shape=(*out_shapes, shaped(8, LANES)),
-            in_specs=[*specs, HBM],
-            out_specs=tuple([VMEM] * len(out_shapes) + [HBM]),
+            out_shape=(*out_shapes, *[shaped(8, LANES) for _ in token]),
+            in_specs=[*specs, *[HBM for _ in token]],
+            out_specs=tuple([VMEM] * len(out_shapes) + [HBM for _ in token]),
             scratch_shapes=[*scratch, *buffers],
-            input_output_aliases={len(arrays): len(out_shapes)},
+            input_output_aliases={len(arrays): len(out_shapes)} if token else {},
             compiler_params=pltpu.CompilerParams(vmem_limit_bytes=megabytes * 1024 * 1024),
             cost_estimate=pl.CostEstimate(flops=0, bytes_accessed=0, transcendentals=0),
-            name=name,
-        )(*arrays, self.token)
-        self.token = results[-1]
-        found = list(results[:-1])
+        )(*arrays, *token)
+        found = list(results)
+        if token:
+            self.token = found.pop()
         return [
             [found.pop(0) for _ in range(count)] if count else found.pop(0) for count in out_layout
         ]
@@ -254,54 +258,97 @@
     refs[-1][...] = terms[0]
 
 
-def add_rows(line, terms, name):
-    return line.call(sum_kernel, [shaped(*terms[0].shape)], terms, name=name)[0]
-
-
-def sum_rows(line, keep, arrived, name):
+def sum_rows(line, keep, arrived, count=1):
     mine, theirs = keep, arrived
     for bit in range(1, log2_of(lax.axis_size("tensor"))):
-        mine = add_rows(line, [mine, theirs], name)
-        theirs = swap(mine, "tensor", 1 << bit)
+        mine = line.call(sum_kernel, [cut(*keep.shape, count)], [mine, theirs])[0]
+        theirs = [swap(piece, "tensor", 1 << bit) for piece in mine]
     return mine, theirs
 
 
-def sum_all(line, values, axis, name, most=2):
-    bits = log2_of(lax.axis_size(axis))
-    for start in range(0, bits, most):
-        taken = min(most, bits - start)
-        terms = [values] + [
-            swap(values, axis, distance << start) for distance in range(1, 1 << taken)
-        ]
-        values = line.call(pairs_kernel, [shaped(*values.shape)], terms, name=name)[0]
-    return values
+def sum_terms(values, axis, start, taken):
+    return [values] + [swap(values, axis, distance << start) for distance in range(1, 1 << taken)]
 
 
 class Piece:
-    def __init__(self, name, window, bits):
-        self.name, self.window, self.bits = name, window, bits
+    def __init__(self, weight, window, bits):
+        self.weight, self.window, self.bits = weight, window, bits
         self.terms, self.stage = [], 0
 
-    def start(self, send):
-        self.terms = [swap(send, "dp", 1 << self.bits[0])]
+    def start(self):
+        send = self.weight.products([self], True)[0]
+        self.terms.append(swap(send, "dp", 1 << self.bits[0]))
         self.stage = 1
 
-    def hold(self, keep):
-        self.terms.insert(0, keep)
-        self.size = keep.shape[0]
-
-    def advance(self, line):
-        self.size //= 2
-        shape = (self.size,) + self.terms[0].shape[1:]
-        index = lambda size=self.size: (pl.ds(size, size),)
-        outgoing = line.call(
-            sum_kernel,
-            [shaped(*shape)],
-            [Take(term, shape, index) for term in self.terms],
-            name="sum_" + self.name,
+    def advance(self):
+        if self.stage == len(self.bits):
+            return
+        size = self.terms[0].shape[0] >> self.stage
+        shape = (size,) + self.terms[0].shape[1:]
+        index = lambda: (pl.ds(size, size),)
+        outgoing = self.weight.line.call(
+            sum_kernel, [shaped(*shape)], [Take(term, shape, index) for term in self.terms]
         )[0]
         self.terms.append(swap(outgoing, "dp", 1 << self.bits[self.stage]))
         self.stage += 1
+
+
+class Weight:
+    tables = {}
+
+    def __init__(self, line, row, size, kernel, factors, master, states):
+        self.line, self.row, self.size, self.kernel = line, row, size, kernel
+        self.factors, self.master, self.states = factors, master, states
+        self.pieces = []
+
+    def piece(self, first, last, count, bits):
+        found = Piece(self, (self.size * first // count, self.size * last // count), bits)
+        self.pieces.append(found)
+        return found
+
+    def products(self, pieces, send):
+        own = self.line.own
+        return owner_products(self.line, self.kernel, *self.factors(), pieces, own, send)
+
+    def hold(self):
+        for piece, keep in zip(self.pieces, self.products(self.pieces, False)):
+            piece.terms.insert(0, keep)
+
+    def stage(self):
+        before = [self.master, *[Take(state) for state in self.states]]
+        self.master, *self.states = self.line.call(
+            copy_kernel, [shaped(*self.master.shape)] * 3, before
+        )
+
+    def moments(self):
+        for piece in self.pieces:
+            while piece.stage < len(piece.bits):
+                piece.advance()
+        everything = slice(None)
+        if self.kernel is owned_rows_kernel:
+            regions = [(everything, slice(*piece.window)) for piece in self.pieces]
+        else:
+            regions = [(slice(*piece.window),) for piece in self.pieces]
+        terms = [
+            Take(term, term.shape[1:], lambda: (0,))
+            for piece in self.pieces
+            for term in piece.terms
+        ]
+        states = self.states
+        if isinstance(self.master, Take):
+            states = [Take(state) for state in states]
+        outs = self.line.call(
+            functools.partial(
+                moments_kernel,
+                row=self.row,
+                regions=regions,
+                counts=[len(piece.terms) for piece in self.pieces],
+            ),
+            [shaped(*self.master.shape)] * 4 + [shaped(8, LANES)],
+            [self.master, *states, self.line.table, *terms],
+            megabytes=16,
+        )
+        self.kept, self.update, self.first_new, self.second_new, self.line.table = outs
 
 
 def project(normed, weights, cosine, sine):
@@ -598,7 +645,7 @@
     for arrays in (left, right):
         rows = sum(array.shape[0] for array in arrays)
         low = shaped(rows, arrays[0].shape[1], kind=LOW)
-        joined.append(line.call(rounded_kernel, [low], arrays, name="rounded")[0])
+        joined.append(line.call(rounded_kernel, [low], arrays)[0])
     results = []
     for (distances, window), out in zip(jobs, outs):
         pick = lambda array: jnp.concatenate(
@@ -619,7 +666,7 @@
     return results
 
 
-def owner_products(line, kernel, left, right, pieces, own, send, name):
+def owner_products(line, kernel, left, right, pieces, own, send):
     count = lax.axis_size("dp")
     jobs, outs = [], []
     for piece in pieces:
@@ -640,7 +687,6 @@
         outs,
         [*left, *right],
         megabytes=20,
-        name=name,
     )
 
 
@@ -694,13 +740,10 @@
     out_ref[6:8, :] = sum(ref[...] for ref in losses[1:]) + losses[0][...]
 
 
-def norm_step_kernel(
-    norm_ref, grad_ref, first_ref, second_ref, norm_new_ref, first_new_ref, second_new_ref
-):
-    first_new, second_new, direction = moment_step(grad_ref[...], first_ref[...], second_ref[...])
-    first_new_ref[...] = first_new
-    second_new_ref[...] = second_new
-    norm_new_ref[...] = norm_ref[...] - learn_rate * direction
+def copy_kernel(*refs):
+    half = len(refs) // 2
+    for source, target in zip(refs[:half], refs[half:]):
+        target[...] = source[...]
 
 
 def moment_step(gradient, first_state, second_state):
@@ -746,19 +789,50 @@
         table_ref[place : place + 1, :] = jnp.broadcast_to(amount, (1, LANES))
 
 
-def masters_kernel(squares_ref, *refs):
-    masters, updates = refs[:4], refs[4:8]
-    outs, norms_ref = refs[8:12], refs[12]
-    sizes = jnp.sqrt(squares_ref[0:4, :])
-    steps = jnp.sqrt(squares_ref[4:8, :] + trust_epsilon)
-    norms_ref[0:4, :] = sizes
-    norms_ref[4:8, :] = steps
+def join_kernel(*refs):
+    terms, norms_ref, out_ref = refs[:-2], refs[-2], refs[-1]
+    terms = [ref[...] for ref in terms]
+    while len(terms) > 1:
+        terms = [terms[i] + terms[i + 1] for i in range(0, len(terms), 2)]
+    out_ref[:, 0:LANES] = terms[0]
+    out_ref[:, LANES:] = norms_ref[...]
+
+
+def masters_kernel(norm_ref, first_ref, second_ref, *refs, terms, own):
+    sums, refs = refs[:terms], refs[terms:]
+    masters, updates, outs = refs[:4], refs[4:8], refs[8:12]
+    norms_ref, norm_new_ref, first_new_ref, second_new_ref = refs[12:]
+    total = sums[0][:, 0:LANES]
+    for ref in sums[1:]:
+        total = total + ref[:, 0:LANES]
+    sizes = jnp.sqrt(total[0:4, :])
+    steps = jnp.sqrt(total[4:8, :] + trust_epsilon)
+    lane = lax.broadcasted_iota(jnp.int32, (1, 4), 1)
+    for place, found in ((0, sizes), (1, steps)):
+        row = jnp.zeros((1, 4), WIDE)
+        for index in range(4):
+            row = jnp.where(lane == index, found[index : index + 1, 0:1], row)
+        norms_ref[place : place + 1, :] = row
     ratio = learn_rate * (sizes / steps)
     for index in range(4):
         scale = ratio[index : index + 1, 0:1]
         if len(masters[index].shape) == 3:
             scale = scale.reshape(1, 1, 1)
         outs[index][...] = masters[index][...] - scale * updates[index][...]
+    if own % LANES:
+        gradient = sums[0][:, LANES:]
+        for ref in sums[1:]:
+            gradient = gradient + ref[:, LANES:]
+        norm_new_ref[...] = gradient
+        return
+    start = pl.multiple_of(lax.axis_index("dp") * own, own)
+    gradient = sums[0][:, pl.ds(LANES + start, own)]
+    for ref in sums[1:]:
+        gradient = gradient + ref[:, pl.ds(LANES + start, own)]
+    first_new, second_new, direction = moment_step(gradient, first_ref[...], second_ref[...])
+    first_new_ref[...] = first_new
+    second_new_ref[...] = second_new
+    norm_new_ref[...] = norm_ref[:, pl.ds(start, own)] - learn_rate * direction
 
 
 def shards(
@@ -791,7 +865,6 @@
     half = part // 2
     chunks = range(CHUNKS)
     bits = list(range(log2_of(group_count)))
-    along = {"A": bits, "B": [1, 0] + bits[2:], "C": bits[1:] + [0]}
 
     line = Line()
     qkv_parts = jnp.transpose(qkv_weight, (1, 0, 2))
@@ -806,7 +879,7 @@
         shaped(part, local, kind=LOW),
         shaped(part, local, kind=LOW),
         shaped(part, LANES),
-        cut(half, width),
+        cut(half, width, CUT_ATTENTION),
         shaped(half, width),
     ]
     outs = line.call(
@@ -823,11 +896,12 @@
             pltpu.VMEM((local, width), WIDE),
             pltpu.SemaphoreType.DMA((8,)),
         ],
-        name="attention_first",
+        megabytes=60,
+        first=True,
     )
     qkv_low, out_low = outs[:2]
     parts = [outs[2:]]
-    arrived = [near(parts[0][6])]
+    branch_terms = [sum_rows(line, parts[0][7], near(parts[0][6]))]
     for c in chunks[1:]:
         before = [p[2] for p in parts] + [p[3] for p in parts]
         parts.append(
@@ -835,26 +909,23 @@
                 functools.partial(next_kernel, first_row=c * part, part=part),
                 chunk_shapes,
                 [live, block_input, norm_params, cosine, sine, qkv_low, out_low] + before,
-                name="attention_next",
             )
         )
-        arrived.append(near(parts[c][6]))
-    normed_in, query, keys, values, attn, masses, sends, keeps = zip(*parts)
-    branch_terms = [sum_rows(line, keeps[c], arrived[c], "sum_branch") for c in chunks]
+        branch_terms.append(sum_rows(line, parts[c][7], near(parts[c][6])))
+    normed_in, query, keys, values, attn, masses, _, _ = zip(*parts)
     up_low = line.call(
-        cast_kernel, [shaped(*up_weight.shape, kind=LOW)], [Take(up_weight)], name="cast_up"
+        cast_kernel, [shaped(*up_weight.shape, kind=LOW)], [Take(up_weight)]
     )[0]
     down_low = line.call(
-        cast_kernel, [shaped(*down_weight.shape, kind=LOW)], [Take(down_weight)], name="cast_down"
+        cast_kernel, [shaped(*down_weight.shape, kind=LOW)], [Take(down_weight)]
     )[0]
 
     branch, hidden, normed_mid, up, active, mlp_terms = [], [], [], [], [], []
     for c in chunks:
         outs = line.call(
             functools.partial(middle_kernel, c * part),
-            [shaped(half, width), shaped(half, width), cut(half, width)],
+            [shaped(half, width), shaped(half, width), cut(half, width, CUT_MIDDLE)],
             [block_input, norm_params, *branch_terms[c]],
-            name="middle",
         )
         branch.append(outs[0])
         hidden.append(outs[1])
@@ -865,245 +936,249 @@
                 shaped(part, width, kind=LOW),
                 shaped(part, hidden_units),
                 shaped(part, hidden_units, kind=LOW),
-                cut(half, width),
+                cut(half, width, CUT_MLP),
                 shaped(half, width),
             ],
             [outs[2], other, up_low, down_low],
-            name="mlp",
         )
         normed_mid.append(outs[0])
         up.append(outs[1])
         active.append(outs[2])
-        mlp_terms.append(sum_rows(line, outs[4], near(outs[3]), "sum_mlp"))
-
-    middle = hidden_units // 2
-    pieces = {
-        "d0": Piece("d0", (0, middle), along["A"]),
-        "d1": Piece("d1", (middle, hidden_units), along["C"]),
-        "u0": Piece("u0", (0, middle), along["A"]),
-        "u1": Piece("u1", (middle, hidden_units), along["A"]),
-        "q0": Piece("q0", (0, 1), along["A"]),
-        "q1": Piece("q1", (1, 2), along["A"]),
-        "q2": Piece("q2", (2, 3), along["B"]),
-        "o0": Piece("o0", (0, local), along["A"]),
-    }
-    of = lambda letter: [piece for name, piece in pieces.items() if name[0] == letter]
-
-    def begin(letter, kernel, left, right, name):
-        for piece, send in zip(
-            of(letter), owner_products(line, kernel, left, right, of(letter), own, True, name)
-        ):
-            piece.start(send)
-
-    def hold(letter, kernel, left, right, name):
-        for piece, keep in zip(
-            of(letter), owner_products(line, kernel, left, right, of(letter), own, False, name)
-        ):
-            piece.hold(keep)
-
-    def advance(*names):
-        for name in names:
-            if pieces[name].stage < len(bits):
-                pieces[name].advance(line)
-
-    block_rows, block_other, loss_sums, grad_final, grad_up_rows, mid_terms = [], [], [], [], [], []
-    grad_blocks = lambda: [block for blocks in grad_final for block in blocks]
-    for c in chunks:
+        mlp_terms.append(sum_rows(line, outs[4], near(outs[3])))
+
+    line.own, line.table = own, jnp.zeros((8, LANES), WIDE)
+    along_a, along_b, along_c, along_d = bits, bits, bits, bits
+    if len(bits) > 1:
+        along_b, along_c, along_d = [1, 0] + bits[2:], bits[1:] + [0], [0] + bits[:0:-1]
+    columns = lambda: (slice(None), pl.ds(pl.multiple_of(lax.axis_index("dp") * own, own), own))
+    rows = lambda: (pl.ds(pl.multiple_of(lax.axis_index("dp") * own, own), own),)
+    part_rows = lambda: (slice(None), *rows())
+    mine = lambda array, axis: lax.dynamic_slice_in_dim(array, own_start, own, axis)
+    block_rows, loss_sums, grad_final, grad_up_rows, mid_terms = [], [], [], [], []
+    grad_hidden, norms_sums, own_back, other_back = [], [], [], []
+    flip = lambda array: jnp.transpose(array, (1, 0, 2))
+    qkv = Weight(
+        line,
+        0,
+        3,
+        owned_parts_kernel,
+        lambda: (normed_in, [grad_rows]),
+        Take(qkv_parts, (3, own, local), part_rows),
+        [flip(qkv_first), flip(qkv_second)],
+    )
+    out = Weight(
+        line,
+        1,
+        local,
+        owned_columns_kernel,
+        lambda: (attn, [grad_branch]),
+        Take(mine(out_weight, 1)) if own % LANES else Take(out_weight, (local, own), columns),
+        [out_first, out_second],
+    )
+    up_matrix = Weight(
+        line,
+        2,
+        hidden_units,
+        owned_rows_kernel,
+        lambda: (normed_mid, grad_up_rows),
+        Take(up_weight, (own, hidden_units), rows),
+        [up_first, up_second],
+    )
+    down = Weight(
+        line,
+        3,
+        hidden_units,
+        owned_columns_kernel,
+        lambda: (active, sum(grad_final, [])),
+        Take(mine(down_weight, 1))
+        if own % LANES
+        else Take(down_weight, (hidden_units, own), columns),
+        [down_first, down_second],
+    )
+    d0 = down.piece(0, 8, 8, along_a)
+    u0 = up_matrix.piece(0, 8, 8, along_b)
+    q0 = qkv.piece(0, 1, 3, along_b)
+    q1 = qkv.piece(1, 2, 3, along_a)
+    q2 = qkv.piece(2, 3, 3, along_d)
+    o0 = out.piece(0, 1, 1, along_a)
+
+    def loss(c):
         outs = line.call(
             functools.partial(loss_kernel, c * part),
-            [cut(half, width), cut(half, width), shaped(2, width)],
+            [cut(half, width, 1), cut(half, width, CUT_LOSS), shaped(2, width)],
             [out_grad, norm_params, hidden[c], *mlp_terms[c]],
-            name="loss",
         )
         block_rows.append(outs[0])
         loss_sums.append(outs[2])
-        grad_final += [outs[1], near(outs[1])]
-        if c == CHUNKS - 1:
-            begin("d", owned_columns_kernel, active, grad_blocks(), "down_send")
+        grad_final.extend([outs[1], near(outs[1])])
+
+    def mlp_back(c):
         outs = line.call(
             mlp_back_kernel,
             [
                 shaped(part, width, kind=LOW),
                 shaped(part, hidden_units, kind=LOW),
-                cut(half, width),
+                cut(half, width, CUT_MLP if c < CHUNKS - 1 else CUT_MID),
                 shaped(half, width),
             ],
             [*grad_final[-2:], up[c], up_low, down_low],
-            name="mlp_back",
         )
         grad_up_rows.append(outs[1])
-        crossing = near(outs[2])
-        if c == CHUNKS - 1:
-            begin("u", owned_rows_kernel, normed_mid, grad_up_rows, "up_send")
-        mid_terms.append(sum_rows(line, outs[3], crossing, "sum_mid"))
-        block_other.append(near(block_rows[c]))
-    hold("d", owned_columns_kernel, active, grad_blocks(), "down_keep")
-    hold("u", owned_rows_kernel, normed_mid, grad_up_rows, "up_keep")
-    block_output = line.call(
-        functools.partial(place_kernel, chunks=CHUNKS),
-        [shaped(row_count, width, kind=LOW)],
-        [sum(block_rows, []), sum(block_other, [])],
-        name="place_output",
-    )[0]
-
-    grad_hidden, norms_sums, own_back, other_back = [], [], [], []
-    for c in chunks:
+        mid_terms.append((outs[3], near(outs[2])))
+
+    def sum_mid(c):
+        mid_terms[c] = sum_rows(line, *mid_terms[c])
+
+    def norms(c):
         outs = line.call(
             functools.partial(norms_back_kernel, c * part),
-            [shaped(half, width), cut(half, width), shaped(4, width)],
+            [shaped(half, width), cut(half, width, CUT_NORMS), shaped(4, width)],
             [out_grad, norm_params, hidden[c], branch[c], *mid_terms[c]],
-            name="norms_back",
         )
         grad_hidden.append(outs[0])
         norms_sums.append(outs[2])
         own_back.append(outs[1])
         other_back.append(near(outs[1]))
-    advance("d1")
-    grad_branch, grad_rows = line.call(
-        functools.partial(attention_back_kernel, chunks=CHUNKS),
-        [shaped(row_count, width, kind=LOW), shaped(row_count, 3 * local, kind=LOW)],
-        [live, out_low, cosine, sine, *own_back, *other_back, *query, *keys, *values, *masses],
-        scratch=[pltpu.VMEM((row_count, local), WIDE), pltpu.VMEM((row_count, local), WIDE)],
-        name="attention_back",
+
+    def norms_before():
+        for c in chunks[:-1]:
+            norms(c)
+
+    def attention_back():
+        return line.call(
+            functools.partial(attention_back_kernel, chunks=CHUNKS),
+            [shaped(row_count, width, kind=LOW), shaped(row_count, 3 * local, kind=LOW)],
+            [live, out_low, cosine, sine, *own_back, *other_back, *query, *keys, *values, *masses],
+            scratch=[pltpu.VMEM((row_count, local), WIDE), pltpu.VMEM((row_count, local), WIDE)],
+        )
+
+    def input_back():
+        return line.call(
+            functools.partial(input_back_kernel, chunks=CHUNKS),
+            [cut(row_count // 2, width, CUT_BACK), shaped(row_count // 2, width)],
+            [grad_rows, qkv_low],
+        )
+
+    def input_norm():
+        return line.call(
+            functools.partial(input_norm_kernel, chunks=CHUNKS),
+            [cut(row_count // 2, width, CUT_INPUT), shaped(2, width)],
+            [block_input, norm_params, *in_terms, *grad_hidden],
+        )
+
+    def place(blocks):
+        return line.call(
+            functools.partial(place_kernel, chunks=CHUNKS),
+            [shaped(row_count, width, kind=LOW)],
+            [blocks, near(blocks)],
+        )[0]
+
+    def norm_sums():
+        return line.call(
+            functools.partial(norm_sums_kernel, chunks=CHUNKS),
+            [shaped(8, width)],
+            [input_sums, *norms_sums, *loss_sums],
+        )[0]
+
+    def sum_norms():
+        return line.call(
+            sum_kernel, [shaped(8, width)], [grad_norms, swap(grad_norms, "tensor", 1)]
+        )[0]
+
+    last = CHUNKS - 1
+    for c in chunks[:-1]:
+        loss(c)
+        mlp_back(c)
+        sum_mid(c)
+    loss(last)
+    d0.start()
+    mlp_back(last)
+    u0.start()
+    up_matrix.hold()
+    sum_mid(last)
+    norms_before()
+    norms(last)
+    down.hold()
+    block_output = place(sum(block_rows, []))
+    grad_branch, grad_rows = attention_back()
+    send, keep = input_back()
+    q2.start()
+    d0.advance()
+    q0.start()
+    qkv.hold()
+    out.hold()
+    q1.start()
+    o0.start()
+    q2.advance()
+    u0.advance()
+    in_terms = sum_rows(line, keep, near(send))
+    d0.advance()
+    u0.advance()
+    q2.advance()
+    q1.advance()
+    input_rows, input_sums = input_norm()
+    down.moments()
+    grad_norms = norm_sums()
+    q1.advance()
+    grad_norms = sum_norms()
+    q0.advance()
+    o0.advance()
+    q0.advance()
+    o0.advance()
+    out.moments()
+    up_matrix.moments()
+    input_grad = place(input_rows)
+    qkv.stage()
+    qkv.moments()
+
+    tensor_bits = log2_of(lax.axis_size("tensor"))
+    found = line.table
+    for start in range(0, tensor_bits, 2):
+        terms = sum_terms(found, "tensor", start, min(2, tensor_bits - start))
+        if start + 2 >= tensor_bits:
+            found = line.call(join_kernel, [shaped(8, LANES + width)], [*terms, grad_norms])[0]
+        else:
+            found = line.call(pairs_kernel, [shaped(8, LANES)], terms)[0]
+    for start in range(0, len(bits), 2):
+        terms = sum_terms(found, "dp", start, min(2, len(bits) - start))
+        if start + 2 < len(bits) or len(terms) > 2:
+            found = line.call(pairs_kernel, [shaped(8, LANES + width)], terms)[0]
+            terms = [found]
+    weights = (qkv, out, up_matrix, down)
+    outs = line.call(
+        functools.partial(masters_kernel, terms=len(terms), own=own),
+        [shaped(*weight.kept.shape) for weight in weights]
+        + [shaped(2, 4), shaped(8, width if own % LANES else own), shaped(8, own), shaped(8, own)],
+        [
+            norm_params,
+            norm_first,
+            norm_second,
+            *terms,
+            *[weight.kept for weight in weights],
+            *[weight.update for weight in weights],
+        ],
     )
-    begin("q", owned_parts_kernel, normed_in, [grad_rows], "qkv_send")
-    begin("o", owned_columns_kernel, attn, [grad_branch], "out_send")
-    send, keep = line.call(
-        functools.partial(input_back_kernel, chunks=CHUNKS),
-        [cut(row_count // 2, width), shaped(row_count // 2, width)],
-        [grad_rows, qkv_low],
-        name="input_back",
-    )
-    crossing = near(send)
-    advance("d0")
-    hold("q", owned_parts_kernel, normed_in, [grad_rows], "qkv_keep")
-    hold("o", owned_columns_kernel, attn, [grad_branch], "out_keep")
-    in_terms = sum_rows(line, keep, crossing, "sum_in")
-    advance("d1", "u0", "d0")
-
-    input_rows, input_sums = line.call(
-        functools.partial(input_norm_kernel, chunks=CHUNKS),
-        [cut(row_count // 2, width), shaped(2, width)],
-        [block_input, norm_params, *in_terms, *grad_hidden],
-        name="input_norm",
-    )
-    input_other = near(input_rows)
-    advance("q2")
-    input_grad = line.call(
-        functools.partial(place_kernel, chunks=CHUNKS),
-        [shaped(row_count, width, kind=LOW)],
-        [input_rows, input_other],
-        name="place_input",
-    )[0]
-    grad_norms = line.call(
-        functools.partial(norm_sums_kernel, chunks=CHUNKS),
-        [shaped(8, width)],
-        [input_sums, *norms_sums, *loss_sums],
-        name="norm_sums",
-    )[0]
-    grad_norms = line.call(
-        sum_kernel,
-        [shaped(8, width)],
-        [grad_norms, swap(grad_norms, "tensor", 1)],
-        name="sum_norms",
-    )[0]
-    advance("u1", "u0")
-    grad_norms = sum_all(line, grad_norms, "dp", "sum_norms")
-    advance("u1", "q0", "q1")
-    columns = lambda: (slice(None), pl.ds(pl.multiple_of(lax.axis_index("dp") * own, own), own))
-    mine = lambda array, axis: lax.dynamic_slice_in_dim(array, own_start, own, axis)
+    matrix_norms, norm_new, norm_first_new, norm_second_new = outs[4:]
     if own % LANES:
-        norm_args = [mine(norm_params, 1), mine(grad_norms, 1)]
-    else:
-        norm_args = [
-            Take(norm_params, (8, own), columns),
-            Take(grad_norms, (8, own), columns),
-        ]
-    norm_new, norm_first_new, norm_second_new = line.call(
-        norm_step_kernel,
-        [shaped(8, own)] * 3,
-        [*norm_args, Take(norm_first), Take(norm_second)],
-        name="norm_step",
-    )
-
-    rows = lambda: (pl.ds(pl.multiple_of(lax.axis_index("dp") * own, own), own),)
-    part_rows = lambda: (slice(None), *rows())
-    masters = [
-        Take(qkv_parts, (3, own, local), part_rows),
-        Take(mine(out_weight, 1)) if own % LANES else Take(out_weight, (local, own), columns),
-        Take(up_weight, (own, hidden_units), rows),
-        Take(mine(down_weight, 1)) if own % LANES else Take(down_weight, (hidden_units, own), columns),
-    ]
-    states = [
-        (jnp.transpose(qkv_first, (1, 0, 2)), jnp.transpose(qkv_second, (1, 0, 2))),
-        (out_first, out_second),
-        (up_first, up_second),
-        (down_first, down_second),
-    ]
-    everything = slice(None)
-    table = jnp.zeros((8, LANES), WIDE)
-    stepped = [None] * 4
-
-    def step(index, letter):
-        nonlocal table
-        found = of(letter)
-        for piece in found:
-            while piece.stage < len(bits):
-                piece.advance(line)
-        if letter == "u":
-            regions = [(everything, slice(*piece.window)) for piece in found]
-        else:
-            regions = [(slice(*piece.window),) for piece in found]
-        terms = [
-            Take(term, term.shape[1:], lambda: (0,)) for piece in found for term in piece.terms
-        ]
-        shape = masters[index].shape
-        outs = line.call(
-            functools.partial(
-                moments_kernel,
-                row=index,
-                regions=regions,
-                counts=[len(piece.terms) for piece in found],
-            ),
-            [shaped(*shape)] * 4 + [shaped(8, LANES)],
-            [masters[index], *[Take(state) for state in states[index]], table, *terms],
-            megabytes=16,
-            name="moments_" + letter,
-        )
-        stepped[index] = outs[:4]
-        table = outs[4]
-
-    step(3, "d")
-    advance("u1", "q0", "q1", "q2", "o0")
-    step(2, "u")
-    advance("q0", "q1", "q2", "o0")
-    step(1, "o")
-    step(0, "q")
-    squares = sum_all(line, table, "tensor", "sum_squares")
-    squares = sum_all(line, squares, "dp", "sum_squares")
-    outs = line.call(
-        masters_kernel,
-        [shaped(*entry[0].shape) for entry in stepped] + [shaped(8, LANES)],
-        [squares, *[entry[0] for entry in stepped], *[entry[1] for entry in stepped]],
-        name="masters",
-    )
-    back = lambda array: jnp.transpose(array, (1, 0, 2))
-    matrix_norms = jnp.stack([outs[4][0:4, 0], outs[4][4:8, 0]])
+        norm_first_new, norm_second_new, direction = moment_step(
+            mine(norm_new, 1), norm_first, norm_second
+        )
+        norm_new = mine(norm_params, 1) - learn_rate * direction
     return (
         block_output,
         input_grad,
-        back(outs[0]),
-        back(stepped[0][2]),
-        back(stepped[0][3]),
+        flip(outs[0]),
+        flip(qkv.first_new),
+        flip(qkv.second_new),
         outs[1],
-        stepped[1][2],
-        stepped[1][3],
+        out.first_new,
+        out.second_new,
         outs[2],
-        stepped[2][2],
-        stepped[2][3],
+        up_matrix.first_new,
+        up_matrix.second_new,
         outs[3],
-        stepped[3][2],
-        stepped[3][3],
+        down.first_new,
+        down.second_new,
         norm_new,
         norm_first_new,
         norm_second_new,

time: 286 us -> 242 us (0.85)
  waiting for transfers between devices: 153 us -> 121 us
  starting transfers between devices: 66.2 us -> 54.3 us
    ppermute x107 -> x73, waiting for transfers between devices: 153 us -> 121 us  [swap(): return lax.ppermute(values, axis, [(i, i ^ distance) for i in range(count)])]
    ppermute x107 -> x73, starting transfers between devices: 66.2 us -> 54.3 us  [swap(): return lax.ppermute(values, axis, [(i, i ^ distance) for i in range(count)])]
    pallas_call x63 -> x58, Pallas kernels: 51.3 us -> 51.8 us  [call(): pl.pallas_call(body, out_shape=(*out_shapes, *[shaped(8, LANES) for _ in...]
    unnamed x50 -> x64, local copies, waits for them, and re-layouts: 7.1 us -> 7.41 us
  transfers between devices with their start and end apart: 107 -> 73, of which waited for: 69 -> 51; matrix products, arithmetic and copies ran while one was open for 0% -> 0% of each run, Pallas kernels for 15% -> 17%
where the time goes in v3:
time: 242 us; the launch traced here: 237 us
  waiting for transfers between devices  121 us (50%)
  starting transfers between devices  54.3 us (22%)
  Pallas kernels  51.8 us (21%)
  local copies, waits for them, and re-layouts  7.42 us (3%)
  between operations  2.54 us (1%)
    ppermute x73, waiting for transfers between devices, swap(): return lax.ppermute(values, axis, [(i, i ^ distance) for i in range(count)])  121 us
    ppermute x73, starting transfers between devices, swap(): return lax.ppermute(values, axis, [(i, i ^ distance) for i in range(count)])  54.3 us
    pallas_call x58, Pallas kernels, call(): pl.pallas_call(body, out_shape=(*out_shapes, *[shaped(8, LANES) for _ in...  51.8 us
    unnamed x64, local copies, waits for them, and re-layouts  7.41 us
  transfers between devices with their start and end apart: 73, of which 51 were waited for; matrix products, arithmetic and copies ran while one was open for 0% of the time, Pallas kernels for 17%

profile of v3, /device:TPU:0, one launch (start us, length us, event | category | flops | bytes accessed | tf_op | source)
XLA Modules:
  0.0 236.9 jit_solution(5422599248358157329)
XLA Ops:
  1.3 6.0 %shard_map.331 = (bf16[3,1024,256]{2,1,0:T(8,128)(2,1)}, bf16[256,1024]{1,0:T(8,128)(2,1)}, bf16[256,1024]{1,0:T(8,128)(2,1)}, bf16[256,256]{1,0:T(8,128)(2,1)},...) custom-call(s32[1]{0:T(128)S(6)} %copy.152.refs_0_, ...), custom_call_target="tpu_custom_call" | custom-call | tf_op jit(solution)/shard_map/pallas_call | solution.py:229
  7.9 1.3 collective-permute-done.refs_1_
  9.6 1.0 copy-done.23
  10.7 2.9 %collective-permute-start.2 = (f32[128,1024]{1,0:T(8,128)S(1)}, f32[128,1024]{1,0:T(8,128)S(1)}, u32[]{:S(2)}, u32[]{:S(2)}) collective-permute-start(f32[128,1024]{1,0:T(8,128)S(1)} %get-tuple-element.229.refs_2_), channel_id=1, source_target_pairs={{0,2},{1,3},{2,0},{3,1},{4,6},{5,7},{6,4},{7,5},{8,10},{9,11},{10,... | collective-permute-start | bytes 1572872 | tf_op jit(solution)/shard_map/ppermute | solution.py:45
  13.6 1.4 copy-done.6
  15.0 1.0 copy-done.12
  16.1 0.9 copy-done.19
  17.0 0.9 copy-done.21
  17.9 2.8 %shard_map.333 = (bf16[256,1024]{1,0:T(8,128)(2,1)S(1)}, bf16[256,256]{1,0:T(8,128)(2,1)S(1)}, bf16[256,256]{1,0:T(8,128)(2,1)S(1)}, bf16[256,256]{1,0:T(8,128)(...) custom-call(s32[1]{0:T(128)S(6)} %copy.152.refs_0_, ...), custom_call_target="tpu_custom_call", output_to_operand_aliasing={{9}: (9, {})} | custom-call | tf_op jit(solution)/shard_map/pallas_call | solution.py:229
  21.2 1.0 collective-permute-done.3.refs_1_
  23.3 1.7 copy-done.1
  28.7 1.9 shard_map.338
  32.9 2.3 collective-permute-start.13
  35.2 2.3 collective-permute-done.14.refs_3_
  40.1 1.9 shard_map.341
  44.2 2.2 collective-permute-start.23
  46.4 2.3 collective-permute-done.13.refs_4_
  49.8 1.0 collective-permute-done.24.refs_2_.refs_4_
  51.2 2.5 %shard_map.344 = (bf16[256,1024]{1,0:T(8,128)(2,1)}, bf16[256,1024]{1,0:T(8,128)(2,1)S(1)}, f32[32,1024]{1,0:T(8,128)S(1)}, f32[32,1024]{1,0:T(8,128)S(1)}, f32[...) custom-call(f32[64,1024]{1,0:T(8,128)S(1)} %get-tuple-element.274.re, ...), custom_call_target="tpu_custom_call", output_to_operand_aliasing={{7}: (7, {})} | custom-call | tf_op jit(solution)/shard_map/pallas_call | solution.py:229
  55.8 3.7 %collective-permute-done.23.refs_4_ = f32[128,1024]{1,0:T(8,128)S(1)} collective-permute-done((f32[128,1024]{1,0:T(8,128)S(1)}, f32[128,1024]{1,0:T(8,128)S(1)}, u32[]{:S(2)}, u32[]{:S(2)}) %collective-permute-start.23) | collective-permute-done | bytes 524320 | tf_op jit(solution)/shard_map/ppermute | solution.py:45
  60.6 1.0 collective-permute-done.32.refs_8_.refs_2_
  62.8 1.8 collective-permute-start.45
  64.6 1.9 shard_map.348
  67.3 1.6 collective-permute-start.44
  69.5 1.5 collective-permute-start.37
  72.5 11.8 %collective-permute-done.37.refs_5_ = f32[128,1024]{1,0:T(8,128)S(1)} collective-permute-done((f32[128,1024]{1,0:T(8,128)S(1)}, f32[128,1024]{1,0:T(8,128)S(1)}, u32[]{:S(2)}, u32[]{:S(2)}) %collective-permute-start.37) | collective-permute-done | bytes 524320 | tf_op jit(solution)/shard_map/ppermute | solution.py:45
  85.3 9.2 %collective-permute-done.36.refs_5_ = f32[128,1024]{1,0:T(8,128)S(1)} collective-permute-done((f32[128,1024]{1,0:T(8,128)S(1)}, f32[128,1024]{1,0:T(8,128)S(1)}, u32[]{:S(2)}, u32[]{:S(2)}) %collective-permute-start.36) | collective-permute-done | bytes 524320 | tf_op jit(solution)/shard_map/ppermute | solution.py:45
  97.3 1.1 shard_map.355
  98.4 4.6 %shard_map.356 = (bf16[512,1024]{1,0:T(8,128)(2,1)S(1)}, bf16[512,768]{1,0:T(8,128)(2,1)S(1)}, f32[8,128]{1,0:T(8,128)S(1)}) custom-call(s32[1]{0:T(128)S(6)} %copy.152.refs_0_, bf16[256,1024]{1,0:T(8,128)(2,1)S(1)} %copy-done.13, f32[512,128]{1,0:T(8,128)S(1)} %copy-done.10, f32[512,128]{1,0:T(8,128)S(1)} %copy-done.11, ...), custom_call_target="tpu_custom_call", output_to_operand_aliasing={{2}: (20, {})} | custom-call | tf_op jit(solution)/shard_map/pallas_call | solution.py:229
  103.0 2.2 shard_map.357
  106.6 4.7 %collective-permute-done.45.refs_1_.refs_5_ = f32[4,1024,128]{2,1,0:T(8,128)S(1)} collective-permute-done((f32[4,1024,128]{2,1,0:T(8,128)S(1)}, f32[4,1024,128]{2,1,0:T(8,128)S(1)}, u32[]{:S(2)}, u32[]{:S(2)}) %collective-permute-start.45) | collective-permute-done | bytes 2097184 | tf_op jit(solution)/shard_map/ppermute | solution.py:45
  111.6 1.9 collective-permute-start.51
  115.7 6.1 %collective-permute-done.46.refs_1_.refs_13_ = f32[4,1,128,256]{3,2,1,0:T(8,128)S(1)} collective-permute-done((f32[4,1,128,256]{3,2,1,0:T(8,128)S(1)}, f32[4,1,128,256]{3,2,1,0:T(8,128)S(1)}, u32[]{:S(2)}, u32[]{:S(2)}) %collective-permute-start.46) | collective-permute-done | bytes 524320 | tf_op jit(solution)/shard_map/ppermute | solution.py:45
  122.2 1.8 collective-permute-start.50
  124.1 1.6 collective-permute-start.47
  126.2 2.6 %collective-permute-start.49 = (f32[2,1,128,256]{3,2,1,0:T(8,128)S(1)}, f32[2,1,128,256]{3,2,1,0:T(8,128)S(1)}, u32[]{:S(2)}, u32[]{:S(2)}) collective-permute-start(f32[2,1,128,256]{3,2,1,0:T(8,128)S(1)} %get-tuple-element.354), channel_id=1, source_target_pairs={{0,16},{4,20},{8,24},{12,28},{16,0},{20,4},{24,8},{28,12},{1,17},{... | collective-permute-start | bytes 786440 | tf_op jit(solution)/shard_map/ppermute | solution.py:45
  128.8 14.1 %collective-permute-done.51.refs_2_.refs_6_ = f32[2,1024,128]{2,1,0:T(8,128)S(1)} collective-permute-done((f32[2,1024,128]{2,1,0:T(8,128)S(1)}, f32[2,1024,128]{2,1,0:T(8,128)S(1)}, u32[]{:S(2)}, u32[]{:S(2)}) %collective-permute-start.51) | collective-permute-done | bytes 1048608 | tf_op jit(solution)/shard_map/ppermute | solution.py:45
  143.1 1.8 collective-permute-start.54
  144.8 2.5 %collective-permute-start.56 = (f32[4,1,128,256]{3,2,1,0:T(8,128)S(1)}, f32[4,1,128,256]{3,2,1,0:T(8,128)S(1)}, u32[]{:S(2)}, u32[]{:S(2)}) collective-permute-start(f32[4,1,128,256]{3,2,1,0:T(8,128)S(1)} %get-tuple-element.370), channel_id=1, source_target_pairs={{0,8},{4,12},{8,0},{12,4},{16,24},{20,28},{24,16},{28,20},{1,9},{5... | collective-permute-start | bytes 1572872 | tf_op jit(solution)/shard_map/ppermute | solution.py:45
  147.3 1.0 collective-permute-done.50.refs_2_.refs_6_
  148.3 1.7 collective-permute-start.55
  151.1 8.5 %collective-permute-done.48.refs_1_.refs_9_ = f32[4,1,128,256]{3,2,1,0:T(8,128)S(1)} collective-permute-done((f32[4,1,128,256]{3,2,1,0:T(8,128)S(1)}, f32[4,1,128,256]{3,2,1,0:T(8,128)S(1)}, u32[]{:S(2)}, u32[]{:S(2)}) %collective-permute-start.48) | collective-permute-done | bytes 524320 | tf_op jit(solution)/shard_map/ppermute | solution.py:45
  159.6 1.9 collective-permute-start.58
  161.5 2.6 %collective-permute-start.62 = (f32[1,128,1024]{2,1,0:T(8,128)S(1)}, f32[1,128,1024]{2,1,0:T(8,128)S(1)}, u32[]{:S(2)}, u32[]{:S(2)}) collective-permute-start(f32[1,128,1024]{2,1,0:T(8,128)S(1)} %get-tuple-element.390), channel_id=1, source_target_pairs={{0,16},{4,20},{8,24},{12,28},{16,0},{20,4},{24,8},{28,12},{1,17},{... | collective-permute-start | bytes 1572872 | tf_op jit(solution)/shard_map/ppermute | solution.py:45
  165.0 4.3 %collective-permute-done.54.refs_7_ = f32[1,1024,128]{2,1,0:T(8,128)S(1)} collective-permute-done((f32[1,1024,128]{2,1,0:T(8,128)S(1)}, f32[1,1024,128]{2,1,0:T(8,128)S(1)}, u32[]{:S(2)}, u32[]{:S(2)}) %collective-permute-start.54) | collective-permute-done | bytes 524320 | tf_op jit(solution)/shard_map/ppermute | solution.py:45
  169.3 1.7 shard_map.373
  171.2 9.4 %collective-permute-done.58.refs_2_.refs_10_ = f32[2,1,128,256]{3,2,1,0:T(8,128)S(1)} collective-permute-done((f32[2,1,128,256]{3,2,1,0:T(8,128)S(1)}, f32[2,1,128,256]{3,2,1,0:T(8,128)S(1)}, u32[]{:S(2)}, u32[]{:S(2)}) %collective-permute-start.58) | collective-permute-done | bytes 262176 | tf_op jit(solution)/shard_map/ppermute | solution.py:45
  182.1 8.0 %collective-permute-done.60.refs_2_.refs_6_ = f32[2,1,128,256]{3,2,1,0:T(8,128)S(1)} collective-permute-done((f32[2,1,128,256]{3,2,1,0:T(8,128)S(1)}, f32[2,1,128,256]{3,2,1,0:T(8,128)S(1)}, u32[]{:S(2)}, u32[]{:S(2)}) %collective-permute-start.60) | collective-permute-done | bytes 262176 | tf_op jit(solution)/shard_map/ppermute | solution.py:45
  190.7 4.2 %collective-permute-done.59.refs_2_.refs_6_ = f32[2,256,128]{2,1,0:T(8,128)S(1)} collective-permute-done((f32[2,256,128]{2,1,0:T(8,128)S(1)}, f32[2,256,128]{2,1,0:T(8,128)S(1)}, u32[]{:S(2)}, u32[]{:S(2)}) %collective-permute-start.59) | collective-permute-done | bytes 262176 | tf_op jit(solution)/shard_map/ppermute | solution.py:45
  196.2 2.5 %collective-permute-start.65 = (f32[1,1,128,256]{3,2,1,0:T(8,128)S(1)}, f32[1,1,128,256]{3,2,1,0:T(8,128)S(1)}, u32[]{:S(2)}, u32[]{:S(2)}) collective-permute-start(f32[1,1,128,256]{3,2,1,0:T(8,128)S(1)} %get-tuple-element.401), channel_id=1, source_target_pairs={{0,8},{4,12},{8,0},{12,4},{16,24},{20,28},{24,16},{28,20},{1,9},{5... | collective-permute-start | bytes 393224 | tf_op jit(solution)/shard_map/ppermute | solution.py:45
  198.8 9.5 %collective-permute-done.61.refs_7_ = f32[1,256,128]{2,1,0:T(8,128)S(1)} collective-permute-done((f32[1,256,128]{2,1,0:T(8,128)S(1)}, f32[1,256,128]{2,1,0:T(8,128)S(1)}, u32[]{:S(2)}, u32[]{:S(2)}) %collective-permute-start.61) | collective-permute-done | bytes 131104 | tf_op jit(solution)/shard_map/ppermute | solution.py:45
  208.3 1.9 shard_map.381
  210.3 1.6 shard_map.382
  212.0 1.1 shard_map.383
  213.9 1.3 collective-permute-done.63.refs_7_
  215.3 3.6 %shard_map.385 = (f32[3,128,256]{2,1,0:T(8,128)S(1)}, f32[3,128,256]{2,1,0:T(8,128)S(1)}, f32[3,128,256]{2,1,0:T(8,128)}, f32[3,128,256]{2,1,0:T(8,128)}, f32[8,128]{1,0:T(8,128)S(1)}, /*index=5*/f32[8,128]{1,0:T(8,128)S(1)}) custom-call(f32[3,128,256]{2,1,0:T(8,128)S(1)} %get-tuple-element.395.refs_0_, ...), custom_call_target="tpu_custom_call", output_to_operand_aliasing={{5}: (16, {})} | custom-call | tf_op jit(solution)/shard_map/pallas_call | solution.py:229
  218.9 1.5 collective-permute-start.67
  220.8 1.8 collective-permute-done.67.refs_2_
  223.5 1.8 collective-permute-start.69
  225.3 1.6 collective-permute-start.71
  227.4 1.8 collective-permute-done.70.refs_2_
  230.2 2.2 collective-permute-start.72
  232.4 2.7 %collective-permute-done.72.refs_4_ = f32[8,1152]{1,0:T(8,128)S(1)} collective-permute-done((f32[8,1152]{1,0:T(8,128)S(1)}, f32[8,1152]{1,0:T(8,128)S(1)}, u32[]{:S(2)}, u32[]{:S(2)}) %collective-permute-start.72) | collective-permute-done | bytes 36896 | tf_op jit(solution)/shard_map/ppermute | solution.py:45
  235.1 1.3 shard_map.388
  (206 shorter events, 40.0 us)
Async XLA Ops:
  7.3 1.9 collective-permute-start
  7.8 1.7 collective-permute-start.1
  10.7 15.4 %collective-permute-start.2 = (f32[128,1024]{1,0:T(8,128)S(1)}, f32[128,1024]{1,0:T(8,128)S(1)}, u32[]{:S(2)}, u32[]{:S(2)}) collective-permute-start(f32[128,1024]{1,0:T(8,128)S(1)} %get-tuple-element.229.refs_2_), channel_id=1, source_target_pairs={{0,2},{1,3},{2,0},{3,1},{4,6},{5,7},{6,4},{7,5},{8,10},{9,11},{10,... | collective-permute-start | bytes 1572872 | tf_op jit(solution)/shard_map/ppermute | solution.py:45
  20.6 1.6 collective-permute-start.3
  20.7 1.9 collective-permute-start.4
  22.7 14.8 %collective-permute-start.14 = (f32[128,1024]{1,0:T(8,128)S(1)}, f32[128,1024]{1,0:T(8,128)S(1)}, u32[]{:S(2)}, u32[]{:S(2)}) collective-permute-start(f32[128,1024]{1,0:T(8,128)S(1)} %get-tuple-element.257.refs_2_), channel_id=1, source_target_pairs={{0,2},{1,3},{2,0},{3,1},{4,6},{5,7},{6,4},{7,5},{8,10},{9,11},{10,... | collective-permute-start | bytes 1572872 | tf_op jit(solution)/shard_map/ppermute | solution.py:45
  26.6 1.4 collective-permute-start.5
  26.7 1.5 collective-permute-start.6
  27.2 1.3 collective-permute-start.7
  27.3 1.5 collective-permute-start.8
  30.6 1.4 collective-permute-start.10
  32.9 15.8 %collective-permute-start.13 = (f32[128,1024]{1,0:T(8,128)S(1)}, f32[128,1024]{1,0:T(8,128)S(1)}, u32[]{:S(2)}, u32[]{:S(2)}) collective-permute-start(f32[128,1024]{1,0:T(8,128)S(1)} %get-tuple-element.256.refs_3_), channel_id=1, source_target_pairs={{0,2},{1,3},{2,0},{3,1},{4,6},{5,7},{6,4},{7,5},{8,10},{9,11},{10,... | collective-permute-start | bytes 1572872 | tf_op jit(solution)/shard_map/ppermute | solution.py:45
  38.0 1.4 collective-permute-start.15
  38.0 1.5 collective-permute-start.16
  38.6 1.5 collective-permute-start.18
  41.9 1.4 collective-permute-start.19
  44.2 15.3 %collective-permute-start.23 = (f32[128,1024]{1,0:T(8,128)S(1)}, f32[128,1024]{1,0:T(8,128)S(1)}, u32[]{:S(2)}, u32[]{:S(2)}) collective-permute-start(f32[128,1024]{1,0:T(8,128)S(1)} %get-tuple-element.273.refs_3_), channel_id=1, source_target_pairs={{0,2},{1,3},{2,0},{3,1},{4,6},{5,7},{6,4},{7,5},{8,10},{9,11},{10,... | collective-permute-start | bytes 1572872 | tf_op jit(solution)/shard_map/ppermute | solution.py:45
  49.2 1.6 collective-permute-start.24
  49.3 1.9 collective-permute-start.25
  53.9 1.4 collective-permute-start.27
  54.4 1.4 collective-permute-start.29
  60.0 1.6 collective-permute-start.32
  60.1 1.9 collective-permute-start.33
  62.8 48.5 %collective-permute-start.45 = (f32[4,1024,128]{2,1,0:T(8,128)S(1)}, f32[4,1024,128]{2,1,0:T(8,128)S(1)}, u32[]{:S(2)}, u32[]{:S(2)}) collective-permute-start(f32[4,1024,128]{2,1,0:T(8,128)S(1)} %get-tuple-element.333), channel_id=1, source_target_pairs={{0,4},{4,0},{8,12},{12,8},{16,20},{20,16},{24,28},{28,24},{1,5},{5... | collective-permute-start | bytes 6291464 | tf_op jit(solution)/shard_map/ppermute | solution.py:45
  67.3 54.5 %collective-permute-start.44 = (f32[4,128,1024]{2,1,0:T(8,128)S(1)}, f32[4,128,1024]{2,1,0:T(8,128)S(1)}, u32[]{:S(2)}, u32[]{:S(2)}) collective-permute-start(f32[4,128,1024]{2,1,0:T(8,128)S(1)} %get-tuple-element.329), channel_id=1, source_target_pairs={{0,8},{4,12},{8,0},{12,4},{16,24},{20,28},{24,16},{28,20},{1,9},{5... | collective-permute-start | bytes 6291464 | tf_op jit(solution)/shard_map/ppermute | solution.py:45
  69.0 2.8 %collective-permute-start.34 = (f32[64,1024]{1,0:T(8,128)S(1)}, f32[64,1024]{1,0:T(8,128)S(1)}, u32[]{:S(2)}, u32[]{:S(2)}) collective-permute-start(f32[64,1024]{1,0:T(8,128)S(1)} %get-tuple-element.295), channel_id=1, source_target_pairs={{0,1},{1,0},{2,3},{3,2},{4,5},{5,4},{6,7},{7,6},{8,9},{9,8},{10,11... | collective-permute-start | bytes 786440 | tf_op jit(solution)/shard_map/ppermute | solution.py:45
  69.0 2.8 %collective-permute-start.35 = (f32[64,1024]{1,0:T(8,128)S(1)}, f32[64,1024]{1,0:T(8,128)S(1)}, u32[]{:S(2)}, u32[]{:S(2)}) collective-permute-start(f32[64,1024]{1,0:T(8,128)S(1)} %get-tuple-element.296), channel_id=1, source_target_pairs={{0,1},{1,0},{2,3},{3,2},{4,5},{5,4},{6,7},{7,6},{8,9},{9,8},{10,11... | collective-permute-start | bytes 786440 | tf_op jit(solution)/shard_map/ppermute | solution.py:45
  69.5 14.8 %collective-permute-start.37 = (f32[128,1024]{1,0:T(8,128)S(1)}, f32[128,1024]{1,0:T(8,128)S(1)}, u32[]{:S(2)}, u32[]{:S(2)}) collective-permute-start(f32[128,1024]{1,0:T(8,128)S(1)} %get-tuple-element.306.refs_4_), channel_id=1, source_target_pairs={{0,2},{1,3},{2,0},{3,1},{4,6},{5,7},{6,4},{7,5},{8,10},{9,11},{10,... | collective-permute-start | bytes 1572872 | tf_op jit(solution)/shard_map/ppermute | solution.py:45
  71.8 22.7 %collective-permute-start.36 = (f32[128,1024]{1,0:T(8,128)S(1)}, f32[128,1024]{1,0:T(8,128)S(1)}, u32[]{:S(2)}, u32[]{:S(2)}) collective-permute-start(f32[128,1024]{1,0:T(8,128)S(1)} %get-tuple-element.304.refs_4_), channel_id=1, source_target_pairs={{0,2},{1,3},{2,0},{3,1},{4,6},{5,7},{6,4},{7,5},{8,10},{9,11},{10,... | collective-permute-start | bytes 1572872 | tf_op jit(solution)/shard_map/ppermute | solution.py:45
  72.5 22.9 %collective-permute-start.30 = (f32[128,1024]{1,0:T(8,128)S(1)}, f32[128,1024]{1,0:T(8,128)S(1)}, u32[]{:S(2)}, u32[]{:S(2)}) collective-permute-start(f32[128,1024]{1,0:T(8,128)S(1)} %get-tuple-element.271.refs_0_), channel_id=1, source_target_pairs={{0,1},{1,0},{2,3},{3,2},{4,5},{5,4},{6,7},{7,6},{8,9},{9,8},{10,11... | collective-permute-start | bytes 1572872 | tf_op jit(solution)/shard_map/ppermute | solution.py:45
  84.3 11.7 %collective-permute-start.31 = (f32[128,1024]{1,0:T(8,128)S(1)}, f32[128,1024]{1,0:T(8,128)S(1)}, u32[]{:S(2)}, u32[]{:S(2)}) collective-permute-start(f32[128,1024]{1,0:T(8,128)S(1)} %get-tuple-element.285.refs_1_), channel_id=1, source_target_pairs={{0,1},{1,0},{2,3},{3,2},{4,5},{5,4},{6,7},{7,6},{8,9},{9,8},{10,11... | collective-permute-start | bytes 1572872 | tf_op jit(solution)/shard_map/ppermute | solution.py:45
  94.5 1.5 collective-permute-start.38
  95.4 3.0 %collective-permute-start.39 = (f32[64,1024]{1,0:T(8,128)S(1)}, f32[64,1024]{1,0:T(8,128)S(1)}, u32[]{:S(2)}, u32[]{:S(2)}) collective-permute-start(f32[64,1024]{1,0:T(8,128)S(1)} %get-tuple-element.313.refs_5_), channel_id=1, source_target_pairs={{0,1},{1,0},{2,3},{3,2},{4,5},{5,4},{6,7},{7,6},{8,9},{9,8},{10,11... | collective-permute-start | bytes 786440 | tf_op jit(solution)/shard_map/ppermute | solution.py:45
  95.9 2.4 %collective-permute-start.40 = (f32[64,1024]{1,0:T(8,128)S(1)}, f32[64,1024]{1,0:T(8,128)S(1)}, u32[]{:S(2)}, u32[]{:S(2)}) collective-permute-start(f32[64,1024]{1,0:T(8,128)S(1)} %get-tuple-element.314.refs_6_), channel_id=1, source_target_pairs={{0,1},{1,0},{2,3},{3,2},{4,5},{5,4},{6,7},{7,6},{8,9},{9,8},{10,11... | collective-permute-start | bytes 786440 | tf_op jit(solution)/shard_map/ppermute | solution.py:45
  96.1 2.3 collective-permute-start.41
  105.6 16.2 %collective-permute-start.46 = (f32[4,1,128,256]{3,2,1,0:T(8,128)S(1)}, f32[4,1,128,256]{3,2,1,0:T(8,128)S(1)}, u32[]{:S(2)}, u32[]{:S(2)}) collective-permute-start(f32[4,1,128,256]{3,2,1,0:T(8,128)S(1)} %get-tuple-element.339), channel_id=1, source_target_pairs={{0,4},{4,0},{8,12},{12,8},{16,20},{20,16},{24,28},{28,24},{1,5},{5... | collective-permute-start | bytes 1572872 | tf_op jit(solution)/shard_map/ppermute | solution.py:45
  106.1 17.8 %collective-permute-start.42 = (f32[128,1024]{1,0:T(8,128)S(1)}, f32[128,1024]{1,0:T(8,128)S(1)}, u32[]{:S(2)}, u32[]{:S(2)}) collective-permute-start(f32[128,1024]{1,0:T(8,128)S(1)} %get-tuple-element.326), channel_id=1, source_target_pairs={{0,1},{1,0},{2,3},{3,2},{4,5},{5,4},{6,7},{7,6},{8,9},{9,8},{10,11... | collective-permute-start | bytes 1572872 | tf_op jit(solution)/shard_map/ppermute | solution.py:45
  106.1 17.8 %collective-permute-start.43 = (f32[128,1024]{1,0:T(8,128)S(1)}, f32[128,1024]{1,0:T(8,128)S(1)}, u32[]{:S(2)}, u32[]{:S(2)}) collective-permute-start(f32[128,1024]{1,0:T(8,128)S(1)} %get-tuple-element.327), channel_id=1, source_target_pairs={{0,1},{1,0},{2,3},{3,2},{4,5},{5,4},{6,7},{7,6},{8,9},{9,8},{10,11... | collective-permute-start | bytes 1572872 | tf_op jit(solution)/shard_map/ppermute | solution.py:45
  111.6 31.3 %collective-permute-start.51 = (f32[2,1024,128]{2,1,0:T(8,128)S(1)}, f32[2,1024,128]{2,1,0:T(8,128)S(1)}, u32[]{:S(2)}, u32[]{:S(2)}) collective-permute-start(f32[2,1024,128]{2,1,0:T(8,128)S(1)} %get-tuple-element.356), channel_id=1, source_target_pairs={{0,8},{4,12},{8,0},{12,4},{16,24},{20,28},{24,16},{28,20},{1,9},{5... | collective-permute-start | bytes 3145736 | tf_op jit(solution)/shard_map/ppermute | solution.py:45
  122.2 26.2 %collective-permute-start.50 = (f32[2,128,1024]{2,1,0:T(8,128)S(1)}, f32[2,128,1024]{2,1,0:T(8,128)S(1)}, u32[]{:S(2)}, u32[]{:S(2)}) collective-permute-start(f32[2,128,1024]{2,1,0:T(8,128)S(1)} %get-tuple-element.355), channel_id=1, source_target_pairs={{0,4},{4,0},{8,12},{12,8},{16,20},{20,16},{24,28},{28,24},{1,5},{5... | collective-permute-start | bytes 3145736 | tf_op jit(solution)/shard_map/ppermute | solution.py:45
  124.1 37.4 %collective-permute-start.47 = (f32[256,1024]{1,0:T(8,128)S(1)}, f32[256,1024]{1,0:T(8,128)S(1)}, u32[]{:S(2)}, u32[]{:S(2)}) collective-permute-start(f32[256,1024]{1,0:T(8,128)S(1)} %get-tuple-element.349.refs_2_), channel_id=1, source_target_pairs={{0,2},{1,3},{2,0},{3,1},{4,6},{5,7},{6,4},{7,5},{8,10},{9,11},{10,... | collective-permute-start | bytes 3145736 | tf_op jit(solution)/shard_map/ppermute | solution.py:45
  125.7 33.9 %collective-permute-start.48 = (f32[4,1,128,256]{3,2,1,0:T(8,128)S(1)}, f32[4,1,128,256]{3,2,1,0:T(8,128)S(1)}, u32[]{:S(2)}, u32[]{:S(2)}) collective-permute-start(f32[4,1,128,256]{3,2,1,0:T(8,128)S(1)} %get-tuple-element.353), channel_id=1, source_target_pairs={{0,4},{4,0},{8,12},{12,8},{16,20},{20,16},{24,28},{28,24},{1,5},{5... | collective-permute-start | bytes 1572872 | tf_op jit(solution)/shard_map/ppermute | solution.py:45
  126.2 18.7 %collective-permute-start.49 = (f32[2,1,128,256]{3,2,1,0:T(8,128)S(1)}, f32[2,1,128,256]{3,2,1,0:T(8,128)S(1)}, u32[]{:S(2)}, u32[]{:S(2)}) collective-permute-start(f32[2,1,128,256]{3,2,1,0:T(8,128)S(1)} %get-tuple-element.354), channel_id=1, source_target_pairs={{0,16},{4,20},{8,24},{12,28},{16,0},{20,4},{24,8},{28,12},{1,17},{... | collective-permute-start | bytes 786440 | tf_op jit(solution)/shard_map/ppermute | solution.py:45
  143.1 26.3 %collective-permute-start.54 = (f32[1,1024,128]{2,1,0:T(8,128)S(1)}, f32[1,1024,128]{2,1,0:T(8,128)S(1)}, u32[]{:S(2)}, u32[]{:S(2)}) collective-permute-start(f32[1,1024,128]{2,1,0:T(8,128)S(1)} %get-tuple-element.364), channel_id=1, source_target_pairs={{0,16},{4,20},{8,24},{12,28},{16,0},{20,4},{24,8},{28,12},{1,17},{... | collective-permute-start | bytes 1572872 | tf_op jit(solution)/shard_map/ppermute | solution.py:45
  144.8 36.9 %collective-permute-start.56 = (f32[4,1,128,256]{3,2,1,0:T(8,128)S(1)}, f32[4,1,128,256]{3,2,1,0:T(8,128)S(1)}, u32[]{:S(2)}, u32[]{:S(2)}) collective-permute-start(f32[4,1,128,256]{3,2,1,0:T(8,128)S(1)} %get-tuple-element.370), channel_id=1, source_target_pairs={{0,8},{4,12},{8,0},{12,4},{16,24},{20,28},{24,16},{28,20},{1,9},{5... | collective-permute-start | bytes 1572872 | tf_op jit(solution)/shard_map/ppermute | solution.py:45
  148.3 33.6 %collective-permute-start.55 = (f32[4,256,128]{2,1,0:T(8,128)S(1)}, f32[4,256,128]{2,1,0:T(8,128)S(1)}, u32[]{:S(2)}, u32[]{:S(2)}) collective-permute-start(f32[4,256,128]{2,1,0:T(8,128)S(1)} %get-tuple-element.368), channel_id=1, source_target_pairs={{0,4},{4,0},{8,12},{12,8},{16,20},{20,16},{24,28},{28,24},{1,5},{5... | collective-permute-start | bytes 1572872 | tf_op jit(solution)/shard_map/ppermute | solution.py:45
  159.6 21.0 %collective-permute-start.58 = (f32[2,1,128,256]{3,2,1,0:T(8,128)S(1)}, f32[2,1,128,256]{3,2,1,0:T(8,128)S(1)}, u32[]{:S(2)}, u32[]{:S(2)}) collective-permute-start(f32[2,1,128,256]{3,2,1,0:T(8,128)S(1)} %get-tuple-element.378), channel_id=1, source_target_pairs={{0,8},{4,12},{8,0},{12,4},{16,24},{20,28},{24,16},{28,20},{1,9},{5... | collective-permute-start | bytes 786440 | tf_op jit(solution)/shard_map/ppermute | solution.py:45
  161.5 37.2 %collective-permute-start.62 = (f32[1,128,1024]{2,1,0:T(8,128)S(1)}, f32[1,128,1024]{2,1,0:T(8,128)S(1)}, u32[]{:S(2)}, u32[]{:S(2)}) collective-permute-start(f32[1,128,1024]{2,1,0:T(8,128)S(1)} %get-tuple-element.390), channel_id=1, source_target_pairs={{0,16},{4,20},{8,24},{12,28},{16,0},{20,4},{24,8},{28,12},{1,17},{... | collective-permute-start | bytes 1572872 | tf_op jit(solution)/shard_map/ppermute | solution.py:45
  171.1 10.1 %collective-permute-start.57 = (f32[8,1024]{1,0:T(8,128)S(1)}, f32[8,1024]{1,0:T(8,128)S(1)}, u32[]{:S(2)}, u32[]{:S(2)}) collective-permute-start(f32[8,1024]{1,0:T(8,128)S(1)} %get-tuple-element.377.refs_0_), channel_id=1, source_target_pairs={{0,1},{1,0},{2,3},{3,2},{4,5},{5,4},{6,7},{7,6},{8,9},{9,8},{10,11... | collective-permute-start | bytes 98312 | tf_op jit(solution)/shard_map/ppermute | solution.py:45
  180.6 31.3 %collective-permute-start.52 = (f32[128,1024]{1,0:T(8,128)S(1)}, f32[128,1024]{1,0:T(8,128)S(1)}, u32[]{:S(2)}, u32[]{:S(2)}) collective-permute-start(f32[128,1024]{1,0:T(8,128)S(1)} %get-tuple-element.362.refs_0_), channel_id=1, source_target_pairs={{0,1},{1,0},{2,3},{3,2},{4,5},{5,4},{6,7},{7,6},{8,9},{9,8},{10,11... | collective-permute-start | bytes 1572872 | tf_op jit(solution)/shard_map/ppermute | solution.py:45
  181.2 30.8 %collective-permute-start.53 = (f32[128,1024]{1,0:T(8,128)S(1)}, f32[128,1024]{1,0:T(8,128)S(1)}, u32[]{:S(2)}, u32[]{:S(2)}) collective-permute-start(f32[128,1024]{1,0:T(8,128)S(1)} %get-tuple-element.363.refs_1_), channel_id=1, source_target_pairs={{0,1},{1,0},{2,3},{3,2},{4,5},{5,4},{6,7},{7,6},{8,9},{9,8},{10,11... | collective-permute-start | bytes 1572872 | tf_op jit(solution)/shard_map/ppermute | solution.py:45
  181.9 8.3 %collective-permute-start.60 = (f32[2,1,128,256]{3,2,1,0:T(8,128)S(1)}, f32[2,1,128,256]{3,2,1,0:T(8,128)S(1)}, u32[]{:S(2)}, u32[]{:S(2)}) collective-permute-start(f32[2,1,128,256]{3,2,1,0:T(8,128)S(1)} %get-tuple-element.384), channel_id=1, source_target_pairs={{0,4},{4,0},{8,12},{12,8},{16,20},{20,16},{24,28},{28,24},{1,5},{5... | collective-permute-start | bytes 786440 | tf_op jit(solution)/shard_map/ppermute | solution.py:45
  182.0 12.8 %collective-permute-start.59 = (f32[2,256,128]{2,1,0:T(8,128)S(1)}, f32[2,256,128]{2,1,0:T(8,128)S(1)}, u32[]{:S(2)}, u32[]{:S(2)}) collective-permute-start(f32[2,256,128]{2,1,0:T(8,128)S(1)} %get-tuple-element.383), channel_id=1, source_target_pairs={{0,8},{4,12},{8,0},{12,4},{16,24},{20,28},{24,16},{28,20},{1,9},{5... | collective-permute-start | bytes 786440 | tf_op jit(solution)/shard_map/ppermute | solution.py:45
  195.4 12.9 %collective-permute-start.61 = (f32[1,256,128]{2,1,0:T(8,128)S(1)}, f32[1,256,128]{2,1,0:T(8,128)S(1)}, u32[]{:S(2)}, u32[]{:S(2)}) collective-permute-start(f32[1,256,128]{2,1,0:T(8,128)S(1)} %get-tuple-element.387), channel_id=1, source_target_pairs={{0,16},{4,20},{8,24},{12,28},{16,0},{20,4},{24,8},{28,12},{1,17},{... | collective-permute-start | bytes 393224 | tf_op jit(solution)/shard_map/ppermute | solution.py:45
  196.2 17.7 %collective-permute-start.65 = (f32[1,1,128,256]{3,2,1,0:T(8,128)S(1)}, f32[1,1,128,256]{3,2,1,0:T(8,128)S(1)}, u32[]{:S(2)}, u32[]{:S(2)}) collective-permute-start(f32[1,1,128,256]{3,2,1,0:T(8,128)S(1)} %get-tuple-element.401), channel_id=1, source_target_pairs={{0,8},{4,12},{8,0},{12,4},{16,24},{20,28},{24,16},{28,20},{1,9},{5... | collective-permute-start | bytes 393224 | tf_op jit(solution)/shard_map/ppermute | solution.py:45
  198.7 15.2 %collective-permute-start.64 = (f32[1,1,128,256]{3,2,1,0:T(8,128)S(1)}, f32[1,1,128,256]{3,2,1,0:T(8,128)S(1)}, u32[]{:S(2)}, u32[]{:S(2)}) collective-permute-start(f32[1,1,128,256]{3,2,1,0:T(8,128)S(1)} %get-tuple-element.400), channel_id=1, source_target_pairs={{0,16},{4,20},{8,24},{12,28},{16,0},{20,4},{24,8},{28,12},{1,17},{... | collective-permute-start | bytes 393224 | tf_op jit(solution)/shard_map/ppermute | solution.py:45
  208.3 6.9 %collective-permute-start.63 = (f32[1,1,128,256]{3,2,1,0:T(8,128)S(1)}, f32[1,1,128,256]{3,2,1,0:T(8,128)S(1)}, u32[]{:S(2)}, u32[]{:S(2)}) collective-permute-start(f32[1,1,128,256]{3,2,1,0:T(8,128)S(1)} %get-tuple-element.399), channel_id=1, source_target_pairs={{0,16},{4,20},{8,24},{12,28},{16,0},{20,4},{24,8},{28,12},{1,17},{... | collective-permute-start | bytes 393224 | tf_op jit(solution)/shard_map/ppermute | solution.py:45
  218.8 1.9 collective-permute-start.66
  218.9 3.7 %collective-permute-start.67 = (f32[8,128]{1,0:T(8,128)S(1)}, f32[8,128]{1,0:T(8,128)S(1)}, u32[]{:S(2)}, u32[]{:S(2)}) collective-permute-start(f32[8,128]{1,0:T(8,128)S(1)} %get-tuple-element.403.refs_0_), channel_id=1, source_target_pairs={{0,2},{1,3},{2,0},{3,1},{4,6},{5,7},{6,4},{7,5},{8,10},{9,11},{10,... | collective-permute-start | bytes 12296 | tf_op jit(solution)/shard_map/ppermute | solution.py:45
  220.4 3.0 %collective-permute-start.68 = (f32[8,128]{1,0:T(8,128)S(1)}, f32[8,128]{1,0:T(8,128)S(1)}, u32[]{:S(2)}, u32[]{:S(2)}) collective-permute-start(f32[8,128]{1,0:T(8,128)S(1)} %get-tuple-element.403.refs_0_), channel_id=1, source_target_pairs={{0,3},{1,2},{2,1},{3,0},{4,7},{5,6},{6,5},{7,4},{8,11},{9,10},{10,... | collective-permute-start | bytes 12296 | tf_op jit(solution)/shard_map/ppermute | solution.py:45
  223.5 4.0 %collective-permute-start.69 = (f32[8,1152]{1,0:T(8,128)S(1)}, f32[8,1152]{1,0:T(8,128)S(1)}, u32[]{:S(2)}, u32[]{:S(2)}) collective-permute-start(f32[8,1152]{1,0:T(8,128)S(1)} %get-tuple-element.406.refs_0_), channel_id=1, source_target_pairs={{0,4},{4,0},{8,12},{12,8},{16,20},{20,16},{24,28},{28,24},{1,5},{5... | collective-permute-start | bytes 110600 | tf_op jit(solution)/shard_map/ppermute | solution.py:45
  225.3 4.0 %collective-permute-start.70 = (f32[8,1152]{1,0:T(8,128)S(1)}, f32[8,1152]{1,0:T(8,128)S(1)}, u32[]{:S(2)}, u32[]{:S(2)}) collective-permute-start(f32[8,1152]{1,0:T(8,128)S(1)} %get-tuple-element.406.refs_0_), channel_id=1, source_target_pairs={{0,8},{4,12},{8,0},{12,4},{16,24},{20,28},{24,16},{28,20},{1,9},{5... | collective-permute-start | bytes 110600 | tf_op jit(solution)/shard_map/ppermute | solution.py:45
  225.3 4.9 %collective-permute-start.71 = (f32[8,1152]{1,0:T(8,128)S(1)}, f32[8,1152]{1,0:T(8,128)S(1)}, u32[]{:S(2)}, u32[]{:S(2)}) collective-permute-start(f32[8,1152]{1,0:T(8,128)S(1)} %get-tuple-element.406.refs_0_), channel_id=1, source_target_pairs={{0,12},{4,8},{8,4},{12,0},{16,28},{20,24},{24,20},{28,16},{1,13},{... | collective-permute-start | bytes 110600 | tf_op jit(solution)/shard_map/ppermute | solution.py:45
  230.2 4.9 %collective-permute-start.72 = (f32[8,1152]{1,0:T(8,128)S(1)}, f32[8,1152]{1,0:T(8,128)S(1)}, u32[]{:S(2)}, u32[]{:S(2)}) collective-permute-start(f32[8,1152]{1,0:T(8,128)S(1)} %get-tuple-element.408.refs_3_), channel_id=1, source_target_pairs={{0,16},{4,20},{8,24},{12,28},{16,0},{20,4},{24,8},{28,12},{1,17},{... | collective-permute-start | bytes 110600 | tf_op jit(solution)/shard_map/ppermute | solution.py:45
  (41 other events, 275.7 us)
